TPU v7x, 32 devices: a whole 2x2x4 slice. The times are simulated.
32 devices in a mesh: gx: 2 (over y), gy: 4 (over x, core), gz: 4 (over z).
Axes of the slice: x: 2, y: 2, z: 4, core: 2. Of those that a mesh axis runs over, the one named last changes fastest.
Arguments:
- inputs: bfloat16 [640, 12288], P(('gy', 'gz'), 'gx'), may hold values from -6 to 6
- pre_act: bfloat16 [640, 24576], P('gx', ('gy', 'gz')), may hold values from -6 to 6
- out_grad: bfloat16 [640, 12288], P(('gy', 'gz'), 'gx'), may hold values from -6 to 6
- w_in: bfloat16 [12288, 24576], P('gx', ('gy', 'gz')), may hold values from -0.0546875 to 0.0546875
- w_out: bfloat16 [24576, 12288], P(('gy', 'gz'), 'gx'), may hold values from -0.0390625 to 0.0390625
Outputs:
- in_grad: bfloat16 [640, 12288], P(('gy', 'gz'), 'gx')
- w_in_grad: bfloat16 [12288, 24576], P('gx', ('gy', 'gz'))
- w_out_grad: bfloat16 [24576, 12288], P(('gy', 'gz'), 'gx')
All inputs are finite; a program needn't handle non-finite values.
Results may differ from a plain program's by a relative error of at most 0.0051.
Values may be sent and summed in bfloat16 or wider, within the bound.
No kernel may reach another device: no remote copies, remote signals or barrier semaphores. Data moves between devices by JAX's collectives and lax.ppermute only.
A program may use at most 192 MiB of HBM per device.

v0:
```python
import math

import jax
import jax.numpy as jnp
from jax import lax
from jax.sharding import PartitionSpec as P


def gelu_parts(pre_values):
    values = pre_values.astype(jnp.float32)
    normal_cdf = 0.5 * (1.0 + lax.erf(values / math.sqrt(2.0)))
    activity = values * normal_cdf
    slope = normal_cdf + values * jnp.exp(-0.5 * values * values) / math.sqrt(2.0 * math.pi)
    return (activity, slope)


def right_trans(left, right):
    return lax.dot_general(
        left, right, (((1,), (1,)), ((), ())), preferred_element_type=jnp.float32
    )


def left_trans(left, right):
    return lax.dot_general(
        left, right, (((0,), (0,)), ((), ())), preferred_element_type=jnp.float32
    )


def shards(inputs, pre_act, out_grad, w_in, w_out):
    groups = lax.axis_size("gy") * lax.axis_size("gz")
    all_rows = inputs.shape[0] * groups
    factor = 1.0 / math.sqrt(all_rows)
    full_grad, full_inputs = (
        lax.all_gather(out_grad, ("gy", "gz"), axis=0, tiled=True),
        lax.all_gather(inputs, ("gy", "gz"), axis=0, tiled=True),
    )
    grad_act = right_trans(full_grad, w_out)
    grad_act = lax.psum(grad_act, "gx")
    full_pre = lax.all_gather(pre_act, "gx", axis=0, tiled=True)
    activity, slope = gelu_parts(full_pre)
    act_low = activity.astype(jnp.bfloat16)
    grad_pre = (grad_act * slope).astype(jnp.bfloat16)
    w_out_grad = (left_trans(act_low, full_grad) * factor).astype(jnp.bfloat16)
    w_in_grad = (left_trans(full_inputs, grad_pre) * factor).astype(jnp.bfloat16)
    in_sum = lax.psum_scatter(
        right_trans(grad_pre, w_in), ("gy", "gz"), scatter_dimension=0, tiled=True
    )
    in_grad = in_sum.astype(jnp.bfloat16)
    return (in_grad, w_in_grad, w_out_grad)


def solution(mesh):
    placed = (
        P(("gy", "gz"), "gx"),
        P("gx", ("gy", "gz")),
        P(("gy", "gz"), "gx"),
        P("gx", ("gy", "gz")),
        P(("gy", "gz"), "gx"),
    )
    return jax.shard_map(
        shards,
        mesh=mesh,
        in_specs=placed,
        out_specs=(P(("gy", "gz"), "gx"), P("gx", ("gy", "gz")), P(("gy", "gz"), "gx")),
        check_vma=False,
    )
```

profile of v0, /device:TPU:0, one launch (start us, length us, event | category | flops | bytes accessed | tf_op | source)
XLA Modules:
  0.0 464.5 jit_solution(8469680548110233836)
XLA Ops:
  7.2 0.0 all-gather.4.cloned.1.call-start
  7.2 0.7 all-gather.4.cloned.1.call-update
  7.9 0.0 all-gather.6.cloned.1.call-start
  7.9 0.7 all-gather.6.cloned.1.call-update
  8.7 0.0 all-reduce.2.cloned.1.call-start
  8.7 75.9 %all-gather.4.cloned.1.call-done = bf16[640,6144]{1,0:T(8,128)(2,1)} async-done(((bf16[40,6144]{1,0:T(8,128)(2,1)}), bf16[640,6144]{1,0:T(8,128)(2,1)}) %all-gather.4.cloned.1.call-update) | async-done | bytes 7864336 | tf_op jit(solution)/shard_map/all_gather | solution.py:34
  84.6 18.9 %fusion.15 = f32[640,1536]{1,0:T(8,128)} fusion(bf16[640,6144]{1,0:T(8,128)(2,1)} %all-gather.4.cloned.1.call-done, bf16[1536,6144]{1,0:T(8,128)(2,1)} %param.9), kind=kOutput, calls=%fused_computation.18 | convolution fusion | flops 12079595520 | bytes 30670848 | tf_op jit(solution)/shard_map/dot_general | solution.py:18
  103.5 0.0 all-reduce.2.cloned.1.call-update
  103.5 0.0 all-gather.8.cloned.1.call-start
  103.6 0.5 all-gather.8.cloned.1.call-update
  104.1 0.2 reduce-scatter.2.cloned.1.call-start
  104.3 11.8 %all-gather.6.cloned.1.call-done = bf16[640,1536]{1,0:T(8,128)(2,1)} async-done(((bf16[320,1536]{1,0:T(8,128)(2,1)}), bf16[640,1536]{1,0:T(8,128)(2,1)}) %all-gather.6.cloned.1.call-update) | async-done | bytes 1966096 | tf_op jit(solution)/shard_map/all_gather | solution.py:39
  116.2 105.8 %all-reduce.2.cloned.1.call-done = f32[640,1536]{1,0:T(8,128)} async-done(((f32[640,1536]{1,0:T(8,128)}), f32[640,1536]{1,0:T(8,128)}) %all-reduce.2.cloned.1.call-update) | async-done | bytes 3932176 | tf_op jit(solution)/shard_map/psum | solution.py:38
  222.0 22.5 %fusion.13 = f32[640,6144]{1,0:T(8,128)} fusion(bf16[6144,1536]{1,0:T(8,128)(2,1)} %param.8, f32[640,1536]{1,0:T(8,128)} %all-reduce.2.cloned.1.call-done, bf16[640,1536]{1,0:T(8,128)(2,1)} %all-gather.6.cloned.1.call-done), kind=kOutput, calls=%fused_computation.17 | convolution fusion | flops 12090408960 | bytes 40501248 | tf_op jit(solution)/shard_map/dot_general | solution.py:18
  244.5 0.0 copy-start
  244.5 0.0 reduce-scatter.2.cloned.1.call-update
  244.5 1.5 copy-done
  246.0 21.3 %multiply_convert_fusion = bf16[1536,6144]{1,0:T(8,128)(2,1)} fusion(bf16[640,6144]{1,0:T(8,128)(2,1)} %all-gather.4.cloned.1.call-done, bf16[640,1536]{1,0:T(8,128)(2,1)S(1)} %copy-done), kind=kOutput, calls=%fused_computation | convolution fusion | flops 12104368128 | bytes 28704768 | tf_op jit(solution)/shard_map/dot_general | solution.py:24
  267.3 28.7 %all-gather.8.cloned.1.call-done = bf16[640,6144]{1,0:T(8,128)(2,1)} async-done(((bf16[40,6144]{1,0:T(8,128)(2,1)}), bf16[640,6144]{1,0:T(8,128)(2,1)}) %all-gather.8.cloned.1.call-update) | async-done | bytes 7864336 | tf_op jit(solution)/shard_map/all_gather | solution.py:35
  296.1 23.2 %fusion = bf16[6144,1536]{0,1:T(8,128)(2,1)} fusion(bf16[640,6144]{1,0:T(8,128)(2,1)} %all-gather.8.cloned.1.call-done, f32[640,1536]{1,0:T(8,128)} %all-reduce.2.cloned.1.call-done, bf16[640,1536]{1,0:T(8,128)(2,1)S(1)} %copy-done), kind=kOutput, calls=%fused_computation.2 | convolution fusion | flops 12109283328 | bytes 32636928 | tf_op jit(solution)/shard_map/dot_general | solution.py:24
  319.2 25.2 %copy.8 = bf16[6144,1536]{1,0:T(8,128)(2,1)} copy(bf16[6144,1536]{0,1:T(8,128)(2,1)} %fusion) | data formatting | bytes 37748736
  344.4 111.5 %reduce-scatter.2.cloned.1.call-done = f32[40,6144]{1,0:T(8,128)} async-done(((f32[640,6144]{1,0:T(8,128)}), f32[40,6144]{1,0:T(8,128)}) %reduce-scatter.2.cloned.1.call-update) | async-done | bytes 983056 | tf_op jit(solution)/shard_map/reduce_scatter | solution.py:45
  455.9 2.0 convert_element_type.23
Async XLA Ops:
  7.2 77.5 %all-gather.4.cloned.1.call-start = ((), (), s32[]{:S(2)}) async-start(), calls=%async_computation.1 | async-start | bytes 8355840 | tf_op jit(solution)/shard_map/all_gather | solution.py:34
  7.9 108.3 %all-gather.6.cloned.1.call-start = ((), (), s32[]{:S(2)}) async-start(), calls=%async_computation.3 | async-start | bytes 2949120 | tf_op jit(solution)/shard_map/all_gather | solution.py:39
  8.7 213.3 %all-reduce.2.cloned.1.call-start = ((), (), s32[]{:S(2)}) async-start(), calls=%async_computation.2 | async-start | bytes 7864320 | tf_op jit(solution)/shard_map/psum | solution.py:38
  103.5 192.5 %all-gather.8.cloned.1.call-start = ((), (), s32[]{:S(2)}) async-start(), calls=%async_computation.5 | async-start | bytes 8355840 | tf_op jit(solution)/shard_map/all_gather | solution.py:35
  104.1 351.8 %reduce-scatter.2.cloned.1.call-start = ((), (), s32[]{:S(2)}) async-start(), calls=%async_computation.4 | async-start | bytes 16711680 | tf_op jit(solution)/shard_map/reduce_scatter | solution.py:45
  244.5 1.6 copy-start
Sparse Core Ops, SparseCore 0:
  10.3 74.2 all-gather.3
  86.2 29.9 all-gather.5
  119.1 102.8 all-reduce.1
  224.4 71.5 all-gather.7
  300.5 155.3 reduce-scatter.1
where the time goes:
time: 465 us; the launch traced here: 464 us
  waiting for transfers between devices  336 us (72%)
  matrix products  85.9 us (18%)
  local copies, waits for them, and re-layouts  26.7 us (6%)
  between operations  13.8 us (3%)
    reduce_scatter x1, waiting for transfers between devices, shards(): lax.psum_scatter(right_trans(grad_pre, w_in), ('gy', 'gz'), scatter_dimen...  111 us
    psum x1, waiting for transfers between devices, shards(): grad_act = lax.psum(grad_act, 'gx')  106 us
    all_gather x1, waiting for transfers between devices, shards(): lax.all_gather(out_grad, ('gy', 'gz'), axis=0, tiled=True)  75.9 us
    dot_general x2, matrix products, left_trans(): lax.dot_general(left, right, (((0,), (0,)), ((), ())), preferred_element_...  44.5 us
    dot_general x2, matrix products, right_trans(): lax.dot_general(left, right, (((1,), (1,)), ((), ())), preferred_element_...  41.4 us
    all_gather x1, waiting for transfers between devices, shards(): lax.all_gather(inputs, ('gy', 'gz'), axis=0, tiled=True)  28.7 us
    unnamed x3, local copies, waits for them, and re-layouts  26.7 us
    all_gather x1, waiting for transfers between devices, shards(): full_pre = lax.all_gather(pre_act, 'gx', axis=0, tiled=True)  11.8 us
  transfers between devices with their start and end apart: 5, of which 5 were waited for; matrix products, arithmetic and copies ran while one was open for 24% of the time, Pallas kernels for 0%

commit v1 on v0

v1 whole, which is shorter than its diff:
```python
import math

import jax
import jax.numpy as jnp
from jax import lax
from jax.sharding import PartitionSpec as P

RING = ("gy", "gz")


def gelu_parts(pre_values):
    values = pre_values.astype(jnp.float32)
    normal_cdf = 0.5 * (1.0 + lax.erf(values / math.sqrt(2.0)))
    activity = values * normal_cdf
    slope = normal_cdf + values * jnp.exp(-0.5 * values * values) / math.sqrt(2.0 * math.pi)
    return (activity, slope)


def right_trans(left, right):
    return lax.dot_general(
        left, right, (((1,), (1,)), ((), ())), preferred_element_type=jnp.float32
    )


def left_trans(left, right):
    return lax.dot_general(
        left, right, (((0,), (0,)), ((), ())), preferred_element_type=jnp.float32
    )


class Ring:
    def __init__(self, gy, gz):
        self.cores = 2 if gy % 2 == 0 else 1
        chips = []
        for x in range(gy // self.cores):
            line = range(gz) if x % 2 == 0 else reversed(range(gz))
            chips += [(x, z) for z in line]
        self.size = len(chips)
        self.half = self.size // 2
        self.even = self.size % 2 == 0
        self.rank = [
            [(x * self.cores + core) * gz + z for core in range(self.cores)] for x, z in chips
        ]

    def shift(self, by):
        pairs = []
        for place in range(self.size):
            target = (place + by) % self.size
            for core in range(self.cores):
                pairs.append((self.rank[place][core], self.rank[target][core]))
        return pairs

    def swap(self):
        return [(ranks[core], ranks[1 - core]) for ranks in self.rank for core in range(2)]

    def groups(self):
        if self.half < 4:
            return [list(range(self.half + 1))]
        middle = [[step] for step in range(2, self.half - 1)]
        return [[0, 1]] + middle + [[self.half - 1, self.half]]

    def offsets(self, step):
        if step == 0:
            return [0]
        if step == self.half and self.even:
            return [self.half]
        return [-step, step]


def gather_steps(ring, block):
    held = {0: block}
    left, right = block, block
    for step in range(1, ring.half + 1):
        if step == ring.half and ring.even:
            cut = block.shape[1] // 2
            low = lax.ppermute(left[:, :cut], RING, ring.shift(1))
            high = lax.ppermute(right[:, cut:], RING, ring.shift(-1))
            held[step] = jnp.concatenate([low, high], axis=1)
        else:
            left = lax.ppermute(left, RING, ring.shift(1))
            right = lax.ppermute(right, RING, ring.shift(-1))
            held[-step], held[step] = left, right
    return held


def with_other_core(ring, mine):
    if ring.cores == 1:
        return mine
    theirs = lax.ppermute(mine, RING, ring.swap())
    return jnp.concatenate([mine, theirs], axis=0)


def exchange(values, axis):
    size = lax.axis_size(axis)
    return [
        lax.ppermute(values, axis, [(i, (i + by) % size) for i in range(size)])
        for by in range(1, size)
    ]


def shards(inputs, pre_act, out_grad, w_in, w_out):
    ring = Ring(lax.axis_size("gy"), lax.axis_size("gz"))
    rows = inputs.shape[0]
    groups = ring.size * ring.cores
    factor = 1.0 / math.sqrt(rows * groups)
    rank = lax.axis_index(RING)
    core = lax.rem(lax.axis_index("gy"), ring.cores)
    place_of = [0] * groups
    for place, ranks in enumerate(ring.rank):
        for one in ranks:
            place_of[one] = place
    place = jnp.array(place_of, jnp.int32)[rank]
    ranks = jnp.array(ring.rank, jnp.int32)

    size_x = lax.axis_size("gx")
    me_x = lax.axis_index("gx")
    full_pre = jnp.zeros((size_x * pre_act.shape[0], pre_act.shape[1]), pre_act.dtype)
    full_pre = lax.dynamic_update_slice(full_pre, pre_act, (me_x * pre_act.shape[0], 0))
    for by, got in enumerate(exchange(pre_act, "gx"), 1):
        owner = lax.rem(me_x - by + size_x, size_x)
        full_pre = lax.dynamic_update_slice(full_pre, got, (owner * pre_act.shape[0], 0))

    order = [[o for step in group for o in ring.offsets(step)] for group in ring.groups()]

    def ordered(full, offsets):
        blocks = []
        for which in range(ring.cores):
            for offset in offsets:
                at = lax.rem(place + offset + ring.size, ring.size)
                owner = ranks[at, lax.rem(core + which, ring.cores)]
                blocks.append(lax.dynamic_slice_in_dim(full, owner * rows, rows, 0))
        return jnp.concatenate(blocks, axis=0)

    grads = gather_steps(ring, out_grad)
    tokens, acts, pres = [], [], []
    for offsets in order:
        chunk = with_other_core(ring, jnp.concatenate([grads[o] for o in offsets], axis=0))
        partial = right_trans(chunk, w_out)
        total = partial
        for got in exchange(partial.astype(jnp.bfloat16), "gx"):
            total = total + got.astype(jnp.float32)
        activity, slope = gelu_parts(ordered(full_pre, offsets))
        tokens.append(chunk)
        acts.append(activity.astype(jnp.bfloat16))
        pres.append((total * slope).astype(jnp.bfloat16))

    sums = {}
    for offsets, pre in reversed(list(zip(order, pres))):
        part = right_trans(pre, w_in)
        count = len(offsets) * rows
        mine = part[:count]
        if ring.cores == 2:
            mine = mine + lax.ppermute(
                part[count:].astype(jnp.bfloat16), RING, ring.swap()
            ).astype(jnp.float32)
        for i, offset in enumerate(offsets):
            sums[offset] = mine[i * rows : (i + 1) * rows]

    low = jnp.bfloat16
    right = left = None
    for step in range(ring.half, 0, -1):
        if step == ring.half and ring.even:
            cut = out_grad.shape[1] // 2
            here = sums[step].astype(low)
            right = lax.ppermute(here[:, :cut], RING, ring.shift(1)).astype(jnp.float32)
            left = lax.ppermute(here[:, cut:], RING, ring.shift(-1)).astype(jnp.float32)
            right = jnp.pad(right, ((0, 0), (0, right.shape[1])))
            left = jnp.pad(left, ((0, 0), (left.shape[1], 0)))
        else:
            go_right, go_left = sums[step], sums[-step]
            if right is not None:
                go_right, go_left = go_right + right, go_left + left
            right = lax.ppermute(go_right.astype(low), RING, ring.shift(1)).astype(jnp.float32)
            left = lax.ppermute(go_left.astype(low), RING, ring.shift(-1)).astype(jnp.float32)
    in_grad = (sums[0] + right + left).astype(jnp.bfloat16)

    w_out_grad = left_trans(jnp.concatenate(acts, axis=0), jnp.concatenate(tokens, axis=0))
    w_out_grad = (w_out_grad * factor).astype(jnp.bfloat16)

    held = gather_steps(ring, inputs)
    mine = jnp.concatenate([held[o] for offsets in order for o in offsets], axis=0)
    theirs = lax.ppermute(mine, RING, ring.swap()) if ring.cores == 2 else None
    pieces, at = [], 0
    for offsets in order:
        count = len(offsets) * rows
        pieces.append(mine[at : at + count])
        if theirs is not None:
            pieces.append(theirs[at : at + count])
        at += count
    w_in_grad = left_trans(jnp.concatenate(pieces, axis=0), jnp.concatenate(pres, axis=0))
    w_in_grad = (w_in_grad * factor).astype(jnp.bfloat16)
    return (in_grad, w_in_grad, w_out_grad)


def solution(mesh):
    placed = (
        P(("gy", "gz"), "gx"),
        P("gx", ("gy", "gz")),
        P(("gy", "gz"), "gx"),
        P("gx", ("gy", "gz")),
        P(("gy", "gz"), "gx"),
    )
    return jax.shard_map(
        shards,
        mesh=mesh,
        in_specs=placed,
        out_specs=(P(("gy", "gz"), "gx"), P("gx", ("gy", "gz")), P(("gy", "gz"), "gx")),
        check_vma=False,
    )
```

time: 465 us -> 303 us (0.65)
  waiting for transfers between devices: 336 us -> 71.1 us
  starting transfers between devices: 0.37 us -> 32.9 us
  local copies, waits for them, and re-layouts: 26.7 us -> 55 us
  matrix products: 85.9 us -> 111 us
  other arithmetic: 2.03 us -> 15.8 us
    all_gather x3 -> x0, waiting for transfers between devices: 116 us -> none  [the longest x1 75.9 us: shards(): lax.all_gather(out_grad, ('gy', 'gz'), axis=0, tiled=True)]
    reduce_scatter x1 -> x0, waiting for transfers between devices: 111 us -> none  [shards(): lax.psum_scatter(right_trans(grad_pre, w_in), ('gy', 'gz'), scatter_dimen...]
    psum x1 -> x0, waiting for transfers between devices: 106 us -> none  [shards(): grad_act = lax.psum(grad_act, 'gx')]
    ppermute x0 -> x35, waiting for transfers between devices: none -> 71.1 us  [the longest x4 19.8 us: exchange(): lax.ppermute(values, axis, [(i, (i + by) % size) for i in range(size)])]
    ppermute x0 -> x35, starting transfers between devices: none -> 32.9 us  [the longest x6 8.03 us: gather_steps(): right = lax.ppermute(right, RING, ring.shift(-1))]
    dot_general x2 -> x6, matrix products: 41.4 us -> 67.7 us  [right_trans(): lax.dot_general(left, right, (((1,), (1,)), ((), ())), preferred_element_...]
    unnamed x3 -> x87, local copies, waits for them, and re-layouts: 26.7 us -> 35.4 us
    slice x0 -> x8, local copies, waits for them, and re-layouts: none -> 7.49 us  [the longest x3 5.99 us: shards(): part[count:].astype(jnp.bfloat16)]
  transfers between devices with their start and end apart: 5 -> 35, of which waited for: 5 -> 14; matrix products, arithmetic and copies ran while one was open for 24% -> 58% of each run, Pallas kernels for 0% -> 0%
where the time goes in v1:
time: 303 us; the launch traced here: 302 us
  matrix products  111 us (37%)
  waiting for transfers between devices  71.1 us (23%)
  local copies, waits for them, and re-layouts  55 us (18%)
  starting transfers between devices  32.9 us (11%)
  between operations  16.3 us (5%)
  other arithmetic  15.8 us (5%)
    dot_general x6, matrix products, right_trans(): lax.dot_general(left, right, (((1,), (1,)), ((), ())), preferred_element_...  67.7 us
    dot_general x2, matrix products, left_trans(): lax.dot_general(left, right, (((0,), (0,)), ((), ())), preferred_element_...  43 us
    unnamed x87, local copies, waits for them, and re-layouts  35.4 us
    ppermute x4, waiting for transfers between devices, exchange(): lax.ppermute(values, axis, [(i, (i + by) % size) for i in range(size)])  19.8 us
    ppermute x3, waiting for transfers between devices, shards(): lax.ppermute(go_right.astype(low), RING, ring.shift(1)).astype(jnp.float32)  16 us
    ppermute x6, waiting for transfers between devices, gather_steps(): right = lax.ppermute(right, RING, ring.shift(-1))  14.6 us
    ppermute x6, waiting for transfers between devices, gather_steps(): left = lax.ppermute(left, RING, ring.shift(1))  11.3 us
    ppermute x6, starting transfers between devices, gather_steps(): right = lax.ppermute(right, RING, ring.shift(-1))  8.03 us
  transfers between devices with their start and end apart: 35, of which 14 were waited for; matrix products, arithmetic and copies ran while one was open for 58% of the time, Pallas kernels for 0%

profile of v1, /device:TPU:0, one launch (start us, length us, event | category | flops | bytes accessed | tf_op | source)
XLA Modules:
  0.0 301.7 jit_solution(9405149140392464700)
XLA Ops:
  0.6 3.0 collective-permute-start.1
  26.2 2.1 constant_dynamic-update-slice_fusion.8
  33.7 2.1 constant_dynamic-update-slice_fusion.7
  38.2 2.1 constant_dynamic-update-slice_fusion.6
  42.1 5.1 %collective-permute-done.6 = bf16[40,6144]{1,0:T(8,128)(2,1)S(1)} collective-permute-done((bf16[40,6144]{1,0:T(8,128)(2,1)S(1)}, bf16[40,6144]{1,0:T(8,128)(2,1)S(1)}, u32[]{:S(2)}, u32[]{:S(2)}) %collective-permute-start.6) | collective-permute-done | bytes 491552 | tf_op jit(solution)/shard_map/ppermute | solution.py:80
  52.0 5.7 %collective-permute-done.28 = bf16[40,6144]{1,0:T(8,128)(2,1)S(1)} collective-permute-done((bf16[40,6144]{1,0:T(8,128)(2,1)}, bf16[40,6144]{1,0:T(8,128)(2,1)S(1)}, u32[]{:S(2)}, u32[]{:S(2)}) %collective-permute-start.28) | collective-permute-done | bytes 491552 | tf_op jit(solution)/shard_map/ppermute | solution.py:80
  61.4 14.6 %collective-permute-done.31 = bf16[40,6144]{1,0:T(8,128)(2,1)S(1)} collective-permute-done((bf16[40,6144]{1,0:T(8,128)(2,1)S(1)}, bf16[40,6144]{1,0:T(8,128)(2,1)S(1)}, u32[]{:S(2)}, u32[]{:S(2)}) %collective-permute-start.31) | collective-permute-done | bytes 491552 | tf_op jit(solution)/shard_map/ppermute | solution.py:81
  87.1 10.7 %fusion.75 = (bf16[240,1536]{1,0:T(8,128)(2,1)}, f32[240,1536]{1,0:T(8,128)}) fusion(bf16[1536,6144]{1,0:T(8,128)(2,1)} %param.11, bf16[120,6144]{1,0:T(8,128)(2,1)S(1)} %collective-permute-done.2, bf16[40,6144]{1,0:T(8,128)(2,1)S(1)} %collective-permute-done.1, bf16[40,6144]{1,0:T(8,128)(2,1)S(1)} %copy-done.4, bf16[40,6144]{1,0:T(8,128)(2,1)S(1)} %copy-done.2), kind=kOutput, calls=%fused_computation.161 | convolution fusion | flops 4542013440 | bytes 24035328 | tf_op jit(solution)/shard_map/dot_general | solution.py:20
  98.5 10.4 %fusion.76 = (bf16[160,1536]{1,0:T(8,128)(2,1)S(1)}, f32[160,1536]{1,0:T(8,128)S(1)}) fusion(bf16[1536,6144]{1,0:T(8,128)(2,1)} %param.11, bf16[80,6144]{1,0:T(8,128)(2,1)} %collective-permute-done.8, bf16[40,6144]{1,0:T(8,128)(2,1)S(1)} %collective-permute-done.7, bf16[40,6144]{1,0:T(8,128)(2,1)S(1)} %collective-permute-done.6), kind=kOutput, calls=%fused_computation.162 | convolution fusion | flops 3026042880 | bytes 22315008 | tf_op jit(solution)/shard_map/dot_general | solution.py:20
  113.3 2.3 constant_dynamic-update-slice_fusion.21
  121.7 5.8 %collective-permute-done.9 = bf16[160,1536]{1,0:T(8,128)(2,1)S(1)} collective-permute-done((bf16[160,1536]{1,0:T(8,128)(2,1)S(1)}, bf16[160,1536]{1,0:T(8,128)(2,1)S(1)}, u32[]{:S(2)}, u32[]{:S(2)}) %collective-permute-start.9) | collective-permute-done | bytes 491552 | tf_op jit(solution)/shard_map/ppermute | solution.py:96
  128.1 14.5 %fusion.79 = f32[160,6144]{1,0:T(8,128)} fusion(bf16[160,1536]{1,0:T(8,128)(2,1)S(1)} %get-tuple-element.34, bf16[6144,1536]{1,0:T(8,128)(2,1)} %param.10), kind=kOutput, calls=%fused_computation.165 | convolution fusion | flops 3019898880 | bytes 23298048 | tf_op jit(solution)/shard_map/dot_general | solution.py:20
  142.6 2.6 slice.157
  145.3 3.4 %fusion.40 = (bf16[240,1536]{1,0:T(8,128)(2,1)}, bf16[240,1536]{1,0:T(8,128)(2,1)S(1)}) fusion(bf16[240,1536]{1,0:T(8,128)(2,1)} %copy-done.12, f32[240,1536]{1,0:T(8,128)} %get-tuple-element.62, bf16[240,1536]{1,0:T(8,128)(2,1)} %collective-permute-done.3), kind=kLoop, calls=%fused_computation.63 | loop fusion | flops 5529600 | bytes 4423680 | tf_op jit(solution)/shard_map/convert_element_type | solution.py:144
  148.7 9.3 %fusion.78 = f32[240,6144]{1,0:T(8,128)S(1)} fusion(bf16[240,1536]{1,0:T(8,128)(2,1)S(1)} %get-tuple-element.30, bf16[6144,1536]{1,0:T(8,128)(2,1)} %param.10), kind=kOutput, calls=%fused_computation.164 | convolution fusion | flops 4529848320 | bytes 25509888 | tf_op jit(solution)/shard_map/dot_general | solution.py:20
  158.1 2.6 copy-done.1
  162.5 10.7 %fusion.77 = (bf16[240,1536]{1,0:T(8,128)(2,1)}, f32[240,1536]{1,0:T(8,128)}) fusion(bf16[1536,6144]{1,0:T(8,128)(2,1)} %param.11, bf16[120,6144]{1,0:T(8,128)(2,1)} %collective-permute-done.15, bf16[40,6144]{1,0:T(8,128)(2,1)S(1)} %get-tuple-element.42, bf16[40,6144]{1,0:T(8,128)(2,1)S(1)} %collective-permute-done.12, ...), kind=kOutput, calls=%fused_computation.163 | convolution fusion | flops 4542013440 | bytes 24035328 | tf_op jit(solution)/shard_map/dot_general | solution.py:20
  175.4 2.6 constant_dynamic-update-slice_fusion.17
  178.0 14.0 %collective-permute-done.16 = bf16[240,1536]{1,0:T(8,128)(2,1)S(1)} collective-permute-done((bf16[240,1536]{1,0:T(8,128)(2,1)}, bf16[240,1536]{1,0:T(8,128)(2,1)S(1)}, u32[]{:S(2)}, u32[]{:S(2)}) %collective-permute-start.16) | collective-permute-done | bytes 737312 | tf_op jit(solution)/shard_map/ppermute | solution.py:96
  193.7 12.0 %fusion.80 = f32[240,6144]{1,0:T(8,128)} fusion(bf16[240,1536]{1,0:T(8,128)(2,1)S(1)} %get-tuple-element.32, bf16[6144,1536]{1,0:T(8,128)(2,1)} %param.10), kind=kOutput, calls=%fused_computation.166 | convolution fusion | flops 4529848320 | bytes 25509888 | tf_op jit(solution)/shard_map/dot_general | solution.py:20
  209.6 21.6 %multiply_convert_fusion = bf16[1536,6144]{1,0:T(8,128)(2,1)} fusion(bf16[640,6144]{1,0:T(8,128)(2,1)} %constant_dynamic-update-slice_fusion.17, bf16[240,1536]{1,0:T(8,128)(2,1)} %get-tuple-element.31, bf16[160,1536]{1,0:T(8,128)(2,1)S(1)} %get-tuple-element.33, bf16[240,1536]{1,0:T(8,128)(2,1)S(1)} %copy-done.21), kind=kOutput, calls=%fused_computation | convolution fusion | flops 12104368128 | bytes 28704768 | tf_op jit(solution)/shard_map/dot_general | solution.py:26
  231.2 2.7 slice_dynamic-update-slice_fusion.1
  235.6 2.2 slice_dynamic-update-slice_fusion.2
  238.6 2.2 fusion.72
  241.3 2.0 collective-permute-start.22
  244.1 5.4 %collective-permute-done.18 = bf16[40,3072]{1,0:T(8,128)(2,1)S(1)} collective-permute-done((bf16[40,3072]{1,0:T(8,128)(2,1)S(1)}, bf16[40,3072]{1,0:T(8,128)(2,1)S(1)}, u32[]{:S(2)}, u32[]{:S(2)}) %collective-permute-start.18) | collective-permute-done | bytes 245792 | tf_op jit(solution)/shard_map/ppermute | solution.py:165
  253.3 9.3 %collective-permute-done.19 = bf16[40,6144]{1,0:T(8,128)(2,1)S(1)} collective-permute-done((bf16[40,6144]{1,0:T(8,128)(2,1)S(1)}, bf16[40,6144]{1,0:T(8,128)(2,1)S(1)}, u32[]{:S(2)}, u32[]{:S(2)}) %collective-permute-start.19) | collective-permute-done | bytes 491552 | tf_op jit(solution)/shard_map/ppermute | solution.py:173
  263.1 2.5 collective-permute-start.20
  265.6 2.7 slice_dynamic-update-slice_fusion
  268.3 6.7 %collective-permute-done.20 = bf16[40,6144]{1,0:T(8,128)(2,1)S(1)} collective-permute-done((bf16[40,6144]{1,0:T(8,128)(2,1)S(1)}, bf16[40,6144]{1,0:T(8,128)(2,1)S(1)}, u32[]{:S(2)}, u32[]{:S(2)}) %collective-permute-start.20) | collective-permute-done | bytes 491552 | tf_op jit(solution)/shard_map/ppermute | solution.py:173
  275.0 2.2 collective-permute-done.24
  279.4 21.4 %multiply_convert_fusion.1 = bf16[6144,1536]{1,0:T(8,128)(2,1)} fusion(bf16[640,6144]{1,0:T(8,128)(2,1)} %slice_dynamic-update-slice_fusion, bf16[240,1536]{1,0:T(8,128)(2,1)S(1)} %copy-done.20, bf16[160,1536]{1,0:T(8,128)(2,1)S(1)} %get-tuple-element.34, bf16[240,1536]{1,0:T(8,128)(2,1)S(1)} %copy-done.18), kind=kOutput, calls=%fused_computation.1 | convolution fusion | flops 12104368128 | bytes 28704768 | tf_op jit(solution)/shard_map/dot_general | solution.py:26
  (164 shorter events, 68.8 us)
Async XLA Ops:
  0.6 30.0 %collective-permute-start.1 = (bf16[40,6144]{1,0:T(8,128)(2,1)}, bf16[40,6144]{1,0:T(8,128)(2,1)S(1)}, u32[]{:S(2)}, u32[]{:S(2)}) collective-permute-start(bf16[40,6144]{1,0:T(8,128)(2,1)} %param.9), channel_id=1, source_target_pairs={{0,8},{4,12},{1,0},{5,4},{2,1},{6,5},{3,2},{7,6},{11,3},{15,7},{10... | collective-permute-start | bytes 1474568 | tf_op jit(solution)/shard_map/ppermute | solution.py:81
  3.6 27.0 %collective-permute-start = (bf16[40,6144]{1,0:T(8,128)(2,1)}, bf16[40,6144]{1,0:T(8,128)(2,1)S(1)}, u32[]{:S(2)}, u32[]{:S(2)}) collective-permute-start(bf16[40,6144]{1,0:T(8,128)(2,1)} %param.9), channel_id=1, source_target_pairs={{0,1},{4,5},{1,2},{5,6},{2,3},{6,7},{3,11},{7,15},{11,10},{15,14},... | collective-permute-start | bytes 1474568 | tf_op jit(solution)/shard_map/ppermute | solution.py:80
  3.8 29.4 %collective-permute-start.26 = (bf16[40,6144]{1,0:T(8,128)(2,1)}, bf16[40,6144]{1,0:T(8,128)(2,1)}, u32[]{:S(2)}, u32[]{:S(2)}) collective-permute-start(bf16[40,6144]{1,0:T(8,128)(2,1)} %param.7), channel_id=1, source_target_pairs={{0,1},{4,5},{1,2},{5,6},{2,3},{6,7},{3,11},{7,15},{11,10},{15,14},... | collective-permute-start | bytes 1474568 | tf_op jit(solution)/shard_map/ppermute | solution.py:80
  5.7 30.8 %collective-permute-start.27 = (bf16[40,6144]{1,0:T(8,128)(2,1)}, bf16[40,6144]{1,0:T(8,128)(2,1)}, u32[]{:S(2)}, u32[]{:S(2)}) collective-permute-start(bf16[40,6144]{1,0:T(8,128)(2,1)} %param.7), channel_id=1, source_target_pairs={{0,8},{4,12},{1,0},{5,4},{2,1},{6,5},{3,2},{7,6},{11,3},{15,7},{10... | collective-permute-start | bytes 1474568 | tf_op jit(solution)/shard_map/ppermute | solution.py:81
  5.8 34.4 %collective-permute-start.4 = (bf16[320,1536]{1,0:T(8,128)(2,1)}, bf16[320,1536]{1,0:T(8,128)(2,1)}, u32[]{:S(2)}, u32[]{:S(2)}) collective-permute-start(bf16[320,1536]{1,0:T(8,128)(2,1)} %param.8), channel_id=1, source_target_pairs={{0,16},{16,0},{1,17},{17,1},{2,18},{18,2},{3,19},{19,3},{4,20},{20... | collective-permute-start | bytes 2949128 | tf_op jit(solution)/shard_map/ppermute | solution.py:96
  30.7 56.4 %collective-permute-start.2 = (bf16[120,6144]{1,0:T(8,128)(2,1)S(1)}, bf16[120,6144]{1,0:T(8,128)(2,1)S(1)}, u32[]{:S(2)}, u32[]{:S(2)}) collective-permute-start(bf16[120,6144]{1,0:T(8,128)(2,1)S(1)} %pad_maximum_fusion), channel_id=1, source_target_pairs={{0,4},{4,0},{1,5},{5,1},{2,6},{6,2},{3,7},{7,3},{11,15},{15,11},{1... | collective-permute-start | bytes 4423688 | tf_op jit(solution)/shard_map/ppermute | solution.py:89
  30.8 17.8 %collective-permute-start.7 = (bf16[40,6144]{1,0:T(8,128)(2,1)S(1)}, bf16[40,6144]{1,0:T(8,128)(2,1)S(1)}, u32[]{:S(2)}, u32[]{:S(2)}) collective-permute-start(bf16[40,6144]{1,0:T(8,128)(2,1)S(1)} %collective-permute-done.1), channel_id=1, source_target_pairs={{0,8},{4,12},{1,0},{5,4},{2,1},{6,5},{3,2},{7,6},{11,3},{15,7},{10... | collective-permute-start | bytes 1474568 | tf_op jit(solution)/shard_map/ppermute | solution.py:81
  33.2 14.1 %collective-permute-start.6 = (bf16[40,6144]{1,0:T(8,128)(2,1)S(1)}, bf16[40,6144]{1,0:T(8,128)(2,1)S(1)}, u32[]{:S(2)}, u32[]{:S(2)}) collective-permute-start(bf16[40,6144]{1,0:T(8,128)(2,1)S(1)} %collective-permute-done), channel_id=1, source_target_pairs={{0,1},{4,5},{1,2},{5,6},{2,3},{6,7},{3,11},{7,15},{11,10},{15,14},... | collective-permute-start | bytes 1474568 | tf_op jit(solution)/shard_map/ppermute | solution.py:80
  36.6 21.2 %collective-permute-start.28 = (bf16[40,6144]{1,0:T(8,128)(2,1)}, bf16[40,6144]{1,0:T(8,128)(2,1)S(1)}, u32[]{:S(2)}, u32[]{:S(2)}) collective-permute-start(bf16[40,6144]{1,0:T(8,128)(2,1)} %collective-permute-done.26), channel_id=1, source_target_pairs={{0,1},{4,5},{1,2},{5,6},{2,3},{6,7},{3,11},{7,15},{11,10},{15,14},... | collective-permute-start | bytes 1474568 | tf_op jit(solution)/shard_map/ppermute | solution.py:80
  40.2 18.9 %collective-permute-start.29 = (bf16[40,6144]{1,0:T(8,128)(2,1)}, bf16[40,6144]{1,0:T(8,128)(2,1)S(1)}, u32[]{:S(2)}, u32[]{:S(2)}) collective-permute-start(bf16[40,6144]{1,0:T(8,128)(2,1)} %collective-permute-done.27), channel_id=1, source_target_pairs={{0,8},{4,12},{1,0},{5,4},{2,1},{6,5},{3,2},{7,6},{11,3},{15,7},{10... | collective-permute-start | bytes 1474568 | tf_op jit(solution)/shard_map/ppermute | solution.py:81
  47.2 33.1 %collective-permute-start.11 = (bf16[40,6144]{1,0:T(8,128)(2,1)S(1)}, bf16[40,6144]{1,0:T(8,128)(2,1)S(1)}, u32[]{:S(2)}, u32[]{:S(2)}) collective-permute-start(bf16[40,6144]{1,0:T(8,128)(2,1)S(1)} %collective-permute-done.6), channel_id=1, source_target_pairs={{0,1},{4,5},{1,2},{5,6},{2,3},{6,7},{3,11},{7,15},{11,10},{15,14},... | collective-permute-start | bytes 1474568 | tf_op jit(solution)/shard_map/ppermute | solution.py:80
  49.5 31.5 %collective-permute-start.12 = (bf16[40,6144]{1,0:T(8,128)(2,1)S(1)}, bf16[40,6144]{1,0:T(8,128)(2,1)S(1)}, u32[]{:S(2)}, u32[]{:S(2)}) collective-permute-start(bf16[40,6144]{1,0:T(8,128)(2,1)S(1)} %collective-permute-done.7), channel_id=1, source_target_pairs={{0,8},{4,12},{1,0},{5,4},{2,1},{6,5},{3,2},{7,6},{11,3},{15,7},{10... | collective-permute-start | bytes 1474568 | tf_op jit(solution)/shard_map/ppermute | solution.py:81
  57.8 20.3 %collective-permute-start.30 = (bf16[40,6144]{1,0:T(8,128)(2,1)S(1)}, bf16[40,6144]{1,0:T(8,128)(2,1)S(1)}, u32[]{:S(2)}, u32[]{:S(2)}) collective-permute-start(bf16[40,6144]{1,0:T(8,128)(2,1)S(1)} %collective-permute-done.28), channel_id=1, source_target_pairs={{0,1},{4,5},{1,2},{5,6},{2,3},{6,7},{3,11},{7,15},{11,10},{15,14},... | collective-permute-start | bytes 1474568 | tf_op jit(solution)/shard_map/ppermute | solution.py:80
  59.1 16.9 %collective-permute-start.31 = (bf16[40,6144]{1,0:T(8,128)(2,1)S(1)}, bf16[40,6144]{1,0:T(8,128)(2,1)S(1)}, u32[]{:S(2)}, u32[]{:S(2)}) collective-permute-start(bf16[40,6144]{1,0:T(8,128)(2,1)S(1)} %collective-permute-done.29), channel_id=1, source_target_pairs={{0,8},{4,12},{1,0},{5,4},{2,1},{6,5},{3,2},{7,6},{11,3},{15,7},{10... | collective-permute-start | bytes 1474568 | tf_op jit(solution)/shard_map/ppermute | solution.py:81
  80.3 18.2 %collective-permute-start.8 = (bf16[80,6144]{1,0:T(8,128)(2,1)}, bf16[80,6144]{1,0:T(8,128)(2,1)}, u32[]{:S(2)}, u32[]{:S(2)}) collective-permute-start(bf16[80,6144]{1,0:T(8,128)(2,1)} %pad_maximum_fusion.2), channel_id=1, source_target_pairs={{0,4},{4,0},{1,5},{5,1},{2,6},{6,2},{3,7},{7,3},{11,15},{15,11},{1... | collective-permute-start | bytes 2949128 | tf_op jit(solution)/shard_map/ppermute | solution.py:89
  81.1 36.1 %collective-permute-start.13 = (bf16[40,3072]{1,0:T(8,128)(2,1)}, bf16[40,3072]{1,0:T(8,128)(2,1)}, u32[]{:S(2)}, u32[]{:S(2)}) collective-permute-start(bf16[40,3072]{1,0:T(8,128)(2,1)} %slice.108), channel_id=1, source_target_pairs={{0,1},{4,5},{1,2},{5,6},{2,3},{6,7},{3,11},{7,15},{11,10},{15,14},... | collective-permute-start | bytes 737288 | tf_op jit(solution)/shard_map/ppermute | solution.py:76
  83.6 35.2 %collective-permute-start.14 = (bf16[40,3072]{1,0:T(8,128)(2,1)}, bf16[40,3072]{1,0:T(8,128)(2,1)}, u32[]{:S(2)}, u32[]{:S(2)}) collective-permute-start(bf16[40,3072]{1,0:T(8,128)(2,1)} %slice.109), channel_id=1, source_target_pairs={{0,8},{4,12},{1,0},{5,4},{2,1},{6,5},{3,2},{7,6},{11,3},{15,7},{10... | collective-permute-start | bytes 737288 | tf_op jit(solution)/shard_map/ppermute | solution.py:77
  87.1 144.1 %collective-permute-start.34 = (bf16[320,6144]{1,0:T(8,128)(2,1)}, bf16[320,6144]{1,0:T(8,128)(2,1)}, u32[]{:S(2)}, u32[]{:S(2)}) collective-permute-start(bf16[320,6144]{1,0:T(8,128)(2,1)} %maximum_dynamic-update-slice_fusion), channel_id=1, source_target_pairs={{0,4},{4,0},{1,5},{5,1},{2,6},{6,2},{3,7},{7,3},{11,15},{15,11},{1... | collective-permute-start | bytes 11796488 | tf_op jit(solution)/shard_map/ppermute | solution.py:182
  97.8 47.5 %collective-permute-start.3 = (bf16[240,1536]{1,0:T(8,128)(2,1)}, bf16[240,1536]{1,0:T(8,128)(2,1)}, u32[]{:S(2)}, u32[]{:S(2)}) collective-permute-start(bf16[240,1536]{1,0:T(8,128)(2,1)} %get-tuple-element.61), channel_id=1, source_target_pairs={{0,16},{16,0},{1,17},{17,1},{2,18},{18,2},{3,19},{19,3},{4,20},{20... | collective-permute-start | bytes 2211848 | tf_op jit(solution)/shard_map/ppermute | solution.py:96
  109.0 18.5 %collective-permute-start.9 = (bf16[160,1536]{1,0:T(8,128)(2,1)S(1)}, bf16[160,1536]{1,0:T(8,128)(2,1)S(1)}, u32[]{:S(2)}, u32[]{:S(2)}) collective-permute-start(bf16[160,1536]{1,0:T(8,128)(2,1)S(1)} %get-tuple-element.63), channel_id=1, source_target_pairs={{0,16},{16,0},{1,17},{17,1},{2,18},{18,2},{3,19},{19,3},{4,20},{20... | collective-permute-start | bytes 1474568 | tf_op jit(solution)/shard_map/ppermute | solution.py:96
  121.7 40.8 %collective-permute-start.15 = (bf16[120,6144]{1,0:T(8,128)(2,1)}, bf16[120,6144]{1,0:T(8,128)(2,1)}, u32[]{:S(2)}, u32[]{:S(2)}) collective-permute-start(bf16[120,6144]{1,0:T(8,128)(2,1)} %pad_maximum_fusion.1), channel_id=1, source_target_pairs={{0,4},{4,0},{1,5},{5,1},{2,6},{6,2},{3,7},{7,3},{11,15},{15,11},{1... | collective-permute-start | bytes 4423688 | tf_op jit(solution)/shard_map/ppermute | solution.py:89
  145.3 28.6 %collective-permute-start.10 = (bf16[80,6144]{1,0:T(8,128)(2,1)}, bf16[80,6144]{1,0:T(8,128)(2,1)}, u32[]{:S(2)}, u32[]{:S(2)}) collective-permute-start(bf16[80,6144]{1,0:T(8,128)(2,1)} %slice.157), channel_id=1, source_target_pairs={{0,4},{4,0},{1,5},{5,1},{2,6},{6,2},{3,7},{7,3},{11,15},{15,11},{1... | collective-permute-start | bytes 2949128 | tf_op jit(solution)/shard_map/ppermute | solution.py:153
  162.0 45.8 %collective-permute-start.5 = (bf16[120,6144]{1,0:T(8,128)(2,1)}, bf16[120,6144]{1,0:T(8,128)(2,1)}, u32[]{:S(2)}, u32[]{:S(2)}) collective-permute-start(bf16[120,6144]{1,0:T(8,128)(2,1)} %slice.156), channel_id=1, source_target_pairs={{0,4},{4,0},{1,5},{5,1},{2,6},{6,2},{3,7},{7,3},{11,15},{15,11},{1... | collective-permute-start | bytes 4423688 | tf_op jit(solution)/shard_map/ppermute | solution.py:153
  173.2 18.8 %collective-permute-start.16 = (bf16[240,1536]{1,0:T(8,128)(2,1)}, bf16[240,1536]{1,0:T(8,128)(2,1)S(1)}, u32[]{:S(2)}, u32[]{:S(2)}) collective-permute-start(bf16[240,1536]{1,0:T(8,128)(2,1)} %get-tuple-element.65), channel_id=1, source_target_pairs={{0,16},{16,0},{1,17},{17,1},{2,18},{18,2},{3,19},{19,3},{4,20},{20... | collective-permute-start | bytes 2211848 | tf_op jit(solution)/shard_map/ppermute | solution.py:96
  207.7 31.0 %collective-permute-start.17 = (bf16[120,6144]{1,0:T(8,128)(2,1)S(1)}, bf16[120,6144]{1,0:T(8,128)(2,1)S(1)}, u32[]{:S(2)}, u32[]{:S(2)}) collective-permute-start(bf16[120,6144]{1,0:T(8,128)(2,1)S(1)} %slice.155), channel_id=1, source_target_pairs={{0,4},{4,0},{1,5},{5,1},{2,6},{6,2},{3,7},{7,3},{11,15},{15,11},{1... | collective-permute-start | bytes 4423688 | tf_op jit(solution)/shard_map/ppermute | solution.py:153
  240.9 8.6 %collective-permute-start.18 = (bf16[40,3072]{1,0:T(8,128)(2,1)S(1)}, bf16[40,3072]{1,0:T(8,128)(2,1)S(1)}, u32[]{:S(2)}, u32[]{:S(2)}) collective-permute-start(bf16[40,3072]{1,0:T(8,128)(2,1)S(1)} %get-tuple-element.27), channel_id=1, source_target_pairs={{0,1},{4,5},{1,2},{5,6},{2,3},{6,7},{3,11},{7,15},{11,10},{15,14},... | collective-permute-start | bytes 737288 | tf_op jit(solution)/shard_map/ppermute | solution.py:165
  249.8 12.8 %collective-permute-start.19 = (bf16[40,6144]{1,0:T(8,128)(2,1)S(1)}, bf16[40,6144]{1,0:T(8,128)(2,1)S(1)}, u32[]{:S(2)}, u32[]{:S(2)}) collective-permute-start(bf16[40,6144]{1,0:T(8,128)(2,1)S(1)} %get-tuple-element.7), channel_id=1, source_target_pairs={{0,1},{4,5},{1,2},{5,6},{2,3},{6,7},{3,11},{7,15},{11,10},{15,14},... | collective-permute-start | bytes 1474568 | tf_op jit(solution)/shard_map/ppermute | solution.py:173
  250.7 12.2 %collective-permute-start.23 = (bf16[40,6144]{1,0:T(8,128)(2,1)S(1)}, bf16[40,6144]{1,0:T(8,128)(2,1)S(1)}, u32[]{:S(2)}, u32[]{:S(2)}) collective-permute-start(bf16[40,6144]{1,0:T(8,128)(2,1)S(1)} %get-tuple-element.8), channel_id=1, source_target_pairs={{0,8},{4,12},{1,0},{5,4},{2,1},{6,5},{3,2},{7,6},{11,3},{15,7},{10... | collective-permute-start | bytes 1474568 | tf_op jit(solution)/shard_map/ppermute | solution.py:174
  263.1 11.9 %collective-permute-start.20 = (bf16[40,6144]{1,0:T(8,128)(2,1)S(1)}, bf16[40,6144]{1,0:T(8,128)(2,1)S(1)}, u32[]{:S(2)}, u32[]{:S(2)}) collective-permute-start(bf16[40,6144]{1,0:T(8,128)(2,1)S(1)} %get-tuple-element.9), channel_id=1, source_target_pairs={{0,1},{4,5},{1,2},{5,6},{2,3},{6,7},{3,11},{7,15},{11,10},{15,14},... | collective-permute-start | bytes 1474568 | tf_op jit(solution)/shard_map/ppermute | solution.py:173
  265.6 11.6 %collective-permute-start.24 = (bf16[40,6144]{1,0:T(8,128)(2,1)S(1)}, bf16[40,6144]{1,0:T(8,128)(2,1)S(1)}, u32[]{:S(2)}, u32[]{:S(2)}) collective-permute-start(bf16[40,6144]{1,0:T(8,128)(2,1)S(1)} %get-tuple-element.10), channel_id=1, source_target_pairs={{0,8},{4,12},{1,0},{5,4},{2,1},{6,5},{3,2},{7,6},{11,3},{15,7},{10... | collective-permute-start | bytes 1474568 | tf_op jit(solution)/shard_map/ppermute | solution.py:174
  277.3 23.4 %collective-permute-start.25 = (bf16[40,6144]{1,0:T(8,128)(2,1)S(1)}, bf16[40,6144]{1,0:T(8,128)(2,1)S(1)}, u32[]{:S(2)}, u32[]{:S(2)}) collective-permute-start(bf16[40,6144]{1,0:T(8,128)(2,1)S(1)} %get-tuple-element.6), channel_id=1, source_target_pairs={{0,8},{4,12},{1,0},{5,4},{2,1},{6,5},{3,2},{7,6},{11,3},{15,7},{10... | collective-permute-start | bytes 1474568 | tf_op jit(solution)/shard_map/ppermute | solution.py:174
  277.7 23.1 %collective-permute-start.21 = (bf16[40,6144]{1,0:T(8,128)(2,1)S(1)}, bf16[40,6144]{1,0:T(8,128)(2,1)S(1)}, u32[]{:S(2)}, u32[]{:S(2)}) collective-permute-start(bf16[40,6144]{1,0:T(8,128)(2,1)S(1)} %get-tuple-element.5), channel_id=1, source_target_pairs={{0,1},{4,5},{1,2},{5,6},{2,3},{6,7},{3,11},{7,15},{11,10},{15,14},... | collective-permute-start | bytes 1474568 | tf_op jit(solution)/shard_map/ppermute | solution.py:173
  (31 other events, 483.5 us)

commit v2 on v0

v2 whole, which is shorter than its diff:
```python
import math

import jax
import jax.numpy as jnp
from jax import lax
from jax.experimental import pallas as pl
from jax.experimental.pallas import tpu as pltpu
from jax.sharding import PartitionSpec as P

RING = ("gy", "gz")


class Ring:
    def __init__(self, gy, gz):
        self.cores = 2 if gy % 2 == 0 else 1
        chips = []
        for x in range(gy // self.cores):
            line = range(gz) if x % 2 == 0 else reversed(range(gz))
            chips += [(x, z) for z in line]
        self.size, self.line = len(chips), gz
        self.half = self.size // 2
        self.even = self.size % 2 == 0
        self.rank = [
            [(x * self.cores + core) * gz + z for core in range(self.cores)] for x, z in chips
        ]

    def place(self, x, z):
        return x * self.line + jnp.where(x % 2 == 0, z, self.line - 1 - z)

    def rank_at(self, place, core):
        x, z = place // self.line, place % self.line
        return (x * 2 + core) * self.line + jnp.where(x % 2 == 0, z, self.line - 1 - z)

    def shift(self, by):
        pairs = []
        for place in range(self.size):
            target = (place + by) % self.size
            for core in range(self.cores):
                pairs.append((self.rank[place][core], self.rank[target][core]))
        return pairs

    def swap(self):
        return [(ranks[core], ranks[1 - core]) for ranks in self.rank for core in range(2)]

    def groups(self):
        cut = max(self.half - 1, 1)
        return [list(range(cut)), list(range(cut, self.half + 1))]

    def offsets(self, step):
        if step == 0:
            return [0]
        if step == self.half and self.even:
            return [self.half]
        return [-step, step]


def gelu_parts(values):
    normal_cdf = 0.5 * (1.0 + lax.erf(values / math.sqrt(2.0)))
    activity = values * normal_cdf
    slope = normal_cdf + values * jnp.exp(-0.5 * values * values) / math.sqrt(2.0 * math.pi)
    return (activity, slope)


def right_trans(left, right):
    return lax.dot_general(
        left, right, (((1,), (1,)), ((), ())), preferred_element_type=jnp.float32
    )


def left_trans(left, right):
    return lax.dot_general(
        left, right, (((0,), (0,)), ((), ())), preferred_element_type=jnp.float32
    )


VMEM = pl.BlockSpec(memory_space=pltpu.VMEM)
SMEM = pl.BlockSpec(memory_space=pltpu.SMEM)
MIB = 1 << 20


def shape(rows, columns, dtype=jnp.bfloat16):
    return jax.ShapeDtypeStruct((rows, columns), dtype)


def in_hbm(rows, columns, dtype=jnp.bfloat16):
    return pltpu.HBM((rows, columns), dtype)


def constrained(arrays):
    return [pltpu.with_memory_space_constraint(each, pltpu.HBM) for each in arrays]


def cost(flops, moved, exps=0):
    return pl.CostEstimate(flops=flops, bytes_accessed=moved, transcendentals=exps)


def tile_of(total, most):
    for tile in range(most, 127, -128):
        if total % tile == 0:
            return tile
    return total


def gelu_call(ring, pres, offsets, rows):
    held, hidden = pres[0].shape
    many, count = sum(each.shape[0] for each in pres) // held, 2 * len(offsets)

    def kernel(*refs):
        given, (act_ref, slope_ref, wide) = refs[:-3], refs[-3:]
        at = 0
        for ref in given:
            wide[at : at + ref.shape[0], :] = ref[...].astype(jnp.float32)
            at += ref.shape[0]
        me, gy = lax.axis_index("gx"), lax.axis_index("gy")
        place = ring.place(gy // 2, lax.axis_index("gz"))
        for block in range(count):
            which, offset = divmod(block, len(offsets))
            there = (place + offsets[offset] + ring.size) % ring.size
            rank = ring.rank_at(there, (gy + which) % 2)
            slot = (me - rank * rows // held + many) % many
            at = pl.multiple_of(slot * held + rank * rows % held, 8)
            activity, slope = gelu_parts(wide[pl.ds(at, rows), :])
            act_ref[block * rows : (block + 1) * rows, :] = activity.astype(act_ref.dtype)
            slope_ref[block * rows : (block + 1) * rows, :] = slope

    return pl.pallas_call(
        kernel,
        grid=(1,),
        in_specs=[VMEM] * len(pres),
        out_specs=[whole(count * rows, hidden)] * 2,
        out_shape=[in_hbm(count * rows, hidden), in_hbm(count * rows, hidden, jnp.float32)],
        scratch_shapes=[pltpu.VMEM((many * held, hidden), jnp.float32)],
        cost_estimate=cost(6000 * count * rows * hidden, 1),
        compiler_params=pltpu.CompilerParams(vmem_limit_bytes=10 * MIB),
        name="gelu",
    )(*pres)


def hold_call(weights):
    rows = weights.shape[0]
    cut = rows // 4
    weights = pltpu.with_memory_space_constraint(weights, pltpu.HBM)

    def kernel(weight_ref, out_ref, here_ref, sems):
        here_ref[...] = jnp.zeros_like(here_ref)
        copies = [
            pltpu.make_async_copy(
                weight_ref.at[pl.ds(i * cut, cut)], out_ref.at[pl.ds(i * cut, cut)], sems.at[i]
            )
            for i in range(4)
        ]
        for copy in copies:
            copy.start()
        for copy in copies:
            copy.wait()

    return pl.pallas_call(
        kernel,
        in_specs=[pl.BlockSpec(memory_space=pl.ANY)],
        out_specs=[VMEM] * 2,
        out_shape=[pltpu.VMEM(weights.shape, weights.dtype), shape(8, 128, jnp.float32)],
        scratch_shapes=[pltpu.SemaphoreType.DMA((4,))],
        cost_estimate=cost(1, 1),
        compiler_params=pltpu.CompilerParams(vmem_limit_bytes=10 * MIB),
        name="hold",
    )(weights)


def whole(rows, columns):
    return pl.BlockSpec((rows, columns), lambda i: (0, 0), pipeline_mode=pl.Buffered(1))


def split_call(left, right, cut):
    def kernel(left_ref, right_ref, low_ref, high_ref):
        low_ref[...] = left_ref[:, :cut]
        high_ref[...] = right_ref[:, cut:]

    rows, width = left.shape
    return pl.pallas_call(
        kernel,
        in_specs=[VMEM] * 2,
        out_specs=[VMEM] * 2,
        out_shape=[shape(rows, cut), shape(rows, width - cut)],
        cost_estimate=cost(1, 1),
        compiler_params=pltpu.CompilerParams(vmem_limit_bytes=10 * MIB),
        name="split",
    )(left, right)


def parts_call(values):
    rows, width = values.shape
    cut = rows * 2 // 5 // 16 * 16

    def kernel(ref, upper_ref, lower_ref):
        upper_ref[...] = ref[:cut, :]
        lower_ref[...] = ref[cut:, :]

    return pl.pallas_call(
        kernel,
        in_specs=[VMEM],
        out_specs=[VMEM] * 2,
        out_shape=[shape(cut, width), shape(rows - cut, width)],
        cost_estimate=cost(1, 1),
        compiler_params=pltpu.CompilerParams(vmem_limit_bytes=10 * MIB),
        name="parts",
    )(values)


def pack_call(blocks, rows, width):
    flat = [piece for block in blocks for piece in block]

    def kernel(*refs):
        given, out_ref = iter(refs), refs[-1]
        for i, block in enumerate(blocks):
            at = 0
            for piece in block:
                size = piece.shape[1]
                out_ref[i * rows : (i + 1) * rows, at : at + size] = next(given)[...]
                at += size

    return pl.pallas_call(
        kernel,
        grid=(1,),
        in_specs=[VMEM] * len(flat),
        out_specs=whole(len(blocks) * rows, width),
        out_shape=in_hbm(len(blocks) * rows, width),
        cost_estimate=cost(1, 1),
        compiler_params=pltpu.CompilerParams(vmem_limit_bytes=8 * MIB),
        name="pack",
    )(*flat)


def add_call(mine, theirs, places, arrived, rows, outs):
    width = mine.shape[1]
    flat = [value for block in arrived for value, _ in block]

    def kernel(*refs):
        wide, theirs_ref = refs[: len(places)], refs[len(places)]
        given = iter(refs[len(places) + 1 : len(refs) - len(outs) - len(places)])
        made = refs[len(refs) - len(places) :]
        for i, (place, block) in enumerate(zip(places, arrived)):
            at = slice(place * rows, (place + 1) * rows)
            made[i][...] = wide[i][...] + theirs_ref[at, :].astype(jnp.float32)
            for value, first in block:
                columns = slice(first, first + value.shape[1])
                made[i][:, columns] += next(given)[...].astype(jnp.float32)
        for ref, (i, first, last) in zip(refs[-len(outs) - len(places) :], outs):
            ref[...] = made[i][:, first:last].astype(ref.dtype)

    return pl.pallas_call(
        kernel,
        grid=(1,),
        in_specs=[
            pl.BlockSpec((rows, width), lambda i, p=p: (p, 0), pipeline_mode=pl.Buffered(1))
            for p in places
        ]
        + [VMEM] * (1 + len(flat)),
        out_specs=[VMEM] * len(outs),
        out_shape=[shape(rows, last - first) for _, first, last in outs],
        scratch_shapes=[pltpu.VMEM((rows, width), jnp.float32)] * len(places),
        cost_estimate=cost(1, 1),
        compiler_params=pltpu.CompilerParams(vmem_limit_bytes=8 * MIB),
        name="add",
    )(*constrained([mine] * len(places)), theirs, *flat)


def grad_act_call(blocks, weights, rows, cuts):
    hidden, width = weights.shape
    flat = [piece for block in blocks for piece in block]
    count = len(blocks) * rows
    tile = tile_of(hidden, 256)
    steps = hidden // tile
    spans = list(zip([0] + cuts, cuts + [count]))

    def kernel(*refs):
        weight_ref, chunk_ref, part_ref, *low_refs, joined, sem = refs[len(flat) :]
        i = pl.program_id(0)
        copy = pltpu.make_async_copy(joined, chunk_ref, sem)

        @pl.when(i == 0)
        def _():
            given = iter(refs)
            for j, block in enumerate(blocks):
                at = 0
                for piece in block:
                    size = piece.shape[1]
                    joined[j * rows : (j + 1) * rows, at : at + size] = next(given)[...]
                    at += size
            copy.start()

        at = pl.ds(pl.multiple_of(i * tile, tile), tile)
        got = right_trans(joined[...], weight_ref[at, :])
        part_ref[...] = got
        for ref, (begin, end) in zip(low_refs, spans):
            ref[...] = got[begin:end].astype(ref.dtype)

        @pl.when(i == steps - 1)
        def _():
            copy.wait()

    return pl.pallas_call(
        kernel,
        grid=(steps,),
        in_specs=[VMEM] * (len(flat) + 1),
        out_specs=[
            pl.BlockSpec(memory_space=pl.ANY),
            pl.BlockSpec((count, tile), lambda i: (0, i)),
        ]
        + [pl.BlockSpec((end - begin, tile), lambda i: (0, i)) for begin, end in spans],
        out_shape=[in_hbm(count, width), in_hbm(count, hidden, jnp.float32)]
        + [shape(end - begin, hidden) for begin, end in spans],
        scratch_shapes=[pltpu.VMEM((count, width), jnp.bfloat16), pltpu.SemaphoreType.DMA],
        cost_estimate=cost(1, 1),
        compiler_params=pltpu.CompilerParams(vmem_limit_bytes=10 * MIB),
        name="grad_act",
    )(*flat, weights)


def in_grad_call(part, others, slope, weights):
    flat = [piece for pieces in zip(*others) for piece in pieces]
    width, hidden = weights.shape
    count = part.shape[0]
    half = count // 2
    tile = tile_of(width, 1024)

    def kernel(*refs):
        part_ref, slope_ref = refs[:2]
        weight_ref, pre_ref, mine_ref, theirs_ref = refs[-4:]
        i = pl.program_id(0)

        @pl.when(i == 0)
        def _():
            given, at = iter(refs[2:-4]), 0
            for pieces in zip(*others):
                here = slice(at, at + pieces[0].shape[0])
                total = part_ref[here, :]
                for _ in pieces:
                    total = total + next(given)[...].astype(jnp.float32)
                pre_ref[here, :] = (total * slope_ref[here, :]).astype(pre_ref.dtype)
                at = here.stop

        at = pl.ds(pl.multiple_of(i * tile, tile), tile)
        got = right_trans(pre_ref[...], weight_ref[at, :])
        mine_ref[...] = got[:half]
        theirs_ref[...] = got[half:].astype(theirs_ref.dtype)

    return pl.pallas_call(
        kernel,
        grid=(width // tile,),
        in_specs=[whole(count, hidden)] * 2 + [whole(*each.shape) for each in flat] + [VMEM],
        out_specs=[
            whole(count, hidden),
            pl.BlockSpec((half, tile), lambda i: (0, i)),
            pl.BlockSpec((half, tile), lambda i: (0, i)),
        ],
        out_shape=[
            in_hbm(count, hidden),
            in_hbm(half, width, jnp.float32),
            shape(half, width),
        ],
        cost_estimate=cost(1, 1),
        compiler_params=pltpu.CompilerParams(vmem_limit_bytes=14 * MIB),
        name="in_grad",
    )(part, slope, *flat, weights)


def pieces_of(width, most):
    tile = tile_of(width, 1024)
    tiles = width // tile
    calls = min(most, tiles)
    ends = [tiles * i // calls for i in range(calls + 1)]
    return tile, [(first, last - first) for first, last in zip(ends, ends[1:])]


def w_out_grad_call(acts, chunks, factor, tile, first, count, earlier):
    sizes = [chunk.shape[0] for chunk in chunks]
    many, total = len(sizes), sum(sizes)
    hidden, width = acts[0].shape[1], chunks[0].shape[1]

    def kernel(*refs):
        given, tokens, (out_ref, turned) = refs[:many], refs[many : 2 * many], refs[-2:]

        @pl.when(pl.program_id(0) == 0)
        def _():
            turned[...] = jnp.concatenate([ref[...] for ref in given], axis=0).T

        joined = jnp.concatenate([ref[...] for ref in tokens], axis=0)
        got = jnp.dot(turned[...], joined, preferred_element_type=jnp.float32)
        out_ref[...] = (got * factor).astype(out_ref.dtype)

    return pl.pallas_call(
        kernel,
        grid=(count,),
        in_specs=[whole(size, hidden) for size in sizes]
        + [pl.BlockSpec((size, tile), lambda i: (0, first + i)) for size in sizes]
        + [pl.BlockSpec(memory_space=pl.ANY)] * len(earlier),
        out_specs=pl.BlockSpec((hidden, tile), lambda i: (0, first + i)),
        out_shape=shape(hidden, width),
        input_output_aliases={2 * many: 0} if earlier else {},
        scratch_shapes=[pltpu.VMEM((hidden, total), jnp.bfloat16)],
        cost_estimate=cost(3 * total * tile * count * hidden, 2 * hidden * tile * count),
        compiler_params=pltpu.CompilerParams(vmem_limit_bytes=26 * MIB),
        name="w_out_grad",
    )(*acts, *chunks, *earlier)


def w_in_grad_call(blocks, pres, factor, tile, first, count, earlier):
    width = blocks[0].shape[1]
    many, sizes = len(blocks), [pre.shape[0] for pre in pres]
    total, hidden = sum(sizes), pres[0].shape[1]

    def kernel(*refs):
        given, wanted = refs[:many], refs[many : many + len(sizes)]
        out_ref, tokens, grads = refs[-3:]

        @pl.when(pl.program_id(0) == 0)
        def _():
            at = 0
            for ref, size in zip(wanted, sizes):
                grads[at : at + size, :] = ref[...]
                at += size

        at = 0
        for ref in given:
            tokens[at : at + ref.shape[0], :] = ref[...]
            at += ref.shape[0]
        got = left_trans(tokens[...], grads[...])
        out_ref[...] = (got * factor).astype(out_ref.dtype)

    return pl.pallas_call(
        kernel,
        grid=(count,),
        in_specs=[pl.BlockSpec((each.shape[0], tile), lambda i: (0, first + i)) for each in blocks]
        + [whole(size, hidden) for size in sizes]
        + [pl.BlockSpec(memory_space=pl.ANY)] * len(earlier),
        out_specs=pl.BlockSpec((tile, hidden), lambda i: (first + i, 0)),
        out_shape=shape(width, hidden),
        input_output_aliases={many + len(sizes): 0} if earlier else {},
        scratch_shapes=[
            pltpu.VMEM((total, tile), jnp.bfloat16),
            pltpu.VMEM((total, hidden), jnp.bfloat16),
        ],
        cost_estimate=cost(3 * total * tile * count * hidden, 2 * hidden * tile * count),
        compiler_params=pltpu.CompilerParams(vmem_limit_bytes=26 * MIB),
        name="w_in_grad",
    )(*blocks, *pres, *earlier)


def after(values, *others):
    return lax.optimization_barrier((values, others))[0]


class Gather:
    def __init__(self, ring, block, halve):
        self.ring, self.halve = ring, halve
        self.held = {0: [block]}
        self.left = self.right = block
        self.done = 0

    def step(self, *others):
        ring = self.ring
        self.done += 1
        left, right = self.left, self.right
        if others:
            left, right = after((left, right), *others)
        if self.done == ring.half and ring.even:
            if self.halve:
                cut = left.shape[1] // 2
                low, high = split_call(left, right, cut)
                low = lax.ppermute(low, RING, ring.shift(1))
                high = lax.ppermute(high, RING, ring.shift(-1))
                self.held[self.done] = [low, high]
            else:
                self.held[self.done] = [lax.ppermute(left, RING, ring.shift(1))]
        else:
            self.left = lax.ppermute(left, RING, ring.shift(1))
            self.right = lax.ppermute(right, RING, ring.shift(-1))
            self.held[-self.done], self.held[self.done] = [self.left], [self.right]


def other_core(ring, pieces):
    return [lax.ppermute(piece, RING, ring.swap()) for piece in pieces]


def exchange(values, axis):
    size = lax.axis_size(axis)
    return [
        lax.ppermute(values, axis, [(i, (i + by) % size) for i in range(size)])
        for by in range(1, size)
    ]


def shards(inputs, pre_act, out_grad, w_in, w_out):
    ring = Ring(lax.axis_size("gy"), lax.axis_size("gz"))
    assert ring.cores == 2
    rows, width = inputs.shape
    groups = ring.size * 2
    factor = 1.0 / math.sqrt(rows * groups)
    order = [[o for step in group for o in ring.offsets(step)] for group in ring.groups()]

    w_out, here = hold_call(w_out)
    upper, lower = parts_call(pre_act)
    came = [exchange(upper, "gx")]

    grads = Gather(ring, out_grad, True)
    chunks, partials, swapped = [], [], {0: other_core(ring, grads.held[0])}
    for number, offsets in enumerate(order):
        first, last = ring.groups()[number][0], ring.groups()[number][-1]
        while grads.done < last:
            if number > 0 and grads.done >= first:
                grads.step(sent)
            elif grads.done == 1:
                grads.step(here, came[0], swapped[0])
                came.append(exchange(after(lower, came[0], here), "gx"))
            else:
                earlier = [each for offset, each in swapped.items() if abs(offset) < grads.done]
                grads.step(*([earlier, came] if grads.done > 1 else []))
            if number > 0 and grads.done == last:
                pres_x = [pre_act] + [each for pieces in zip(*came) for each in pieces]
                ready = after(pres_x, sent)
                acts, slopes = zip(*[gelu_call(ring, ready, each, rows) for each in order])
            for offset in ring.offsets(grads.done):
                ahead = here if number == 0 else slopes if grads.done == last else sent
                swapped[offset] = other_core(ring, after(grads.held[offset], ahead))
        blocks = [grads.held[o] for o in offsets] + [swapped[o] for o in offsets]
        cuts = [2 * len(blocks) * rows // 5 // 16 * 16] if number == 0 else []
        chunk, partial, *sent = grad_act_call(blocks, w_out, rows, cuts)
        chunks.append(chunk)
        partials.append(partial)
        if number == 0:
            early, late = exchange(sent[0], "gx"), sent[1]
    received = [[each] for each in exchange(sent[0], "gx")]

    tokens = Gather(ring, after(inputs, grads.held[ring.half], swapped), True)
    chunks = constrained(chunks)

    def advance(*others):
        arrived = list(tokens.held.values())[1:]
        if tokens.done < ring.half:
            tokens.step(*others)
        return arrived

    tile, out_cuts = pieces_of(width, 3)
    tile, in_cuts = pieces_of(width, 2)
    w_out_grad, w_in_grad = [], []

    def w_out_piece(*others):
        nonlocal w_out_grad
        first, count = out_cuts.pop(0)
        given = [after(acts[0], *others)] + list(acts[1:])
        w_out_grad = [w_out_grad_call(given, chunks, factor, tile, first, count, w_out_grad)]
        return w_out_grad

    def w_in_piece(*others):
        nonlocal w_in_grad
        first, count = in_cuts.pop(0)
        flat = [each for number in range(len(order)) for each in packed[number]]
        given = constrained([after(pres[0], *others)] + pres[1:])
        w_in_grad = [w_in_grad_call(flat, given, factor, tile, first, count, w_in_grad)]
        return w_in_grad

    w_out_piece(advance(), early)
    arrived = advance()
    w_in = pltpu.with_memory_space_constraint(w_in, pltpu.VMEM)
    if len(out_cuts) > 1:
        w_out_piece(arrived)

    sums, pres = {}, [None] * len(order)

    def in_grad_chunk(i, received, *others):
        partial = after(partials[i], *others)
        pres[i], mine, theirs = in_grad_call(partial, received, slopes[i], w_in)
        return mine, theirs

    def swap_sums(i, mine, theirs):
        got = lax.ppermute(theirs, RING, ring.swap())
        for j, offset in enumerate(order[i]):
            sums[offset] = (mine, got, j)

    def add(offsets, arrived, outs, *others):
        mine, theirs, _ = sums[offsets[0]]
        places = [sums[offset][2] for offset in offsets]
        return add_call(mine, after(theirs, *others), places, arrived, rows, outs)

    packed = {}

    def pack(number, *others):
        blocks = after([tokens.held[o] for o in order[number]], *others)
        packed[number] = [pack_call(blocks, rows, width)]
        return packed[number]

    mine, theirs = in_grad_chunk(1, received, w_out_grad, advance())
    swap_sums(1, mine, theirs)
    right, left, beside = [], [], []
    for step in range(ring.half, 0, -1):
        if step == ring.half and ring.even:
            cut = width // 2
            outs = [(0, 0, cut), (0, cut, width)]
            going = add([step], [[]], outs, beside)
        else:
            cut = 0
            outs = [(0, 0, width), (1, 0, width)]
            going = add([step, -step], [right, left], outs, beside)
        right = [(lax.ppermute(going[0], RING, ring.shift(1)), 0)]
        left = [(lax.ppermute(going[1], RING, ring.shift(-1)), cut)]
        beside = []
        for one in packed.values():
            if len(one) == 1:
                one += other_core(ring, after(one, *going))
        if step == ring.half:
            late = exchange(after(late, *going), "gx")
            if out_cuts:
                beside = w_out_piece(*going)
            beside = [beside, late, list(tokens.held.values())]
            tokens.step(*going)
            if order[0][-1] in tokens.held:
                beside = [beside, pack(0, *going)]
        if 0 not in sums and step <= ring.half - (1 if beside or step < ring.half else 0):
            while tokens.done < ring.half:
                tokens.step(*going)
            mine, theirs = in_grad_chunk(0, list(zip(early, late)), *going, list(packed.values()))
            last = pack(1, *going, pres[0])
            swap_sums(0, mine, after(theirs, right, left, last))
            beside = [pres[0]]
        elif step < ring.half and in_cuts and len(packed) == len(order):
            beside = w_in_piece(*going)
    while tokens.done < ring.half:
        tokens.step()
    for number, offsets in enumerate(order):
        if number not in packed:
            pack(number)
        if len(packed[number]) == 1:
            packed[number] += other_core(ring, packed[number])
    while out_cuts:
        w_out_piece()
    while in_cuts:
        w_in_piece()
    (in_grad,) = add([0], [right + left], [(0, 0, width)])
    return (in_grad, w_in_grad[0], w_out_grad[0])


def solution(mesh):
    placed = (
        P(("gy", "gz"), "gx"),
        P("gx", ("gy", "gz")),
        P(("gy", "gz"), "gx"),
        P("gx", ("gy", "gz")),
        P(("gy", "gz"), "gx"),
    )
    return jax.shard_map(
        shards,
        mesh=mesh,
        in_specs=placed,
        out_specs=(P(("gy", "gz"), "gx"), P("gx", ("gy", "gz")), P(("gy", "gz"), "gx")),
        check_vma=False,
    )
```

time: 465 us -> 185 us (0.40)
  waiting for transfers between devices: 336 us -> 38.7 us
  Pallas kernels: 0 us -> 110 us
  matrix products: 85.9 us -> 0 us
  starting transfers between devices: 0.37 us -> 34.4 us
  local copies, waits for them, and re-layouts: 26.7 us -> 1.32 us
  between operations: 13.8 us -> 0.87 us
    all_gather x3 -> x0, waiting for transfers between devices: 116 us -> none  [the longest x1 75.9 us: shards(): lax.all_gather(out_grad, ('gy', 'gz'), axis=0, tiled=True)]
    reduce_scatter x1 -> x0, waiting for transfers between devices: 111 us -> none  [shards(): lax.psum_scatter(right_trans(grad_pre, w_in), ('gy', 'gz'), scatter_dimen...]
    pallas_call x0 -> x22, Pallas kernels: none -> 110 us  [the longest x3 27.3 us: w_out_grad_call(): pl.pallas_call(kernel, grid=(count,), in_specs=[whole(size, hidden) for s...]
    psum x1 -> x0, waiting for transfers between devices: 106 us -> none  [shards(): grad_act = lax.psum(grad_act, 'gx')]
    dot_general x4 -> x0, matrix products: 85.9 us -> none  [the longest x2 44.5 us: left_trans(): lax.dot_general(left, right, (((0,), (0,)), ((), ())), preferred_element_...]
    ppermute x0 -> x42, waiting for transfers between devices: none -> 38.7 us  [the longest x6 11.2 us: step(): self.left = lax.ppermute(left, RING, ring.shift(1))]
    ppermute x0 -> x42, starting transfers between devices: none -> 34.4 us  [the longest x6 10.9 us: step(): self.left = lax.ppermute(left, RING, ring.shift(1))]
    unnamed x3 -> x32, local copies, waits for them, and re-layouts: 26.7 us -> 1.32 us
  transfers between devices with their start and end apart: 5 -> 42, of which waited for: 5 -> 21; matrix products, arithmetic and copies ran while one was open for 24% -> 0% of each run, Pallas kernels for 0% -> 51%
where the time goes in v2:
time: 185 us
  Pallas kernels  110 us (59%)
  waiting for transfers between devices  38.7 us (21%)
  starting transfers between devices  34.4 us (19%)
    pallas_call x3, Pallas kernels, w_out_grad_call(): pl.pallas_call(kernel, grid=(count,), in_specs=[whole(size, hidden) for s...  27.3 us
    pallas_call x2, Pallas kernels, w_in_grad_call(): pl.pallas_call(kernel, grid=(count,), in_specs=[pl.BlockSpec((each.shape[...  22.9 us
    pallas_call x2, Pallas kernels, grad_act_call(): pl.pallas_call(kernel, grid=(steps,), in_specs=[VMEM] * (len(flat) + 1),...  17.5 us
    pallas_call x2, Pallas kernels, in_grad_call(): pl.pallas_call(kernel, grid=(width // tile,), in_specs=[whole(count, hidd...  17.3 us
    ppermute x6, waiting for transfers between devices, step(): self.left = lax.ppermute(left, RING, ring.shift(1))  11.2 us
    ppermute x6, starting transfers between devices, step(): self.left = lax.ppermute(left, RING, ring.shift(1))  10.9 us
    pallas_call x5, Pallas kernels, add_call(): pl.pallas_call(kernel, grid=(1,), in_specs=[pl.BlockSpec((rows, width), l...  9.03 us
    ppermute x2, waiting for transfers between devices, swap_sums(): got = lax.ppermute(theirs, RING, ring.swap())  7.93 us
  transfers between devices with their start and end apart: 42, of which 21 were waited for; matrix products, arithmetic and copies ran while one was open for 0% of the time, Pallas kernels for 51%

profile of v2, /device:TPU:0, one launch (start us, length us, event | category | flops | bytes accessed | tf_op | source)
XLA Modules:
  0.0 185.0 jit_solution(4032828552925579689)
XLA Ops:
  0.6 3.1 %collective-permute-start = (bf16[40,6144]{1,0:T(8,128)(2,1)}, bf16[40,6144]{1,0:T(8,128)(2,1)S(1)}, u32[]{:S(2)}, u32[]{:S(2)}) collective-permute-start(bf16[40,6144]{1,0:T(8,128)(2,1)} %refs_0_.1), channel_id=1, source_target_pairs={{0,1},{4,5},{1,2},{5,6},{2,3},{6,7},{3,11},{7,15},{11,10},{15,14},... | collective-permute-start | bytes 1474568 | tf_op jit(solution)/shard_map/ppermute | solution.py:476
  5.0 2.0 %collective-permute-start.2 = (bf16[128,1536]{1,0:T(8,128)(2,1)S(1)}, bf16[128,1536]{1,0:T(8,128)(2,1)S(1)}, u32[]{:S(2)}, u32[]{:S(2)}) collective-permute-start(bf16[128,1536]{1,0:T(8,128)(2,1)S(1)} %get-tuple-element.81), channel_id=1, source_target_pairs={{0,16},{16,0},{1,17},{17,1},{2,18},{18,2},{3,19},{19,3},{4,20},{20... | collective-permute-start | bytes 1179656 | tf_op jit(solution)/shard_map/ppermute | solution.py:488
  7.0 7.1 %hold.1 = (bf16[1536,6144]{1,0:T(8,128)(2,1)S(1)}, f32[8,128]{1,0:T(8,128)}) custom-call(bf16[1536,6144]{1,0:T(8,128)(2,1)} %weight_ref.1), custom_call_target="tpu_custom_call" | custom-call | flops 1 | bytes 1 | tf_op jit(solution)/shard_map/hold/pallas_call | solution.py:157
  14.1 2.7 %collective-permute-done.2.refs_1_ = bf16[128,1536]{1,0:T(8,128)(2,1)S(1)} collective-permute-done((bf16[128,1536]{1,0:T(8,128)(2,1)S(1)}, bf16[128,1536]{1,0:T(8,128)(2,1)S(1)}, u32[]{:S(2)}, u32[]{:S(2)}) %collective-permute-start.2) | collective-permute-done | bytes 393248 | tf_op jit(solution)/shard_map/ppermute | solution.py:488
  16.8 1.7 collective-permute-start.10
  18.6 1.6 collective-permute-start.4
  21.2 10.0 %collective-permute-done.4.refs_3_ = bf16[40,6144]{1,0:T(8,128)(2,1)S(1)} collective-permute-done((bf16[40,6144]{1,0:T(8,128)(2,1)S(1)}, bf16[40,6144]{1,0:T(8,128)(2,1)S(1)}, u32[]{:S(2)}, u32[]{:S(2)}) %collective-permute-start.4) | collective-permute-done | bytes 491552 | tf_op jit(solution)/shard_map/ppermute | solution.py:476
  32.5 1.6 collective-permute-start.11
  34.6 10.2 %grad_act.2 = (bf16[400,6144]{1,0:T(8,128)(2,1)}, f32[400,1536]{1,0:T(8,128)}, bf16[160,1536]{1,0:T(8,128)(2,1)S(1)}, bf16[240,1536]{1,0:T(8,128)(2,1)S(1)}) custom-call(bf16[40,6144]{1,0:T(8,128)(2,1)S(1)} %copy-done.9, bf16[40,6144]{1,0:T(8,128)(2,1)S(1)} %collective-permute-done.refs_1_, bf16[40,6144]{1,0:T(8,128)(2,1)S(1)} %collective-permute-done.1.refs_2_, ...), custom_call_target="tpu_custom_call" | custom-call | flops 1 | bytes 1 | tf_op jit(solution)/shard_map/grad_act/pallas_call | solution.py:301
  47.5 1.6 collective-permute-start.13
  50.1 3.4 %gelu.2 = (bf16[400,1536]{1,0:T(8,128)(2,1)}, f32[400,1536]{1,0:T(8,128)}) custom-call(bf16[320,1536]{1,0:T(8,128)(2,1)S(1)} %copy-done.8, bf16[128,1536]{1,0:T(8,128)(2,1)S(1)} %collective-permute-done.2.refs_1_, bf16[192,1536]{1,0:T(8,128)(2,1)S(1)} %collective-permute-done.10.refs_2_), custom_call_target="tpu_custom_call" | custom-call | flops 3686400000 | bytes 1 | tf_op jit(solution)/shard_map/gelu/pallas_call | solution.py:126
  53.5 2.4 %gelu.3 = (bf16[240,1536]{1,0:T(8,128)(2,1)}, f32[240,1536]{1,0:T(8,128)}) custom-call(bf16[320,1536]{1,0:T(8,128)(2,1)S(1)} %copy-done.8, bf16[128,1536]{1,0:T(8,128)(2,1)S(1)} %collective-permute-done.2.refs_1_, bf16[192,1536]{1,0:T(8,128)(2,1)S(1)} %collective-permute-done.10.refs_2_), custom_call_target="tpu_custom_call" | custom-call | flops 2211840000 | bytes 1 | tf_op jit(solution)/shard_map/gelu/pallas_call | solution.py:126
  60.0 7.2 %grad_act.3 = (bf16[240,6144]{1,0:T(8,128)(2,1)}, f32[240,1536]{1,0:T(8,128)}, bf16[240,1536]{1,0:T(8,128)(2,1)S(1)}) custom-call(bf16[40,6144]{1,0:T(8,128)(2,1)S(1)} %collective-permute-done.11.left_ref.refs_0_, bf16[40,6144]{1,0:T(8,128)(2,1)S(1)} %collective-permute-done.12.right_ref.refs_1_, bf16[40,3072]{1,0:T(8,128)(2,1)S(1)} %collective-permute-done.13.refs_2_, ...), custom_call_target="tpu_custom_call" | custom-call | flops 1 | bytes 1 | tf_op jit(solution)/shard_map/grad_act/pallas_call | solution.py:301
  67.7 9.0 %w_out_grad.3.refs_4_ = bf16[1536,6144]{1,0:T(8,128)(2,1)} custom-call(bf16[400,1536]{1,0:T(8,128)(2,1)S(1)} %copy-done, bf16[240,1536]{1,0:T(8,128)(2,1)S(1)} %copy-done.2, bf16[400,6144]{1,0:T(8,128)(2,1)} %get-tuple-element.114.refs_2_, bf16[240,6144]{1,0:T(8,128)(2,1)} %get-tuple-element.115.refs_3_), custom_call_target="tpu_custom_call" | custom-call | flops 6039797760 | bytes 6291456 | tf_op jit(solution)/shard_map/w_out_grad/pallas_call | solution.py:391
  76.7 1.7 collective-permute-start.22
  78.8 9.5 %w_out_grad.4.refs_4_ = bf16[1536,6144]{1,0:T(8,128)(2,1)} custom-call(bf16[400,1536]{1,0:T(8,128)(2,1)S(1)} %copy-done, bf16[240,1536]{1,0:T(8,128)(2,1)S(1)} %copy-done.2, bf16[400,6144]{1,0:T(8,128)(2,1)} %get-tuple-element.114.refs_2_, bf16[240,6144]{1,0:T(8,128)(2,1)} %get-tuple-element.115.refs_3_, ...), custom_call_target="tpu_custom_call", output_to_operand_aliasing={{}: (4, {})} | custom-call | flops 6039797760 | bytes 6291456 | tf_op jit(solution)/shard_map/w_out_grad/pallas_call | solution.py:391
  90.5 7.2 %in_grad.2 = (bf16[240,1536]{1,0:T(8,128)(2,1)}, f32[120,6144]{1,0:T(8,128)}, bf16[120,6144]{1,0:T(8,128)(2,1)S(1)}) custom-call(f32[240,1536]{1,0:T(8,128)S(1)} %copy-done.7, f32[240,1536]{1,0:T(8,128)S(1)} %copy-done.6, bf16[240,1536]{1,0:T(8,128)(2,1)S(1)} %collective-permute-done.24.refs_2_, bf16[6144,1536]{1,0:T(8,128)(2,1)S(1)} %bitcast.1), custom_call_target="tpu_custom_call" | custom-call | flops 1 | bytes 1 | tf_op jit(solution)/shard_map/in_grad/pallas_call | solution.py:347
  97.7 3.3 %collective-permute-done.25.refs_1_.refs_2_ = bf16[120,6144]{1,0:T(8,128)(2,1)S(1)} collective-permute-done((bf16[120,6144]{1,0:T(8,128)(2,1)S(1)}, bf16[120,6144]{1,0:T(8,128)(2,1)S(1)}, u32[]{:S(2)}, u32[]{:S(2)}) %collective-permute-start.25) | collective-permute-done | bytes 1474592 | tf_op jit(solution)/shard_map/ppermute | solution.py:576
  102.3 1.7 collective-permute-start.26
  108.0 8.8 %w_out_grad.5 = bf16[1536,6144]{1,0:T(8,128)(2,1)} custom-call(bf16[400,1536]{1,0:T(8,128)(2,1)S(1)} %copy-done, bf16[240,1536]{1,0:T(8,128)(2,1)S(1)} %copy-done.2, bf16[400,6144]{1,0:T(8,128)(2,1)} %get-tuple-element.114.refs_2_, bf16[240,6144]{1,0:T(8,128)(2,1)} %get-tuple-element.115.refs_3_, ...), custom_call_target="tpu_custom_call", output_to_operand_aliasing={{}: (4, {})} | custom-call | flops 6039797760 | bytes 6291456 | tf_op jit(solution)/shard_map/w_out_grad/pallas_call | solution.py:391
  116.8 1.6 pack.2.refs_0_
  123.3 1.9 %add.6 = (bf16[40,6144]{1,0:T(8,128)(2,1)S(1)}, bf16[40,6144]{1,0:T(8,128)(2,1)S(1)}) custom-call(f32[120,6144]{1,0:T(8,128)} %get-tuple-element.119.refs_0_.refs_1_, f32[120,6144]{1,0:T(8,128)} %get-tuple-element.119.refs_0_.refs_1_, bf16[120,6144]{1,0:T(8,128)(2,1)S(1)} %collective-permute-done.25.refs_1_.refs_2_, ...), custom_call_target="tpu_custom_call" | custom-call | flops 1 | bytes 1 | tf_op jit(solution)/shard_map/add/pallas_call | solution.py:250
  125.9 1.5 collective-permute-start.33
  128.0 1.5 collective-permute-start.35
  129.9 10.1 %in_grad.3 = (bf16[400,1536]{1,0:T(8,128)(2,1)}, f32[200,6144]{1,0:T(8,128)}, bf16[200,6144]{1,0:T(8,128)(2,1)S(1)}) custom-call(f32[400,1536]{1,0:T(8,128)S(1)} %copy-done.4, f32[400,1536]{1,0:T(8,128)S(1)} %copy-done.5, bf16[160,1536]{1,0:T(8,128)(2,1)S(1)} %collective-permute-done.21.refs_2_, bf16[240,1536]{1,0:T(8,128)(2,1)S(1)} %collective-permute-done.26.refs_3_, ...), custom_call_target="tpu_custom_call" | custom-call | flops 1 | bytes 1 | tf_op jit(solution)/shard_map/in_grad/pallas_call | solution.py:347
  140.1 4.1 %collective-permute-done.34.refs_2_ = bf16[40,3072]{1,0:T(8,128)(2,1)S(1)} collective-permute-done((bf16[40,3072]{1,0:T(8,128)(2,1)S(1)}, bf16[40,3072]{1,0:T(8,128)(2,1)S(1)}, u32[]{:S(2)}, u32[]{:S(2)}) %collective-permute-start.34) | collective-permute-done | bytes 245792 | tf_op jit(solution)/shard_map/ppermute | solution.py:470
  145.6 4.7 %collective-permute-done.36.refs_2_.refs_1_ = bf16[200,6144]{1,0:T(8,128)(2,1)S(1)} collective-permute-done((bf16[200,6144]{1,0:T(8,128)(2,1)S(1)}, bf16[200,6144]{1,0:T(8,128)(2,1)S(1)}, u32[]{:S(2)}, u32[]{:S(2)}) %collective-permute-start.36) | collective-permute-done | bytes 2457632 | tf_op jit(solution)/shard_map/ppermute | solution.py:576
  150.3 1.9 %add.7 = (bf16[40,6144]{1,0:T(8,128)(2,1)S(1)}, bf16[40,6144]{1,0:T(8,128)(2,1)S(1)}) custom-call(f32[200,6144]{1,0:T(8,128)} %get-tuple-element.135.refs_0_.refs_1_, f32[200,6144]{1,0:T(8,128)} %get-tuple-element.135.refs_0_.refs_1_, bf16[200,6144]{1,0:T(8,128)(2,1)S(1)} %collective-permute-done.36.refs_2_.refs_1_, ...), custom_call_target="tpu_custom_call" | custom-call | flops 1 | bytes 1 | tf_op jit(solution)/shard_map/add/pallas_call | solution.py:250
  155.5 11.4 %w_in_grad.2.refs_6_ = bf16[6144,1536]{1,0:T(8,128)(2,1)} custom-call(bf16[200,6144]{1,0:T(8,128)(2,1)S(1)} %copy-done.1, bf16[200,6144]{1,0:T(8,128)(2,1)S(1)} %collective-permute-done.31.refs_1_, bf16[120,6144]{1,0:T(8,128)(2,1)S(1)} %copy-done.3, bf16[120,6144]{1,0:T(8,128)(2,1)S(1)} %collective-permute-done.37.refs_3_, ...), custom_call_target="tpu_custom_call" | custom-call | flops 9059696640 | bytes 9437184 | tf_op jit(solution)/shard_map/w_in_grad/pallas_call | solution.py:430
  167.0 1.8 add.8
  170.9 11.4 %w_in_grad.3 = bf16[6144,1536]{1,0:T(8,128)(2,1)} custom-call(bf16[200,6144]{1,0:T(8,128)(2,1)S(1)} %copy-done.1, bf16[200,6144]{1,0:T(8,128)(2,1)S(1)} %collective-permute-done.31.refs_1_, bf16[120,6144]{1,0:T(8,128)(2,1)S(1)} %copy-done.3, bf16[120,6144]{1,0:T(8,128)(2,1)S(1)} %collective-permute-done.37.refs_3_, ...), custom_call_target="tpu_custom_call", output_to_operand_aliasing={{}: (6, {})} | custom-call | flops 9059696640 | bytes 9437184 | tf_op jit(solution)/shard_map/w_in_grad/pallas_call | solution.py:430
  182.8 2.2 %add.9 = bf16[40,6144]{1,0:T(8,128)(2,1)} custom-call(f32[200,6144]{1,0:T(8,128)} %get-tuple-element.135.refs_0_.refs_1_, bf16[200,6144]{1,0:T(8,128)(2,1)S(1)} %collective-permute-done.36.refs_2_.refs_1_, bf16[40,6144]{1,0:T(8,128)(2,1)S(1)} %collective-permute-done.40.refs_2_, bf16[40,6144]{1,0:T(8,128)(2,1)S(1)} %collective-permute-done.41.refs_3_), custom_call_target="tpu_custom_call" | custom-call | flops 1 | bytes 1 | tf_op jit(solution)/shard_map/add/pallas_call | solution.py:250
  (107 shorter events, 34.1 us)
Async XLA Ops:
  0.6 17.9 %collective-permute-start = (bf16[40,6144]{1,0:T(8,128)(2,1)}, bf16[40,6144]{1,0:T(8,128)(2,1)S(1)}, u32[]{:S(2)}, u32[]{:S(2)}) collective-permute-start(bf16[40,6144]{1,0:T(8,128)(2,1)} %refs_0_.1), channel_id=1, source_target_pairs={{0,1},{4,5},{1,2},{5,6},{2,3},{6,7},{3,11},{7,15},{11,10},{15,14},... | collective-permute-start | bytes 1474568 | tf_op jit(solution)/shard_map/ppermute | solution.py:476
  3.7 14.9 %collective-permute-start.1 = (bf16[40,6144]{1,0:T(8,128)(2,1)}, bf16[40,6144]{1,0:T(8,128)(2,1)S(1)}, u32[]{:S(2)}, u32[]{:S(2)}) collective-permute-start(bf16[40,6144]{1,0:T(8,128)(2,1)} %refs_0_.1), channel_id=1, source_target_pairs={{0,8},{4,12},{1,0},{5,4},{2,1},{6,5},{3,2},{7,6},{11,3},{15,7},{10... | collective-permute-start | bytes 1474568 | tf_op jit(solution)/shard_map/ppermute | solution.py:477
  3.7 14.9 %collective-permute-start.3 = (bf16[40,6144]{1,0:T(8,128)(2,1)}, bf16[40,6144]{1,0:T(8,128)(2,1)S(1)}, u32[]{:S(2)}, u32[]{:S(2)}) collective-permute-start(bf16[40,6144]{1,0:T(8,128)(2,1)} %refs_0_.1), channel_id=1, source_target_pairs={{0,4},{4,0},{1,5},{5,1},{2,6},{6,2},{3,7},{7,3},{11,15},{15,11},{1... | collective-permute-start | bytes 1474568 | tf_op jit(solution)/shard_map/ppermute | solution.py:482
  5.0 11.8 %collective-permute-start.2 = (bf16[128,1536]{1,0:T(8,128)(2,1)S(1)}, bf16[128,1536]{1,0:T(8,128)(2,1)S(1)}, u32[]{:S(2)}, u32[]{:S(2)}) collective-permute-start(bf16[128,1536]{1,0:T(8,128)(2,1)S(1)} %get-tuple-element.81), channel_id=1, source_target_pairs={{0,16},{16,0},{1,17},{17,1},{2,18},{18,2},{3,19},{19,3},{4,20},{20... | collective-permute-start | bytes 1179656 | tf_op jit(solution)/shard_map/ppermute | solution.py:488
  16.8 15.7 %collective-permute-start.10 = (bf16[192,1536]{1,0:T(8,128)(2,1)S(1)}, bf16[192,1536]{1,0:T(8,128)(2,1)S(1)}, u32[]{:S(2)}, u32[]{:S(2)}) collective-permute-start(bf16[192,1536]{1,0:T(8,128)(2,1)S(1)} %get-tuple-element.91), channel_id=1, source_target_pairs={{0,16},{16,0},{1,17},{17,1},{2,18},{18,2},{3,19},{19,3},{4,20},{20... | collective-permute-start | bytes 1769480 | tf_op jit(solution)/shard_map/ppermute | solution.py:488
  18.6 12.6 %collective-permute-start.4 = (bf16[40,6144]{1,0:T(8,128)(2,1)S(1)}, bf16[40,6144]{1,0:T(8,128)(2,1)S(1)}, u32[]{:S(2)}, u32[]{:S(2)}) collective-permute-start(bf16[40,6144]{1,0:T(8,128)(2,1)S(1)} %collective-permute-done.refs_1_), channel_id=1, source_target_pairs={{0,1},{4,5},{1,2},{5,6},{2,3},{6,7},{3,11},{7,15},{11,10},{15,14},... | collective-permute-start | bytes 1474568 | tf_op jit(solution)/shard_map/ppermute | solution.py:476
  20.2 12.3 %collective-permute-start.5 = (bf16[40,6144]{1,0:T(8,128)(2,1)S(1)}, bf16[40,6144]{1,0:T(8,128)(2,1)S(1)}, u32[]{:S(2)}, u32[]{:S(2)}) collective-permute-start(bf16[40,6144]{1,0:T(8,128)(2,1)S(1)} %collective-permute-done.1.refs_2_), channel_id=1, source_target_pairs={{0,8},{4,12},{1,0},{5,4},{2,1},{6,5},{3,2},{7,6},{11,3},{15,7},{10... | collective-permute-start | bytes 1474568 | tf_op jit(solution)/shard_map/ppermute | solution.py:477
  20.6 11.8 %collective-permute-start.6 = (bf16[40,6144]{1,0:T(8,128)(2,1)S(1)}, bf16[40,6144]{1,0:T(8,128)(2,1)S(1)}, u32[]{:S(2)}, u32[]{:S(2)}) collective-permute-start(bf16[40,6144]{1,0:T(8,128)(2,1)S(1)} %collective-permute-done.refs_1_), channel_id=1, source_target_pairs={{0,4},{4,0},{1,5},{5,1},{2,6},{6,2},{3,7},{7,3},{11,15},{15,11},{1... | collective-permute-start | bytes 1474568 | tf_op jit(solution)/shard_map/ppermute | solution.py:482
  20.6 11.8 %collective-permute-start.7 = (bf16[40,6144]{1,0:T(8,128)(2,1)S(1)}, bf16[40,6144]{1,0:T(8,128)(2,1)S(1)}, u32[]{:S(2)}, u32[]{:S(2)}) collective-permute-start(bf16[40,6144]{1,0:T(8,128)(2,1)S(1)} %collective-permute-done.1.refs_2_), channel_id=1, source_target_pairs={{0,4},{4,0},{1,5},{5,1},{2,6},{6,2},{3,7},{7,3},{11,15},{15,11},{1... | collective-permute-start | bytes 1474568 | tf_op jit(solution)/shard_map/ppermute | solution.py:482
  32.5 13.7 %collective-permute-start.11 = (bf16[40,6144]{1,0:T(8,128)(2,1)S(1)}, bf16[40,6144]{1,0:T(8,128)(2,1)S(1)}, u32[]{:S(2)}, u32[]{:S(2)}) collective-permute-start(bf16[40,6144]{1,0:T(8,128)(2,1)S(1)} %collective-permute-done.4.refs_3_), channel_id=1, source_target_pairs={{0,1},{4,5},{1,2},{5,6},{2,3},{6,7},{3,11},{7,15},{11,10},{15,14},... | collective-permute-start | bytes 1474568 | tf_op jit(solution)/shard_map/ppermute | solution.py:476
  34.1 13.3 %collective-permute-start.12 = (bf16[40,6144]{1,0:T(8,128)(2,1)S(1)}, bf16[40,6144]{1,0:T(8,128)(2,1)S(1)}, u32[]{:S(2)}, u32[]{:S(2)}) collective-permute-start(bf16[40,6144]{1,0:T(8,128)(2,1)S(1)} %collective-permute-done.5.refs_4_), channel_id=1, source_target_pairs={{0,8},{4,12},{1,0},{5,4},{2,1},{6,5},{3,2},{7,6},{11,3},{15,7},{10... | collective-permute-start | bytes 1474568 | tf_op jit(solution)/shard_map/ppermute | solution.py:477
  44.8 15.2 %collective-permute-start.21 = (bf16[160,1536]{1,0:T(8,128)(2,1)S(1)}, bf16[160,1536]{1,0:T(8,128)(2,1)S(1)}, u32[]{:S(2)}, u32[]{:S(2)}) collective-permute-start(bf16[160,1536]{1,0:T(8,128)(2,1)S(1)} %get-tuple-element.94), channel_id=1, source_target_pairs={{0,16},{16,0},{1,17},{17,1},{2,18},{18,2},{3,19},{19,3},{4,20},{20... | collective-permute-start | bytes 1474568 | tf_op jit(solution)/shard_map/ppermute | solution.py:488
  47.5 8.4 %collective-permute-start.13 = (bf16[40,3072]{1,0:T(8,128)(2,1)S(1)}, bf16[40,3072]{1,0:T(8,128)(2,1)S(1)}, u32[]{:S(2)}, u32[]{:S(2)}) collective-permute-start(bf16[40,3072]{1,0:T(8,128)(2,1)S(1)} %get-tuple-element.98), channel_id=1, source_target_pairs={{0,1},{4,5},{1,2},{5,6},{2,3},{6,7},{3,11},{7,15},{11,10},{15,14},... | collective-permute-start | bytes 737288 | tf_op jit(solution)/shard_map/ppermute | solution.py:470
  49.6 7.0 %collective-permute-start.15 = (bf16[40,6144]{1,0:T(8,128)(2,1)S(1)}, bf16[40,6144]{1,0:T(8,128)(2,1)S(1)}, u32[]{:S(2)}, u32[]{:S(2)}) collective-permute-start(bf16[40,6144]{1,0:T(8,128)(2,1)S(1)} %collective-permute-done.11.left_ref.refs_0_), channel_id=1, source_target_pairs={{0,4},{4,0},{1,5},{5,1},{2,6},{6,2},{3,7},{7,3},{11,15},{15,11},{1... | collective-permute-start | bytes 1474568 | tf_op jit(solution)/shard_map/ppermute | solution.py:482
  58.0 18.7 %collective-permute-start.19 = (bf16[40,6144]{1,0:T(8,128)(2,1)S(1)}, bf16[40,6144]{1,0:T(8,128)(2,1)S(1)}, u32[]{:S(2)}, u32[]{:S(2)}) collective-permute-start(bf16[40,6144]{1,0:T(8,128)(2,1)S(1)} %copy-done.10), channel_id=1, source_target_pairs={{0,1},{4,5},{1,2},{5,6},{2,3},{6,7},{3,11},{7,15},{11,10},{15,14},... | collective-permute-start | bytes 1474568 | tf_op jit(solution)/shard_map/ppermute | solution.py:476
  59.5 17.2 %collective-permute-start.20 = (bf16[40,6144]{1,0:T(8,128)(2,1)S(1)}, bf16[40,6144]{1,0:T(8,128)(2,1)S(1)}, u32[]{:S(2)}, u32[]{:S(2)}) collective-permute-start(bf16[40,6144]{1,0:T(8,128)(2,1)S(1)} %copy-done.10), channel_id=1, source_target_pairs={{0,8},{4,12},{1,0},{5,4},{2,1},{6,5},{3,2},{7,6},{11,3},{15,7},{10... | collective-permute-start | bytes 1474568 | tf_op jit(solution)/shard_map/ppermute | solution.py:477
  67.3 23.2 %collective-permute-start.24 = (bf16[240,1536]{1,0:T(8,128)(2,1)S(1)}, bf16[240,1536]{1,0:T(8,128)(2,1)S(1)}, u32[]{:S(2)}, u32[]{:S(2)}) collective-permute-start(bf16[240,1536]{1,0:T(8,128)(2,1)S(1)} %get-tuple-element.118), channel_id=1, source_target_pairs={{0,16},{16,0},{1,17},{17,1},{2,18},{18,2},{3,19},{19,3},{4,20},{20... | collective-permute-start | bytes 2211848 | tf_op jit(solution)/shard_map/ppermute | solution.py:488
  76.7 12.5 %collective-permute-start.22 = (bf16[40,6144]{1,0:T(8,128)(2,1)S(1)}, bf16[40,6144]{1,0:T(8,128)(2,1)S(1)}, u32[]{:S(2)}, u32[]{:S(2)}) collective-permute-start(bf16[40,6144]{1,0:T(8,128)(2,1)S(1)} %collective-permute-done.19.refs_1_), channel_id=1, source_target_pairs={{0,1},{4,5},{1,2},{5,6},{2,3},{6,7},{3,11},{7,15},{11,10},{15,14},... | collective-permute-start | bytes 1474568 | tf_op jit(solution)/shard_map/ppermute | solution.py:476
  78.4 12.1 %collective-permute-start.23 = (bf16[40,6144]{1,0:T(8,128)(2,1)S(1)}, bf16[40,6144]{1,0:T(8,128)(2,1)S(1)}, u32[]{:S(2)}, u32[]{:S(2)}) collective-permute-start(bf16[40,6144]{1,0:T(8,128)(2,1)S(1)} %collective-permute-done.20.refs_2_), channel_id=1, source_target_pairs={{0,8},{4,12},{1,0},{5,4},{2,1},{6,5},{3,2},{7,6},{11,3},{15,7},{10... | collective-permute-start | bytes 1474568 | tf_op jit(solution)/shard_map/ppermute | solution.py:477
  102.3 18.6 %collective-permute-start.26 = (bf16[240,1536]{1,0:T(8,128)(2,1)S(1)}, bf16[240,1536]{1,0:T(8,128)(2,1)S(1)}, u32[]{:S(2)}, u32[]{:S(2)}) collective-permute-start(bf16[240,1536]{1,0:T(8,128)(2,1)S(1)} %get-tuple-element.124), channel_id=1, source_target_pairs={{0,16},{16,0},{1,17},{17,1},{2,18},{18,2},{3,19},{19,3},{4,20},{20... | collective-permute-start | bytes 2211848 | tf_op jit(solution)/shard_map/ppermute | solution.py:488
  104.0 14.5 %collective-permute-start.27 = (bf16[40,6144]{1,0:T(8,128)(2,1)S(1)}, bf16[40,6144]{1,0:T(8,128)(2,1)S(1)}, u32[]{:S(2)}, u32[]{:S(2)}) collective-permute-start(bf16[40,6144]{1,0:T(8,128)(2,1)S(1)} %collective-permute-done.22.refs_3_), channel_id=1, source_target_pairs={{0,1},{4,5},{1,2},{5,6},{2,3},{6,7},{3,11},{7,15},{11,10},{15,14},... | collective-permute-start | bytes 1474568 | tf_op jit(solution)/shard_map/ppermute | solution.py:476
  105.3 14.2 %collective-permute-start.28 = (bf16[40,6144]{1,0:T(8,128)(2,1)S(1)}, bf16[40,6144]{1,0:T(8,128)(2,1)S(1)}, u32[]{:S(2)}, u32[]{:S(2)}) collective-permute-start(bf16[40,6144]{1,0:T(8,128)(2,1)S(1)} %collective-permute-done.23.refs_4_), channel_id=1, source_target_pairs={{0,8},{4,12},{1,0},{5,4},{2,1},{6,5},{3,2},{7,6},{11,3},{15,7},{10... | collective-permute-start | bytes 1474568 | tf_op jit(solution)/shard_map/ppermute | solution.py:477
  106.0 16.2 %collective-permute-start.29 = (bf16[40,3072]{1,0:T(8,128)(2,1)S(1)}, bf16[40,3072]{1,0:T(8,128)(2,1)S(1)}, u32[]{:S(2)}, u32[]{:S(2)}) collective-permute-start(bf16[40,3072]{1,0:T(8,128)(2,1)S(1)} %get-tuple-element.121), channel_id=1, source_target_pairs={{0,1},{4,5},{1,2},{5,6},{2,3},{6,7},{3,11},{7,15},{11,10},{15,14},... | collective-permute-start | bytes 737288 | tf_op jit(solution)/shard_map/ppermute | solution.py:604
  107.4 15.9 %collective-permute-start.30 = (bf16[40,3072]{1,0:T(8,128)(2,1)S(1)}, bf16[40,3072]{1,0:T(8,128)(2,1)S(1)}, u32[]{:S(2)}, u32[]{:S(2)}) collective-permute-start(bf16[40,3072]{1,0:T(8,128)(2,1)S(1)} %get-tuple-element.122), channel_id=1, source_target_pairs={{0,8},{4,12},{1,0},{5,4},{2,1},{6,5},{3,2},{7,6},{11,3},{15,7},{10... | collective-permute-start | bytes 737288 | tf_op jit(solution)/shard_map/ppermute | solution.py:605
  125.3 20.3 %collective-permute-start.32 = (bf16[40,6144]{1,0:T(8,128)(2,1)S(1)}, bf16[40,6144]{1,0:T(8,128)(2,1)S(1)}, u32[]{:S(2)}, u32[]{:S(2)}) collective-permute-start(bf16[40,6144]{1,0:T(8,128)(2,1)S(1)} %get-tuple-element.131), channel_id=1, source_target_pairs={{0,1},{4,5},{1,2},{5,6},{2,3},{6,7},{3,11},{7,15},{11,10},{15,14},... | collective-permute-start | bytes 1474568 | tf_op jit(solution)/shard_map/ppermute | solution.py:604
  125.9 19.8 %collective-permute-start.33 = (bf16[40,6144]{1,0:T(8,128)(2,1)S(1)}, bf16[40,6144]{1,0:T(8,128)(2,1)S(1)}, u32[]{:S(2)}, u32[]{:S(2)}) collective-permute-start(bf16[40,6144]{1,0:T(8,128)(2,1)S(1)} %get-tuple-element.132), channel_id=1, source_target_pairs={{0,8},{4,12},{1,0},{5,4},{2,1},{6,5},{3,2},{7,6},{11,3},{15,7},{10... | collective-permute-start | bytes 1474568 | tf_op jit(solution)/shard_map/ppermute | solution.py:605
  127.4 16.8 %collective-permute-start.34 = (bf16[40,3072]{1,0:T(8,128)(2,1)S(1)}, bf16[40,3072]{1,0:T(8,128)(2,1)S(1)}, u32[]{:S(2)}, u32[]{:S(2)}) collective-permute-start(bf16[40,3072]{1,0:T(8,128)(2,1)S(1)} %get-tuple-element.139), channel_id=1, source_target_pairs={{0,1},{4,5},{1,2},{5,6},{2,3},{6,7},{3,11},{7,15},{11,10},{15,14},... | collective-permute-start | bytes 737288 | tf_op jit(solution)/shard_map/ppermute | solution.py:470
  128.0 16.4 %collective-permute-start.35 = (bf16[40,3072]{1,0:T(8,128)(2,1)S(1)}, bf16[40,3072]{1,0:T(8,128)(2,1)S(1)}, u32[]{:S(2)}, u32[]{:S(2)}) collective-permute-start(bf16[40,3072]{1,0:T(8,128)(2,1)S(1)} %get-tuple-element.140), channel_id=1, source_target_pairs={{0,8},{4,12},{1,0},{5,4},{2,1},{6,5},{3,2},{7,6},{11,3},{15,7},{10... | collective-permute-start | bytes 737288 | tf_op jit(solution)/shard_map/ppermute | solution.py:471
  152.4 14.6 %collective-permute-start.38 = (bf16[40,6144]{1,0:T(8,128)(2,1)S(1)}, bf16[40,6144]{1,0:T(8,128)(2,1)S(1)}, u32[]{:S(2)}, u32[]{:S(2)}) collective-permute-start(bf16[40,6144]{1,0:T(8,128)(2,1)S(1)} %get-tuple-element.148), channel_id=1, source_target_pairs={{0,1},{4,5},{1,2},{5,6},{2,3},{6,7},{3,11},{7,15},{11,10},{15,14},... | collective-permute-start | bytes 1474568 | tf_op jit(solution)/shard_map/ppermute | solution.py:604
  153.4 13.6 %collective-permute-start.39 = (bf16[40,6144]{1,0:T(8,128)(2,1)S(1)}, bf16[40,6144]{1,0:T(8,128)(2,1)S(1)}, u32[]{:S(2)}, u32[]{:S(2)}) collective-permute-start(bf16[40,6144]{1,0:T(8,128)(2,1)S(1)} %get-tuple-element.149), channel_id=1, source_target_pairs={{0,8},{4,12},{1,0},{5,4},{2,1},{6,5},{3,2},{7,6},{11,3},{15,7},{10... | collective-permute-start | bytes 1474568 | tf_op jit(solution)/shard_map/ppermute | solution.py:605
  168.8 13.5 %collective-permute-start.40 = (bf16[40,6144]{1,0:T(8,128)(2,1)S(1)}, bf16[40,6144]{1,0:T(8,128)(2,1)S(1)}, u32[]{:S(2)}, u32[]{:S(2)}) collective-permute-start(bf16[40,6144]{1,0:T(8,128)(2,1)S(1)} %get-tuple-element.154), channel_id=1, source_target_pairs={{0,1},{4,5},{1,2},{5,6},{2,3},{6,7},{3,11},{7,15},{11,10},{15,14},... | collective-permute-start | bytes 1474568 | tf_op jit(solution)/shard_map/ppermute | solution.py:604
  169.8 13.0 %collective-permute-start.41 = (bf16[40,6144]{1,0:T(8,128)(2,1)S(1)}, bf16[40,6144]{1,0:T(8,128)(2,1)S(1)}, u32[]{:S(2)}, u32[]{:S(2)}) collective-permute-start(bf16[40,6144]{1,0:T(8,128)(2,1)S(1)} %get-tuple-element.155), channel_id=1, source_target_pairs={{0,8},{4,12},{1,0},{5,4},{2,1},{6,5},{3,2},{7,6},{11,3},{15,7},{10... | collective-permute-start | bytes 1474568 | tf_op jit(solution)/shard_map/ppermute | solution.py:605
  (26 other events, 226.4 us)

commit v3 on v2

--- a/solution.py
+++ b/solution.py
@@ -189,7 +189,7 @@
 
 def parts_call(values):
     rows, width = values.shape
-    cut = rows * 2 // 5 // 16 * 16
+    cut = rows * 7 // 20 // 16 * 16
 
     def kernel(ref, upper_ref, lower_ref):
         upper_ref[...] = ref[:cut, :]
@@ -206,7 +206,7 @@
     )(values)
 
 
-def pack_call(blocks, rows, width):
+def pack_call(blocks, rows, width, space):
     flat = [piece for block in blocks for piece in block]
 
     def kernel(*refs):
@@ -222,46 +222,42 @@
         kernel,
         grid=(1,),
         in_specs=[VMEM] * len(flat),
-        out_specs=whole(len(blocks) * rows, width),
-        out_shape=in_hbm(len(blocks) * rows, width),
+        out_specs=whole(len(blocks) * rows, width) if space is pltpu.HBM else VMEM,
+        out_shape=space((len(blocks) * rows, width), jnp.bfloat16),
         cost_estimate=cost(1, 1),
         compiler_params=pltpu.CompilerParams(vmem_limit_bytes=8 * MIB),
         name="pack",
     )(*flat)
 
 
-def add_call(mine, theirs, places, arrived, rows, outs):
-    width = mine.shape[1]
-    flat = [value for block in arrived for value, _ in block]
+def add_call(parts, arrived, rows, outs):
+    width = parts[0][0].shape[1]
+    flat = [each for part in parts for each in part[:2]]
+    flat += [value for block in arrived for value, _ in block]
 
     def kernel(*refs):
-        wide, theirs_ref = refs[: len(places)], refs[len(places)]
-        given = iter(refs[len(places) + 1 : len(refs) - len(outs) - len(places)])
-        made = refs[len(refs) - len(places) :]
-        for i, (place, block) in enumerate(zip(places, arrived)):
-            at = slice(place * rows, (place + 1) * rows)
-            made[i][...] = wide[i][...] + theirs_ref[at, :].astype(jnp.float32)
+        given = iter(refs[2 * len(parts) :])
+        made = refs[len(refs) - len(parts) :]
+        for i, ((_, _, one, other), block) in enumerate(zip(parts, arrived)):
+            mine, theirs = refs[2 * i], refs[2 * i + 1]
+            low = theirs[other * rows : (other + 1) * rows, :]
+            made[i][...] = mine[one * rows : (one + 1) * rows, :] + low.astype(jnp.float32)
             for value, first in block:
                 columns = slice(first, first + value.shape[1])
                 made[i][:, columns] += next(given)[...].astype(jnp.float32)
-        for ref, (i, first, last) in zip(refs[-len(outs) - len(places) :], outs):
+        for ref, (i, first, last) in zip(refs[len(flat) :], outs):
             ref[...] = made[i][:, first:last].astype(ref.dtype)
 
     return pl.pallas_call(
         kernel,
-        grid=(1,),
-        in_specs=[
-            pl.BlockSpec((rows, width), lambda i, p=p: (p, 0), pipeline_mode=pl.Buffered(1))
-            for p in places
-        ]
-        + [VMEM] * (1 + len(flat)),
+        in_specs=[VMEM] * len(flat),
         out_specs=[VMEM] * len(outs),
         out_shape=[shape(rows, last - first) for _, first, last in outs],
-        scratch_shapes=[pltpu.VMEM((rows, width), jnp.float32)] * len(places),
+        scratch_shapes=[pltpu.VMEM((rows, width), jnp.float32)] * len(parts),
         cost_estimate=cost(1, 1),
         compiler_params=pltpu.CompilerParams(vmem_limit_bytes=8 * MIB),
         name="add",
-    )(*constrained([mine] * len(places)), theirs, *flat)
+    )(*flat)
 
 
 def grad_act_call(blocks, weights, rows, cuts):
@@ -308,7 +304,7 @@
         ]
         + [pl.BlockSpec((end - begin, tile), lambda i: (0, i)) for begin, end in spans],
         out_shape=[in_hbm(count, width), in_hbm(count, hidden, jnp.float32)]
-        + [shape(end - begin, hidden) for begin, end in spans],
+        + [(in_hbm if begin > 0 else shape)(end - begin, hidden) for begin, end in spans],
         scratch_shapes=[pltpu.VMEM((count, width), jnp.bfloat16), pltpu.SemaphoreType.DMA],
         cost_estimate=cost(1, 1),
         compiler_params=pltpu.CompilerParams(vmem_limit_bytes=10 * MIB),
@@ -316,21 +312,22 @@
     )(*flat, weights)
 
 
-def in_grad_call(part, others, slope, weights):
+def in_grad_call(part, others, slope, weights, cuts):
     flat = [piece for pieces in zip(*others) for piece in pieces]
     width, hidden = weights.shape
     count = part.shape[0]
     half = count // 2
     tile = tile_of(width, 1024)
+    spans = list(zip([0] + cuts, cuts + [half]))
 
     def kernel(*refs):
         part_ref, slope_ref = refs[:2]
-        weight_ref, pre_ref, mine_ref, theirs_ref = refs[-4:]
+        weight_ref, pre_ref, mine_ref, *theirs_refs = refs[2 + len(flat) :]
         i = pl.program_id(0)
 
         @pl.when(i == 0)
         def _():
-            given, at = iter(refs[2:-4]), 0
+            given, at = iter(refs[2:]), 0
             for pieces in zip(*others):
                 here = slice(at, at + pieces[0].shape[0])
                 total = part_ref[here, :]
@@ -341,8 +338,9 @@
 
         at = pl.ds(pl.multiple_of(i * tile, tile), tile)
         got = right_trans(pre_ref[...], weight_ref[at, :])
-        mine_ref[...] = got[:half]
-        theirs_ref[...] = got[half:].astype(theirs_ref.dtype)
+        mine_ref[:, at] = got[:half]
+        for ref, (begin, end) in zip(theirs_refs, spans):
+            ref[...] = got[half + begin : half + end].astype(ref.dtype)
 
     return pl.pallas_call(
         kernel,
@@ -350,14 +348,14 @@
         in_specs=[whole(count, hidden)] * 2 + [whole(*each.shape) for each in flat] + [VMEM],
         out_specs=[
             whole(count, hidden),
-            pl.BlockSpec((half, tile), lambda i: (0, i)),
-            pl.BlockSpec((half, tile), lambda i: (0, i)),
-        ],
+            VMEM,
+        ]
+        + [pl.BlockSpec((end - begin, tile), lambda i: (0, i)) for begin, end in spans],
         out_shape=[
             in_hbm(count, hidden),
-            in_hbm(half, width, jnp.float32),
-            shape(half, width),
-        ],
+            pltpu.VMEM((half, width), jnp.float32),
+        ]
+        + [shape(end - begin, width) for begin, end in spans],
         cost_estimate=cost(1, 1),
         compiler_params=pltpu.CompilerParams(vmem_limit_bytes=14 * MIB),
         name="in_grad",
@@ -375,30 +373,34 @@
 def w_out_grad_call(acts, chunks, factor, tile, first, count, earlier):
     sizes = [chunk.shape[0] for chunk in chunks]
     many, total = len(sizes), sum(sizes)
-    hidden, width = acts[0].shape[1], chunks[0].shape[1]
+    hidden, width = earlier[0].shape if earlier else (acts[0].shape[1], chunks[0].shape[1])
 
     def kernel(*refs):
-        given, tokens, (out_ref, turned) = refs[:many], refs[many : 2 * many], refs[-2:]
-
-        @pl.when(pl.program_id(0) == 0)
-        def _():
-            turned[...] = jnp.concatenate([ref[...] for ref in given], axis=0).T
+        given, tokens = refs[: len(acts)], refs[len(acts) : len(acts) + many]
+        if earlier:
+            turned, out_ref = given[0], refs[-1]
+        else:
+            out_ref, turned = refs[-2:]
+
+            @pl.when(pl.program_id(0) == 0)
+            def _():
+                turned[...] = jnp.concatenate([ref[...] for ref in given], axis=0).T
 
         joined = jnp.concatenate([ref[...] for ref in tokens], axis=0)
         got = jnp.dot(turned[...], joined, preferred_element_type=jnp.float32)
         out_ref[...] = (got * factor).astype(out_ref.dtype)
 
+    out_spec = pl.BlockSpec((hidden, tile), lambda i: (0, first + i))
     return pl.pallas_call(
         kernel,
         grid=(count,),
-        in_specs=[whole(size, hidden) for size in sizes]
+        in_specs=[whole(*act.shape) for act in acts]
         + [pl.BlockSpec((size, tile), lambda i: (0, first + i)) for size in sizes]
         + [pl.BlockSpec(memory_space=pl.ANY)] * len(earlier),
-        out_specs=pl.BlockSpec((hidden, tile), lambda i: (0, first + i)),
-        out_shape=shape(hidden, width),
-        input_output_aliases={2 * many: 0} if earlier else {},
-        scratch_shapes=[pltpu.VMEM((hidden, total), jnp.bfloat16)],
-        cost_estimate=cost(3 * total * tile * count * hidden, 2 * hidden * tile * count),
+        out_specs=[out_spec] + ([] if earlier else [whole(hidden, total)]),
+        out_shape=[shape(hidden, width)] + ([] if earlier else [shape(hidden, total)]),
+        input_output_aliases={len(acts) + many: 0} if earlier else {},
+        cost_estimate=cost(16 * total * tile // 4 * count * hidden, 2 * hidden * tile * count),
         compiler_params=pltpu.CompilerParams(vmem_limit_bytes=26 * MIB),
         name="w_out_grad",
     )(*acts, *chunks, *earlier)
@@ -523,12 +525,14 @@
                 ahead = here if number == 0 else slopes if grads.done == last else sent
                 swapped[offset] = other_core(ring, after(grads.held[offset], ahead))
         blocks = [grads.held[o] for o in offsets] + [swapped[o] for o in offsets]
-        cuts = [2 * len(blocks) * rows // 5 // 16 * 16] if number == 0 else []
+        cuts = [len(blocks) * rows * part // 25 // 16 * 16 for part in (10, 17)] if number == 0 else []
+        if number > 0:
+            blocks[0] = after(blocks[0], early)
         chunk, partial, *sent = grad_act_call(blocks, w_out, rows, cuts)
         chunks.append(chunk)
         partials.append(partial)
         if number == 0:
-            early, late = exchange(sent[0], "gx"), sent[1]
+            early, late = exchange(sent[0], "gx"), sent[1:]
     received = [[each] for each in exchange(sent[0], "gx")]
 
     tokens = Gather(ring, after(inputs, grads.held[ring.half], swapped), True)
@@ -540,22 +544,28 @@
             tokens.step(*others)
         return arrived
 
-    tile, out_cuts = pieces_of(width, 3)
     tile, in_cuts = pieces_of(width, 2)
-    w_out_grad, w_in_grad = [], []
+    out_cuts = pieces_of(width, 6)[1]
+    if len(out_cuts) == 6:
+        out_cuts = [(0, 1), (1, 3), (4, 2)]
+    w_out_grad, w_in_grad, turned = [], [], None
 
     def w_out_piece(*others):
-        nonlocal w_out_grad
+        nonlocal w_out_grad, turned
         first, count = out_cuts.pop(0)
-        given = [after(acts[0], *others)] + list(acts[1:])
-        w_out_grad = [w_out_grad_call(given, chunks, factor, tile, first, count, w_out_grad)]
+        given = list(acts) if turned is None else [turned]
+        given[0] = after(given[0], *others)
+        got = w_out_grad_call(given, chunks, factor, tile, first, count, w_out_grad)
+        w_out_grad = got[:1]
+        if turned is None:
+            turned = got[1]
         return w_out_grad
 
     def w_in_piece(*others):
         nonlocal w_in_grad
         first, count = in_cuts.pop(0)
         flat = [each for number in range(len(order)) for each in packed[number]]
-        given = constrained([after(pres[0], *others)] + pres[1:])
+        given = [after(pres[0], *others)] + pres[1:]
         w_in_grad = [w_in_grad_call(flat, given, factor, tile, first, count, w_in_grad)]
         return w_in_grad
 
@@ -569,28 +579,34 @@
 
     def in_grad_chunk(i, received, *others):
         partial = after(partials[i], *others)
-        pres[i], mine, theirs = in_grad_call(partial, received, slopes[i], w_in)
+        cuts = [(len(order[i]) - 2) * rows] if i == 0 and len(order[i]) > 2 else []
+        pres[i], mine, *theirs = in_grad_call(partial, received, slopes[i], w_in, cuts)
         return mine, theirs
 
     def swap_sums(i, mine, theirs):
-        got = lax.ppermute(theirs, RING, ring.swap())
-        for j, offset in enumerate(order[i]):
-            sums[offset] = (mine, got, j)
+        place = len(order[i])
+        for piece in reversed(theirs):
+            got = lax.ppermute(piece, RING, ring.swap())
+            for other in reversed(range(piece.shape[0] // rows)):
+                place -= 1
+                sums[order[i][place]] = (mine, got, place, other)
 
     def add(offsets, arrived, outs, *others):
-        mine, theirs, _ = sums[offsets[0]]
-        places = [sums[offset][2] for offset in offsets]
-        return add_call(mine, after(theirs, *others), places, arrived, rows, outs)
+        parts = [sums[offset] for offset in offsets]
+        parts[0] = (parts[0][0], after(parts[0][1], *others)) + parts[0][2:]
+        return add_call(parts, arrived, rows, outs)
 
     packed = {}
 
     def pack(number, *others):
         blocks = after([tokens.held[o] for o in order[number]], *others)
-        packed[number] = [pack_call(blocks, rows, width)]
+        space = pltpu.HBM if number == 0 else pltpu.VMEM
+        packed[number] = [pack_call(blocks, rows, width, space)]
         return packed[number]
 
-    mine, theirs = in_grad_chunk(1, received, w_out_grad, advance())
-    swap_sums(1, mine, theirs)
+    mine, theirs = in_grad_chunk(1, received, w_out_grad, advance(*w_out_grad))
+    middle = exchange(after(late[0], received), "gx")
+    swap_sums(1, mine, after(theirs, list(tokens.held.values()), middle))
     right, left, beside = [], [], []
     for step in range(ring.half, 0, -1):
         if step == ring.half and ring.even:
@@ -608,17 +624,17 @@
             if len(one) == 1:
                 one += other_core(ring, after(one, *going))
         if step == ring.half:
-            late = exchange(after(late, *going), "gx")
+            late = exchange(after(late[1], middle), "gx")
             if out_cuts:
                 beside = w_out_piece(*going)
+            tokens.step(*going)
             beside = [beside, late, list(tokens.held.values())]
-            tokens.step(*going)
             if order[0][-1] in tokens.held:
                 beside = [beside, pack(0, *going)]
         if 0 not in sums and step <= ring.half - (1 if beside or step < ring.half else 0):
             while tokens.done < ring.half:
                 tokens.step(*going)
-            mine, theirs = in_grad_chunk(0, list(zip(early, late)), *going, list(packed.values()))
+            mine, theirs = in_grad_chunk(0, list(zip(early, middle, late)), *going, list(packed.values()))
             last = pack(1, *going, pres[0])
             swap_sums(0, mine, after(theirs, right, left, last))
             beside = [pres[0]]

time: 185 us -> 166 us (0.90)
  Pallas kernels: 110 us -> 95.3 us
  waiting for transfers between devices: 38.7 us -> 30.2 us
  starting transfers between devices: 34.4 us -> 37 us
    pallas_call x8, Pallas kernels: 36.4 us -> 27.4 us  [the longest x3 25.5 us: w_out_grad_call(): pl.pallas_call(kernel, grid=(count,), in_specs=[whole(*act.shape) for act...]
    ppermute x2 -> x3, waiting for transfers between devices: 7.93 us -> 3.83 us  [swap_sums(): got = lax.ppermute(piece, RING, ring.swap())]
    ppermute x2, waiting for transfers between devices: 4.1 us -> 0.01 us  [step(): low = lax.ppermute(low, RING, ring.shift(1))]
    pallas_call x2, Pallas kernels: 22.9 us -> 20.1 us  [w_in_grad_call(): pl.pallas_call(kernel, grid=(count,), in_specs=[pl.BlockSpec((each.shape[...]
    ppermute x11, waiting for transfers between devices: 2.92 us -> 5.68 us  [other_core(): return [lax.ppermute(piece, RING, ring.swap()) for piece in pieces]]
    ppermute x5 -> x6, starting transfers between devices: 6.85 us -> 9.04 us  [exchange(): lax.ppermute(values, axis, [(i, (i + by) % size) for i in range(size)])]
    ppermute x5 -> x6, waiting for transfers between devices: 4.07 us -> 2.28 us  [exchange(): lax.ppermute(values, axis, [(i, (i + by) % size) for i in range(size)])]
  transfers between devices with their start and end apart: 42 -> 44, of which waited for: 21 -> 19; matrix products, arithmetic and copies ran while one was open for 0% -> 0% of each run, Pallas kernels for 51% -> 57%
where the time goes in v3:
time: 166 us
  Pallas kernels  95.3 us (57%)
  starting transfers between devices  37 us (22%)
  waiting for transfers between devices  30.2 us (18%)
  local copies, waits for them, and re-layouts  2.27 us (1%)
    pallas_call x3, Pallas kernels, w_out_grad_call(): pl.pallas_call(kernel, grid=(count,), in_specs=[whole(*act.shape) for act...  25.5 us
    pallas_call x2, Pallas kernels, w_in_grad_call(): pl.pallas_call(kernel, grid=(count,), in_specs=[pl.BlockSpec((each.shape[...  20.1 us
    pallas_call x2, Pallas kernels, grad_act_call(): pl.pallas_call(kernel, grid=(steps,), in_specs=[VMEM] * (len(flat) + 1),...  17.5 us
    pallas_call x2, Pallas kernels, in_grad_call(): pl.pallas_call(kernel, grid=(width // tile,), in_specs=[whole(count, hidd...  15.6 us
    ppermute x6, waiting for transfers between devices, step(): self.left = lax.ppermute(left, RING, ring.shift(1))  11.7 us
    ppermute x6, starting transfers between devices, step(): self.left = lax.ppermute(left, RING, ring.shift(1))  11.2 us
    ppermute x6, starting transfers between devices, exchange(): lax.ppermute(values, axis, [(i, (i + by) % size) for i in range(size)])  9.04 us
    pallas_call x1, Pallas kernels, hold_call(): pl.pallas_call(kernel, in_specs=[pl.BlockSpec(memory_space=pl.ANY)], out_...  7.09 us
  transfers between devices with their start and end apart: 44, of which 19 were waited for; matrix products, arithmetic and copies ran while one was open for 0% of the time, Pallas kernels for 57%

profile of v3, /device:TPU:0, one launch (start us, length us, event | category | flops | bytes accessed | tf_op | source)
XLA Modules:
  0.0 165.7 jit_solution(14621639059501894183)
XLA Ops:
  0.6 3.1 %collective-permute-start = (bf16[40,6144]{1,0:T(8,128)(2,1)}, bf16[40,6144]{1,0:T(8,128)(2,1)S(1)}, u32[]{:S(2)}, u32[]{:S(2)}) collective-permute-start(bf16[40,6144]{1,0:T(8,128)(2,1)} %refs_0_.1), channel_id=1, source_target_pairs={{0,1},{4,5},{1,2},{5,6},{2,3},{6,7},{3,11},{7,15},{11,10},{15,14},... | collective-permute-start | bytes 1474568 | tf_op jit(solution)/shard_map/ppermute | solution.py:478
  5.0 2.0 %collective-permute-start.2 = (bf16[112,1536]{1,0:T(8,128)(2,1)S(1)}, bf16[112,1536]{1,0:T(8,128)(2,1)S(1)}, u32[]{:S(2)}, u32[]{:S(2)}) collective-permute-start(bf16[112,1536]{1,0:T(8,128)(2,1)S(1)} %get-tuple-element.91), channel_id=1, source_target_pairs={{0,16},{16,0},{1,17},{17,1},{2,18},{18,2},{3,19},{19,3},{4,20},{20... | collective-permute-start | bytes 1032200 | tf_op jit(solution)/shard_map/ppermute | solution.py:490
  7.0 7.1 %hold.1 = (bf16[1536,6144]{1,0:T(8,128)(2,1)S(1)}, f32[8,128]{1,0:T(8,128)}) custom-call(bf16[1536,6144]{1,0:T(8,128)(2,1)} %weight_ref.1), custom_call_target="tpu_custom_call" | custom-call | flops 1 | bytes 1 | tf_op jit(solution)/shard_map/hold/pallas_call | solution.py:157
  14.1 1.6 collective-permute-done.2.refs_1_
  15.8 1.7 %collective-permute-start.10 = (bf16[208,1536]{1,0:T(8,128)(2,1)S(1)}, bf16[208,1536]{1,0:T(8,128)(2,1)S(1)}, u32[]{:S(2)}, u32[]{:S(2)}) collective-permute-start(bf16[208,1536]{1,0:T(8,128)(2,1)S(1)} %get-tuple-element.101), channel_id=1, source_target_pairs={{0,16},{16,0},{1,17},{17,1},{2,18},{18,2},{3,19},{19,3},{4,20},{20... | collective-permute-start | bytes 1916936 | tf_op jit(solution)/shard_map/ppermute | solution.py:490
  17.5 1.6 collective-permute-start.4
  20.1 10.0 %collective-permute-done.4.refs_3_ = bf16[40,6144]{1,0:T(8,128)(2,1)S(1)} collective-permute-done((bf16[40,6144]{1,0:T(8,128)(2,1)S(1)}, bf16[40,6144]{1,0:T(8,128)(2,1)S(1)}, u32[]{:S(2)}, u32[]{:S(2)}) %collective-permute-start.4) | collective-permute-done | bytes 491552 | tf_op jit(solution)/shard_map/ppermute | solution.py:478
  31.9 1.6 collective-permute-start.11
  34.0 10.3 %grad_act.2 = (bf16[400,6144]{1,0:T(8,128)(2,1)}, f32[400,1536]{1,0:T(8,128)}, bf16[160,1536]{1,0:T(8,128)(2,1)S(1)}, bf16[112,1536]{1,0:T(8,128)(2,1)}, bf16[128,1536]{1,0:T(8,128)(2,1)}) custom-call(bf16[40,6144]{1,0:T(8,128)(2,1)S(1)} %copy-done.9, bf16[40,6144]{1,0:T(8,128)(2,1)S(1)} %collective-permute-done.refs_1_, ...), custom_call_target="tpu_custom_call" | custom-call | flops 1 | bytes 1 | tf_op jit(solution)/shard_map/grad_act/pallas_call | solution.py:297
  44.3 1.7 %collective-permute-start.12 = (bf16[160,1536]{1,0:T(8,128)(2,1)S(1)}, bf16[160,1536]{1,0:T(8,128)(2,1)S(1)}, u32[]{:S(2)}, u32[]{:S(2)}) collective-permute-start(bf16[160,1536]{1,0:T(8,128)(2,1)S(1)} %get-tuple-element.103), channel_id=1, source_target_pairs={{0,16},{16,0},{1,17},{17,1},{2,18},{18,2},{3,19},{19,3},{4,20},{20... | collective-permute-start | bytes 1474568 | tf_op jit(solution)/shard_map/ppermute | solution.py:490
  46.5 1.6 collective-permute-start.14
  49.1 3.4 %gelu.2 = (bf16[400,1536]{1,0:T(8,128)(2,1)}, f32[400,1536]{1,0:T(8,128)}) custom-call(bf16[320,1536]{1,0:T(8,128)(2,1)S(1)} %copy-done.7, bf16[112,1536]{1,0:T(8,128)(2,1)S(1)} %collective-permute-done.2.refs_1_, bf16[208,1536]{1,0:T(8,128)(2,1)S(1)} %collective-permute-done.10.refs_2_), custom_call_target="tpu_custom_call" | custom-call | flops 3686400000 | bytes 1 | tf_op jit(solution)/shard_map/gelu/pallas_call | solution.py:126
  52.4 2.4 %gelu.3 = (bf16[240,1536]{1,0:T(8,128)(2,1)}, f32[240,1536]{1,0:T(8,128)}) custom-call(bf16[320,1536]{1,0:T(8,128)(2,1)S(1)} %copy-done.7, bf16[112,1536]{1,0:T(8,128)(2,1)S(1)} %collective-permute-done.2.refs_1_, bf16[208,1536]{1,0:T(8,128)(2,1)S(1)} %collective-permute-done.10.refs_2_), custom_call_target="tpu_custom_call" | custom-call | flops 2211840000 | bytes 1 | tf_op jit(solution)/shard_map/gelu/pallas_call | solution.py:126
  56.8 1.6 collective-permute-start.20
  58.8 7.2 %grad_act.3 = (bf16[240,6144]{1,0:T(8,128)(2,1)}, f32[240,1536]{1,0:T(8,128)}, bf16[240,1536]{1,0:T(8,128)(2,1)}) custom-call(bf16[40,6144]{1,0:T(8,128)(2,1)S(1)} %collective-permute-done.11.left_ref.refs_0_, bf16[40,6144]{1,0:T(8,128)(2,1)S(1)} %collective-permute-done.13.right_ref.refs_1_, bf16[40,3072]{1,0:T(8,128)(2,1)S(1)} %collective-permute-done.14.refs_2_, ...), custom_call_target="tpu_custom_call" | custom-call | flops 1 | bytes 1 | tf_op jit(solution)/shard_map/grad_act/pallas_call | solution.py:297
  66.6 5.6 %w_out_grad.3 = (bf16[1536,6144]{1,0:T(8,128)(2,1)}, bf16[1536,640]{1,0:T(8,128)(2,1)S(1)}) custom-call(bf16[400,1536]{1,0:T(8,128)(2,1)S(1)} %copy-done.11, bf16[240,1536]{1,0:T(8,128)(2,1)S(1)} %copy-done.12, bf16[400,6144]{1,0:T(8,128)(2,1)} %get-tuple-element.125.refs_2_.refs_1_, bf16[240,6144]{1,0:T(8,128)(2,1)} %get-tuple-element.126.refs_3_.refs_2_), custom_call_target="tpu_custom_call" | custom-call | flops 4026531840 | bytes 3145728 | tf_op jit(solution)/shard_map/w_out_grad/pallas_call | solution.py:394
  72.2 1.6 collective-permute-start.22
  74.3 11.7 %w_out_grad.4.refs_3_ = bf16[1536,6144]{1,0:T(8,128)(2,1)} custom-call(bf16[1536,640]{1,0:T(8,128)(2,1)S(1)} %get-tuple-element.141.refs_0_, bf16[400,6144]{1,0:T(8,128)(2,1)} %get-tuple-element.125.refs_2_.refs_1_, bf16[240,6144]{1,0:T(8,128)(2,1)} %get-tuple-element.126.refs_3_.refs_2_, ...), custom_call_target="tpu_custom_call", output_to_operand_aliasing={{}: (3, {})} | custom-call | flops 12079595520 | bytes 9437184 | tf_op jit(solution)/shard_map/w_out_grad/pallas_call | solution.py:394
  86.0 1.6 collective-permute-start.25
  88.0 1.6 collective-permute-start.27
  89.6 6.4 %in_grad.2 = (bf16[240,1536]{1,0:T(8,128)(2,1)}, f32[120,6144]{1,0:T(8,128)S(1)}, bf16[120,6144]{1,0:T(8,128)(2,1)S(1)}) custom-call(f32[240,1536]{1,0:T(8,128)S(1)} %copy-done.5, f32[240,1536]{1,0:T(8,128)S(1)} %copy-done.4, bf16[240,1536]{1,0:T(8,128)(2,1)S(1)} %collective-permute-done.24.refs_2_, bf16[6144,1536]{1,0:T(8,128)(2,1)S(1)} %bitcast.1), custom_call_target="tpu_custom_call" | custom-call | flops 1 | bytes 1 | tf_op jit(solution)/shard_map/in_grad/pallas_call | solution.py:345
  96.2 1.7 %collective-permute-done.25.left_ref.refs_0_ = bf16[40,6144]{1,0:T(8,128)(2,1)S(1)} collective-permute-done((bf16[40,6144]{1,0:T(8,128)(2,1)S(1)}, bf16[40,6144]{1,0:T(8,128)(2,1)S(1)}, u32[]{:S(2)}, u32[]{:S(2)}) %collective-permute-start.25) | collective-permute-done | bytes 491552 | tf_op jit(solution)/shard_map/ppermute | solution.py:478
  100.7 1.8 %collective-permute-done.28.refs_1_.refs_3_ = bf16[120,6144]{1,0:T(8,128)(2,1)S(1)} collective-permute-done((bf16[120,6144]{1,0:T(8,128)(2,1)S(1)}, bf16[120,6144]{1,0:T(8,128)(2,1)S(1)}, u32[]{:S(2)}, u32[]{:S(2)}) %collective-permute-start.28) | collective-permute-done | bytes 1474592 | tf_op jit(solution)/shard_map/ppermute | solution.py:589
  102.6 1.5 collective-permute-start.32
  106.8 8.2 %w_out_grad.5 = bf16[1536,6144]{1,0:T(8,128)(2,1)} custom-call(bf16[1536,640]{1,0:T(8,128)(2,1)S(1)} %get-tuple-element.141.refs_0_, bf16[400,6144]{1,0:T(8,128)(2,1)} %get-tuple-element.125.refs_2_.refs_1_, bf16[240,6144]{1,0:T(8,128)(2,1)} %get-tuple-element.126.refs_3_.refs_2_, bf16[1536,6144]{1,0:T(8,128)(2,1)} %w_out_grad.4.refs_3_), custom_call_target="tpu_custom_call", output_to_operand_aliasing={{}: (3, {})} | custom-call | flops 8053063680 | bytes 6291456 | tf_op jit(solution)/shard_map/w_out_grad/pallas_call | solution.py:394
  115.0 1.6 pack.2.refs_0_
  120.3 2.6 %collective-permute-done.34.refs_1_ = bf16[200,6144]{1,0:T(8,128)(2,1)S(1)} collective-permute-done((bf16[200,6144]{1,0:T(8,128)(2,1)S(1)}, bf16[200,6144]{1,0:T(8,128)(2,1)S(1)}, u32[]{:S(2)}, u32[]{:S(2)}) %collective-permute-start.34) | collective-permute-done | bytes 2457632 | tf_op jit(solution)/shard_map/ppermute | solution.py:484
  123.0 9.2 %in_grad.3 = (bf16[400,1536]{1,0:T(8,128)(2,1)}, f32[200,6144]{1,0:T(8,128)S(1)}, bf16[120,6144]{1,0:T(8,128)(2,1)S(1)}, bf16[80,6144]{1,0:T(8,128)(2,1)S(1)}) custom-call(f32[400,1536]{1,0:T(8,128)S(1)} %copy-done.2, f32[400,1536]{1,0:T(8,128)S(1)} %copy-done.3, bf16[160,1536]{1,0:T(8,128)(2,1)S(1)} %collective-permute-done.12.refs_2_, ...), custom_call_target="tpu_custom_call" | custom-call | flops 1 | bytes 1 | tf_op jit(solution)/shard_map/in_grad/pallas_call | solution.py:345
  133.6 2.1 %collective-permute-done.38.refs_1_.refs_3_ = bf16[80,6144]{1,0:T(8,128)(2,1)S(1)} collective-permute-done((bf16[80,6144]{1,0:T(8,128)(2,1)S(1)}, bf16[80,6144]{1,0:T(8,128)(2,1)S(1)}, u32[]{:S(2)}, u32[]{:S(2)}) %collective-permute-start.38) | collective-permute-done | bytes 983072 | tf_op jit(solution)/shard_map/ppermute | solution.py:589
  138.2 1.7 %collective-permute-done.39.refs_3_ = bf16[120,6144]{1,0:T(8,128)(2,1)S(1)} collective-permute-done((bf16[120,6144]{1,0:T(8,128)(2,1)S(1)}, bf16[120,6144]{1,0:T(8,128)(2,1)S(1)}, u32[]{:S(2)}, u32[]{:S(2)}) %collective-permute-start.39) | collective-permute-done | bytes 1474592 | tf_op jit(solution)/shard_map/ppermute | solution.py:484
  139.9 10.1 %w_in_grad.2.refs_6_ = bf16[6144,1536]{1,0:T(8,128)(2,1)} custom-call(bf16[200,6144]{1,0:T(8,128)(2,1)S(1)} %copy-done.1, bf16[200,6144]{1,0:T(8,128)(2,1)S(1)} %collective-permute-done.34.refs_1_, bf16[120,6144]{1,0:T(8,128)(2,1)S(1)} %pack.3.refs_2_, bf16[120,6144]{1,0:T(8,128)(2,1)S(1)} %collective-permute-done.39.refs_3_, ...), custom_call_target="tpu_custom_call" | custom-call | flops 9059696640 | bytes 9437184 | tf_op jit(solution)/shard_map/w_in_grad/pallas_call | solution.py:432
  153.1 10.1 %w_in_grad.3 = bf16[6144,1536]{1,0:T(8,128)(2,1)} custom-call(bf16[200,6144]{1,0:T(8,128)(2,1)S(1)} %copy-done.1, bf16[200,6144]{1,0:T(8,128)(2,1)S(1)} %collective-permute-done.34.refs_1_, bf16[120,6144]{1,0:T(8,128)(2,1)S(1)} %pack.3.refs_2_, bf16[120,6144]{1,0:T(8,128)(2,1)S(1)} %collective-permute-done.39.refs_3_, ...), custom_call_target="tpu_custom_call", output_to_operand_aliasing={{}: (6, {})} | custom-call | flops 9059696640 | bytes 9437184 | tf_op jit(solution)/shard_map/w_in_grad/pallas_call | solution.py:432
  (119 shorter events, 28.8 us)
Async XLA Ops:
  0.6 16.9 %collective-permute-start = (bf16[40,6144]{1,0:T(8,128)(2,1)}, bf16[40,6144]{1,0:T(8,128)(2,1)S(1)}, u32[]{:S(2)}, u32[]{:S(2)}) collective-permute-start(bf16[40,6144]{1,0:T(8,128)(2,1)} %refs_0_.1), channel_id=1, source_target_pairs={{0,1},{4,5},{1,2},{5,6},{2,3},{6,7},{3,11},{7,15},{11,10},{15,14},... | collective-permute-start | bytes 1474568 | tf_op jit(solution)/shard_map/ppermute | solution.py:478
  3.7 13.8 %collective-permute-start.1 = (bf16[40,6144]{1,0:T(8,128)(2,1)}, bf16[40,6144]{1,0:T(8,128)(2,1)S(1)}, u32[]{:S(2)}, u32[]{:S(2)}) collective-permute-start(bf16[40,6144]{1,0:T(8,128)(2,1)} %refs_0_.1), channel_id=1, source_target_pairs={{0,8},{4,12},{1,0},{5,4},{2,1},{6,5},{3,2},{7,6},{11,3},{15,7},{10... | collective-permute-start | bytes 1474568 | tf_op jit(solution)/shard_map/ppermute | solution.py:479
  3.7 13.8 %collective-permute-start.3 = (bf16[40,6144]{1,0:T(8,128)(2,1)}, bf16[40,6144]{1,0:T(8,128)(2,1)S(1)}, u32[]{:S(2)}, u32[]{:S(2)}) collective-permute-start(bf16[40,6144]{1,0:T(8,128)(2,1)} %refs_0_.1), channel_id=1, source_target_pairs={{0,4},{4,0},{1,5},{5,1},{2,6},{6,2},{3,7},{7,3},{11,15},{15,11},{1... | collective-permute-start | bytes 1474568 | tf_op jit(solution)/shard_map/ppermute | solution.py:484
  5.0 10.8 %collective-permute-start.2 = (bf16[112,1536]{1,0:T(8,128)(2,1)S(1)}, bf16[112,1536]{1,0:T(8,128)(2,1)S(1)}, u32[]{:S(2)}, u32[]{:S(2)}) collective-permute-start(bf16[112,1536]{1,0:T(8,128)(2,1)S(1)} %get-tuple-element.91), channel_id=1, source_target_pairs={{0,16},{16,0},{1,17},{17,1},{2,18},{18,2},{3,19},{19,3},{4,20},{20... | collective-permute-start | bytes 1032200 | tf_op jit(solution)/shard_map/ppermute | solution.py:490
  15.8 16.2 %collective-permute-start.10 = (bf16[208,1536]{1,0:T(8,128)(2,1)S(1)}, bf16[208,1536]{1,0:T(8,128)(2,1)S(1)}, u32[]{:S(2)}, u32[]{:S(2)}) collective-permute-start(bf16[208,1536]{1,0:T(8,128)(2,1)S(1)} %get-tuple-element.101), channel_id=1, source_target_pairs={{0,16},{16,0},{1,17},{17,1},{2,18},{18,2},{3,19},{19,3},{4,20},{20... | collective-permute-start | bytes 1916936 | tf_op jit(solution)/shard_map/ppermute | solution.py:490
  17.5 12.6 %collective-permute-start.4 = (bf16[40,6144]{1,0:T(8,128)(2,1)S(1)}, bf16[40,6144]{1,0:T(8,128)(2,1)S(1)}, u32[]{:S(2)}, u32[]{:S(2)}) collective-permute-start(bf16[40,6144]{1,0:T(8,128)(2,1)S(1)} %collective-permute-done.refs_1_), channel_id=1, source_target_pairs={{0,1},{4,5},{1,2},{5,6},{2,3},{6,7},{3,11},{7,15},{11,10},{15,14},... | collective-permute-start | bytes 1474568 | tf_op jit(solution)/shard_map/ppermute | solution.py:478
  19.1 12.3 %collective-permute-start.5 = (bf16[40,6144]{1,0:T(8,128)(2,1)S(1)}, bf16[40,6144]{1,0:T(8,128)(2,1)S(1)}, u32[]{:S(2)}, u32[]{:S(2)}) collective-permute-start(bf16[40,6144]{1,0:T(8,128)(2,1)S(1)} %collective-permute-done.1.refs_2_), channel_id=1, source_target_pairs={{0,8},{4,12},{1,0},{5,4},{2,1},{6,5},{3,2},{7,6},{11,3},{15,7},{10... | collective-permute-start | bytes 1474568 | tf_op jit(solution)/shard_map/ppermute | solution.py:479
  19.6 11.8 %collective-permute-start.6 = (bf16[40,6144]{1,0:T(8,128)(2,1)S(1)}, bf16[40,6144]{1,0:T(8,128)(2,1)S(1)}, u32[]{:S(2)}, u32[]{:S(2)}) collective-permute-start(bf16[40,6144]{1,0:T(8,128)(2,1)S(1)} %collective-permute-done.refs_1_), channel_id=1, source_target_pairs={{0,4},{4,0},{1,5},{5,1},{2,6},{6,2},{3,7},{7,3},{11,15},{15,11},{1... | collective-permute-start | bytes 1474568 | tf_op jit(solution)/shard_map/ppermute | solution.py:484
  19.6 11.8 %collective-permute-start.7 = (bf16[40,6144]{1,0:T(8,128)(2,1)S(1)}, bf16[40,6144]{1,0:T(8,128)(2,1)S(1)}, u32[]{:S(2)}, u32[]{:S(2)}) collective-permute-start(bf16[40,6144]{1,0:T(8,128)(2,1)S(1)} %collective-permute-done.1.refs_2_), channel_id=1, source_target_pairs={{0,4},{4,0},{1,5},{5,1},{2,6},{6,2},{3,7},{7,3},{11,15},{15,11},{1... | collective-permute-start | bytes 1474568 | tf_op jit(solution)/shard_map/ppermute | solution.py:484
  31.9 14.0 %collective-permute-start.11 = (bf16[40,6144]{1,0:T(8,128)(2,1)S(1)}, bf16[40,6144]{1,0:T(8,128)(2,1)S(1)}, u32[]{:S(2)}, u32[]{:S(2)}) collective-permute-start(bf16[40,6144]{1,0:T(8,128)(2,1)S(1)} %collective-permute-done.4.refs_3_), channel_id=1, source_target_pairs={{0,1},{4,5},{1,2},{5,6},{2,3},{6,7},{3,11},{7,15},{11,10},{15,14},... | collective-permute-start | bytes 1474568 | tf_op jit(solution)/shard_map/ppermute | solution.py:478
  33.6 12.9 %collective-permute-start.13 = (bf16[40,6144]{1,0:T(8,128)(2,1)S(1)}, bf16[40,6144]{1,0:T(8,128)(2,1)S(1)}, u32[]{:S(2)}, u32[]{:S(2)}) collective-permute-start(bf16[40,6144]{1,0:T(8,128)(2,1)S(1)} %collective-permute-done.5.refs_4_), channel_id=1, source_target_pairs={{0,8},{4,12},{1,0},{5,4},{2,1},{6,5},{3,2},{7,6},{11,3},{15,7},{10... | collective-permute-start | bytes 1474568 | tf_op jit(solution)/shard_map/ppermute | solution.py:479
  44.3 14.5 %collective-permute-start.12 = (bf16[160,1536]{1,0:T(8,128)(2,1)S(1)}, bf16[160,1536]{1,0:T(8,128)(2,1)S(1)}, u32[]{:S(2)}, u32[]{:S(2)}) collective-permute-start(bf16[160,1536]{1,0:T(8,128)(2,1)S(1)} %get-tuple-element.103), channel_id=1, source_target_pairs={{0,16},{16,0},{1,17},{17,1},{2,18},{18,2},{3,19},{19,3},{4,20},{20... | collective-permute-start | bytes 1474568 | tf_op jit(solution)/shard_map/ppermute | solution.py:490
  46.5 8.3 %collective-permute-start.14 = (bf16[40,3072]{1,0:T(8,128)(2,1)S(1)}, bf16[40,3072]{1,0:T(8,128)(2,1)S(1)}, u32[]{:S(2)}, u32[]{:S(2)}) collective-permute-start(bf16[40,3072]{1,0:T(8,128)(2,1)S(1)} %get-tuple-element.110), channel_id=1, source_target_pairs={{0,1},{4,5},{1,2},{5,6},{2,3},{6,7},{3,11},{7,15},{11,10},{15,14},... | collective-permute-start | bytes 737288 | tf_op jit(solution)/shard_map/ppermute | solution.py:472
  56.8 15.4 %collective-permute-start.20 = (bf16[40,6144]{1,0:T(8,128)(2,1)S(1)}, bf16[40,6144]{1,0:T(8,128)(2,1)S(1)}, u32[]{:S(2)}, u32[]{:S(2)}) collective-permute-start(bf16[40,6144]{1,0:T(8,128)(2,1)S(1)} %copy-done.10), channel_id=1, source_target_pairs={{0,1},{4,5},{1,2},{5,6},{2,3},{6,7},{3,11},{7,15},{11,10},{15,14},... | collective-permute-start | bytes 1474568 | tf_op jit(solution)/shard_map/ppermute | solution.py:478
  58.4 13.9 %collective-permute-start.21 = (bf16[40,6144]{1,0:T(8,128)(2,1)S(1)}, bf16[40,6144]{1,0:T(8,128)(2,1)S(1)}, u32[]{:S(2)}, u32[]{:S(2)}) collective-permute-start(bf16[40,6144]{1,0:T(8,128)(2,1)S(1)} %copy-done.10), channel_id=1, source_target_pairs={{0,8},{4,12},{1,0},{5,4},{2,1},{6,5},{3,2},{7,6},{11,3},{15,7},{10... | collective-permute-start | bytes 1474568 | tf_op jit(solution)/shard_map/ppermute | solution.py:479
  66.0 22.0 %collective-permute-start.24 = (bf16[240,1536]{1,0:T(8,128)(2,1)}, bf16[240,1536]{1,0:T(8,128)(2,1)S(1)}, u32[]{:S(2)}, u32[]{:S(2)}) collective-permute-start(bf16[240,1536]{1,0:T(8,128)(2,1)} %get-tuple-element.132), channel_id=1, source_target_pairs={{0,16},{16,0},{1,17},{17,1},{2,18},{18,2},{3,19},{19,3},{4,20},{20... | collective-permute-start | bytes 2211848 | tf_op jit(solution)/shard_map/ppermute | solution.py:490
  72.2 13.7 %collective-permute-start.22 = (bf16[40,6144]{1,0:T(8,128)(2,1)S(1)}, bf16[40,6144]{1,0:T(8,128)(2,1)S(1)}, u32[]{:S(2)}, u32[]{:S(2)}) collective-permute-start(bf16[40,6144]{1,0:T(8,128)(2,1)S(1)} %collective-permute-done.20.refs_1_), channel_id=1, source_target_pairs={{0,1},{4,5},{1,2},{5,6},{2,3},{6,7},{3,11},{7,15},{11,10},{15,14},... | collective-permute-start | bytes 1474568 | tf_op jit(solution)/shard_map/ppermute | solution.py:478
  73.8 12.2 %collective-permute-start.23 = (bf16[40,6144]{1,0:T(8,128)(2,1)S(1)}, bf16[40,6144]{1,0:T(8,128)(2,1)S(1)}, u32[]{:S(2)}, u32[]{:S(2)}) collective-permute-start(bf16[40,6144]{1,0:T(8,128)(2,1)S(1)} %collective-permute-done.21.refs_2_), channel_id=1, source_target_pairs={{0,8},{4,12},{1,0},{5,4},{2,1},{6,5},{3,2},{7,6},{11,3},{15,7},{10... | collective-permute-start | bytes 1474568 | tf_op jit(solution)/shard_map/ppermute | solution.py:479
  86.0 11.9 %collective-permute-start.25 = (bf16[40,6144]{1,0:T(8,128)(2,1)S(1)}, bf16[40,6144]{1,0:T(8,128)(2,1)S(1)}, u32[]{:S(2)}, u32[]{:S(2)}) collective-permute-start(bf16[40,6144]{1,0:T(8,128)(2,1)S(1)} %collective-permute-done.22.refs_3_), channel_id=1, source_target_pairs={{0,1},{4,5},{1,2},{5,6},{2,3},{6,7},{3,11},{7,15},{11,10},{15,14},... | collective-permute-start | bytes 1474568 | tf_op jit(solution)/shard_map/ppermute | solution.py:478
  87.6 11.6 %collective-permute-start.26 = (bf16[40,6144]{1,0:T(8,128)(2,1)S(1)}, bf16[40,6144]{1,0:T(8,128)(2,1)S(1)}, u32[]{:S(2)}, u32[]{:S(2)}) collective-permute-start(bf16[40,6144]{1,0:T(8,128)(2,1)S(1)} %collective-permute-done.23.refs_4_), channel_id=1, source_target_pairs={{0,8},{4,12},{1,0},{5,4},{2,1},{6,5},{3,2},{7,6},{11,3},{15,7},{10... | collective-permute-start | bytes 1474568 | tf_op jit(solution)/shard_map/ppermute | solution.py:479
  88.0 8.2 %collective-permute-start.27 = (bf16[112,1536]{1,0:T(8,128)(2,1)S(1)}, bf16[112,1536]{1,0:T(8,128)(2,1)S(1)}, u32[]{:S(2)}, u32[]{:S(2)}) collective-permute-start(bf16[112,1536]{1,0:T(8,128)(2,1)S(1)} %copy-done.14), channel_id=1, source_target_pairs={{0,16},{16,0},{1,17},{17,1},{2,18},{18,2},{3,19},{19,3},{4,20},{20... | collective-permute-start | bytes 1032200 | tf_op jit(solution)/shard_map/ppermute | solution.py:490
  99.2 17.4 %collective-permute-start.29 = (bf16[128,1536]{1,0:T(8,128)(2,1)S(1)}, bf16[128,1536]{1,0:T(8,128)(2,1)S(1)}, u32[]{:S(2)}, u32[]{:S(2)}) collective-permute-start(bf16[128,1536]{1,0:T(8,128)(2,1)S(1)} %copy-done.13), channel_id=1, source_target_pairs={{0,16},{16,0},{1,17},{17,1},{2,18},{18,2},{3,19},{19,3},{4,20},{20... | collective-permute-start | bytes 1179656 | tf_op jit(solution)/shard_map/ppermute | solution.py:490
  102.6 14.5 %collective-permute-start.32 = (bf16[40,3072]{1,0:T(8,128)(2,1)S(1)}, bf16[40,3072]{1,0:T(8,128)(2,1)S(1)}, u32[]{:S(2)}, u32[]{:S(2)}) collective-permute-start(bf16[40,3072]{1,0:T(8,128)(2,1)S(1)} %get-tuple-element.139), channel_id=1, source_target_pairs={{0,1},{4,5},{1,2},{5,6},{2,3},{6,7},{3,11},{7,15},{11,10},{15,14},... | collective-permute-start | bytes 737288 | tf_op jit(solution)/shard_map/ppermute | solution.py:620
  104.1 13.0 %collective-permute-start.33 = (bf16[40,3072]{1,0:T(8,128)(2,1)S(1)}, bf16[40,3072]{1,0:T(8,128)(2,1)S(1)}, u32[]{:S(2)}, u32[]{:S(2)}) collective-permute-start(bf16[40,3072]{1,0:T(8,128)(2,1)S(1)} %get-tuple-element.140), channel_id=1, source_target_pairs={{0,8},{4,12},{1,0},{5,4},{2,1},{6,5},{3,2},{7,6},{11,3},{15,7},{10... | collective-permute-start | bytes 737288 | tf_op jit(solution)/shard_map/ppermute | solution.py:621
  104.7 11.9 %collective-permute-start.30 = (bf16[40,3072]{1,0:T(8,128)(2,1)S(1)}, bf16[40,3072]{1,0:T(8,128)(2,1)S(1)}, u32[]{:S(2)}, u32[]{:S(2)}) collective-permute-start(bf16[40,3072]{1,0:T(8,128)(2,1)S(1)} %get-tuple-element.145), channel_id=1, source_target_pairs={{0,1},{4,5},{1,2},{5,6},{2,3},{6,7},{3,11},{7,15},{11,10},{15,14},... | collective-permute-start | bytes 737288 | tf_op jit(solution)/shard_map/ppermute | solution.py:472
  106.2 10.9 %collective-permute-start.31 = (bf16[40,3072]{1,0:T(8,128)(2,1)S(1)}, bf16[40,3072]{1,0:T(8,128)(2,1)S(1)}, u32[]{:S(2)}, u32[]{:S(2)}) collective-permute-start(bf16[40,3072]{1,0:T(8,128)(2,1)S(1)} %get-tuple-element.146), channel_id=1, source_target_pairs={{0,8},{4,12},{1,0},{5,4},{2,1},{6,5},{3,2},{7,6},{11,3},{15,7},{10... | collective-permute-start | bytes 737288 | tf_op jit(solution)/shard_map/ppermute | solution.py:473
  118.3 14.0 %collective-permute-start.35 = (bf16[40,6144]{1,0:T(8,128)(2,1)S(1)}, bf16[40,6144]{1,0:T(8,128)(2,1)S(1)}, u32[]{:S(2)}, u32[]{:S(2)}) collective-permute-start(bf16[40,6144]{1,0:T(8,128)(2,1)S(1)} %get-tuple-element.153), channel_id=1, source_target_pairs={{0,1},{4,5},{1,2},{5,6},{2,3},{6,7},{3,11},{7,15},{11,10},{15,14},... | collective-permute-start | bytes 1474568 | tf_op jit(solution)/shard_map/ppermute | solution.py:620
  119.8 13.4 %collective-permute-start.36 = (bf16[40,6144]{1,0:T(8,128)(2,1)S(1)}, bf16[40,6144]{1,0:T(8,128)(2,1)S(1)}, u32[]{:S(2)}, u32[]{:S(2)}) collective-permute-start(bf16[40,6144]{1,0:T(8,128)(2,1)S(1)} %get-tuple-element.154), channel_id=1, source_target_pairs={{0,8},{4,12},{1,0},{5,4},{2,1},{6,5},{3,2},{7,6},{11,3},{15,7},{10... | collective-permute-start | bytes 1474568 | tf_op jit(solution)/shard_map/ppermute | solution.py:621
  136.2 13.8 %collective-permute-start.40 = (bf16[40,6144]{1,0:T(8,128)(2,1)S(1)}, bf16[40,6144]{1,0:T(8,128)(2,1)S(1)}, u32[]{:S(2)}, u32[]{:S(2)}) collective-permute-start(bf16[40,6144]{1,0:T(8,128)(2,1)S(1)} %get-tuple-element.168), channel_id=1, source_target_pairs={{0,1},{4,5},{1,2},{5,6},{2,3},{6,7},{3,11},{7,15},{11,10},{15,14},... | collective-permute-start | bytes 1474568 | tf_op jit(solution)/shard_map/ppermute | solution.py:620
  137.6 13.2 %collective-permute-start.41 = (bf16[40,6144]{1,0:T(8,128)(2,1)S(1)}, bf16[40,6144]{1,0:T(8,128)(2,1)S(1)}, u32[]{:S(2)}, u32[]{:S(2)}) collective-permute-start(bf16[40,6144]{1,0:T(8,128)(2,1)S(1)} %get-tuple-element.169), channel_id=1, source_target_pairs={{0,8},{4,12},{1,0},{5,4},{2,1},{6,5},{3,2},{7,6},{11,3},{15,7},{10... | collective-permute-start | bytes 1474568 | tf_op jit(solution)/shard_map/ppermute | solution.py:621
  151.1 12.5 %collective-permute-start.42 = (bf16[40,6144]{1,0:T(8,128)(2,1)S(1)}, bf16[40,6144]{1,0:T(8,128)(2,1)S(1)}, u32[]{:S(2)}, u32[]{:S(2)}) collective-permute-start(bf16[40,6144]{1,0:T(8,128)(2,1)S(1)} %get-tuple-element.174), channel_id=1, source_target_pairs={{0,1},{4,5},{1,2},{5,6},{2,3},{6,7},{3,11},{7,15},{11,10},{15,14},... | collective-permute-start | bytes 1474568 | tf_op jit(solution)/shard_map/ppermute | solution.py:620
  152.4 12.3 %collective-permute-start.43 = (bf16[40,6144]{1,0:T(8,128)(2,1)S(1)}, bf16[40,6144]{1,0:T(8,128)(2,1)S(1)}, u32[]{:S(2)}, u32[]{:S(2)}) collective-permute-start(bf16[40,6144]{1,0:T(8,128)(2,1)S(1)} %get-tuple-element.175), channel_id=1, source_target_pairs={{0,8},{4,12},{1,0},{5,4},{2,1},{6,5},{3,2},{7,6},{11,3},{15,7},{10... | collective-permute-start | bytes 1474568 | tf_op jit(solution)/shard_map/ppermute | solution.py:621
  (32 other events, 265.7 us)

commit v4 on v3

--- a/solution.py
+++ b/solution.py
@@ -189,7 +189,7 @@
 
 def parts_call(values):
     rows, width = values.shape
-    cut = rows * 7 // 20 // 16 * 16
+    cut = rows // 2 // 16 * 16
 
     def kernel(ref, upper_ref, lower_ref):
         upper_ref[...] = ref[:cut, :]
@@ -510,13 +510,13 @@
         first, last = ring.groups()[number][0], ring.groups()[number][-1]
         while grads.done < last:
             if number > 0 and grads.done >= first:
-                grads.step(sent)
+                grads.step(sent, came)
             elif grads.done == 1:
-                grads.step(here, came[0], swapped[0])
-                came.append(exchange(after(lower, came[0], here), "gx"))
+                grads.step(here, swapped[0])
+                came.append(exchange(after(lower, came[0], grads.held[1]), "gx"))
             else:
                 earlier = [each for offset, each in swapped.items() if abs(offset) < grads.done]
-                grads.step(*([earlier, came] if grads.done > 1 else []))
+                grads.step(*([earlier, came[0]] if grads.done > 1 else []))
             if number > 0 and grads.done == last:
                 pres_x = [pre_act] + [each for pieces in zip(*came) for each in pieces]
                 ready = after(pres_x, sent)
@@ -535,7 +535,7 @@
             early, late = exchange(sent[0], "gx"), sent[1:]
     received = [[each] for each in exchange(sent[0], "gx")]
 
-    tokens = Gather(ring, after(inputs, grads.held[ring.half], swapped), True)
+    tokens = Gather(ring, after(inputs, grads.held[ring.half], [each for offset, each in swapped.items() if offset != ring.half]), True)
     chunks = constrained(chunks)
 
     def advance(*others):
@@ -606,7 +606,9 @@
 
     mine, theirs = in_grad_chunk(1, received, w_out_grad, advance(*w_out_grad))
     middle = exchange(after(late[0], received), "gx")
-    swap_sums(1, mine, after(theirs, list(tokens.held.values()), middle))
+    if order[0][-1] in tokens.held:
+        pack(0, pres[1])
+    swap_sums(1, mine, after(theirs, list(tokens.held.values()), middle, list(packed.values())))
     right, left, beside = [], [], []
     for step in range(ring.half, 0, -1):
         if step == ring.half and ring.even:
@@ -621,7 +623,7 @@
         left = [(lax.ppermute(going[1], RING, ring.shift(-1)), cut)]
         beside = []
         for one in packed.values():
-            if len(one) == 1:
+            if len(one) == 1 and step < ring.half:
                 one += other_core(ring, after(one, *going))
         if step == ring.half:
             late = exchange(after(late[1], middle), "gx")
@@ -629,8 +631,6 @@
                 beside = w_out_piece(*going)
             tokens.step(*going)
             beside = [beside, late, list(tokens.held.values())]
-            if order[0][-1] in tokens.held:
-                beside = [beside, pack(0, *going)]
         if 0 not in sums and step <= ring.half - (1 if beside or step < ring.half else 0):
             while tokens.done < ring.half:
                 tokens.step(*going)

time: 166 us -> 161 us (0.970)
  waiting for transfers between devices: 30.2 us -> 27.3 us
    ppermute x4, starting transfers between devices: 5.67 us -> 3.3 us  [shards(): right = [(lax.ppermute(going[0], RING, ring.shift(1)), 0)]]
    ppermute x4, starting transfers between devices: 2.56 us -> 4.92 us  [shards(): left = [(lax.ppermute(going[1], RING, ring.shift(-1)), cut)]]
    ppermute x6, waiting for transfers between devices: 2.28 us -> 0.02 us  [exchange(): lax.ppermute(values, axis, [(i, (i + by) % size) for i in range(size)])]
    ppermute x6, waiting for transfers between devices: 11.7 us -> 9.89 us  [step(): self.left = lax.ppermute(left, RING, ring.shift(1))]
    ppermute x6, waiting for transfers between devices: 3.15 us -> 4.95 us  [step(): self.right = lax.ppermute(right, RING, ring.shift(-1))]
    ppermute x4, waiting for transfers between devices: 2.68 us -> 0.94 us  [shards(): left = [(lax.ppermute(going[1], RING, ring.shift(-1)), cut)]]
  transfers between devices with their start and end apart: 44 -> 44, of which waited for: 19 -> 18; matrix products, arithmetic and copies ran while one was open for 0% -> 0% of each run, Pallas kernels for 57% -> 58%
where the time goes in v4:
time: 161 us
  Pallas kernels  95.3 us (59%)
  starting transfers between devices  35.7 us (22%)
  waiting for transfers between devices  27.3 us (17%)
    pallas_call x3, Pallas kernels, w_out_grad_call(): pl.pallas_call(kernel, grid=(count,), in_specs=[whole(*act.shape) for act...  25.5 us
    pallas_call x2, Pallas kernels, w_in_grad_call(): pl.pallas_call(kernel, grid=(count,), in_specs=[pl.BlockSpec((each.shape[...  20.1 us
    pallas_call x2, Pallas kernels, grad_act_call(): pl.pallas_call(kernel, grid=(steps,), in_specs=[VMEM] * (len(flat) + 1),...  17.6 us
    pallas_call x2, Pallas kernels, in_grad_call(): pl.pallas_call(kernel, grid=(width // tile,), in_specs=[whole(count, hidd...  15.6 us
    ppermute x6, starting transfers between devices, step(): self.left = lax.ppermute(left, RING, ring.shift(1))  10.7 us
    ppermute x6, waiting for transfers between devices, step(): self.left = lax.ppermute(left, RING, ring.shift(1))  9.89 us
    ppermute x6, starting transfers between devices, exchange(): lax.ppermute(values, axis, [(i, (i + by) % size) for i in range(size)])  7.72 us
    pallas_call x1, Pallas kernels, hold_call(): pl.pallas_call(kernel, in_specs=[pl.BlockSpec(memory_space=pl.ANY)], out_...  7.09 us
  transfers between devices with their start and end apart: 44, of which 18 were waited for; matrix products, arithmetic and copies ran while one was open for 0% of the time, Pallas kernels for 58%

profile of v4, /device:TPU:0, one launch (start us, length us, event | category | flops | bytes accessed | tf_op | source)
XLA Modules:
  0.0 160.7 jit_solution(2213813876142043222)
XLA Ops:
  0.6 3.1 %collective-permute-start = (bf16[40,6144]{1,0:T(8,128)(2,1)}, bf16[40,6144]{1,0:T(8,128)(2,1)S(1)}, u32[]{:S(2)}, u32[]{:S(2)}) collective-permute-start(bf16[40,6144]{1,0:T(8,128)(2,1)} %refs_0_.1), channel_id=1, source_target_pairs={{0,1},{4,5},{1,2},{5,6},{2,3},{6,7},{3,11},{7,15},{11,10},{15,14},... | collective-permute-start | bytes 1474568 | tf_op jit(solution)/shard_map/ppermute | solution.py:478
  5.0 2.0 %collective-permute-start.9 = (bf16[160,1536]{1,0:T(8,128)(2,1)S(1)}, bf16[160,1536]{1,0:T(8,128)(2,1)S(1)}, u32[]{:S(2)}, u32[]{:S(2)}) collective-permute-start(bf16[160,1536]{1,0:T(8,128)(2,1)S(1)} %get-tuple-element.99), channel_id=1, source_target_pairs={{0,16},{16,0},{1,17},{17,1},{2,18},{18,2},{3,19},{19,3},{4,20},{20... | collective-permute-start | bytes 1474568 | tf_op jit(solution)/shard_map/ppermute | solution.py:490
  7.0 7.1 %hold.1 = (bf16[1536,6144]{1,0:T(8,128)(2,1)S(1)}, f32[8,128]{1,0:T(8,128)}) custom-call(bf16[1536,6144]{1,0:T(8,128)(2,1)} %weight_ref.1), custom_call_target="tpu_custom_call" | custom-call | flops 1 | bytes 1 | tf_op jit(solution)/shard_map/hold/pallas_call | solution.py:157
  15.1 1.5 collective-permute-done.1.refs_2_
  16.6 1.6 collective-permute-start.3
  19.1 1.5 collective-permute-start.13
  20.7 7.7 %collective-permute-done.3.refs_3_ = bf16[40,6144]{1,0:T(8,128)(2,1)S(1)} collective-permute-done((bf16[40,6144]{1,0:T(8,128)(2,1)S(1)}, bf16[40,6144]{1,0:T(8,128)(2,1)S(1)}, u32[]{:S(2)}, u32[]{:S(2)}) %collective-permute-start.3) | collective-permute-done | bytes 491552 | tf_op jit(solution)/shard_map/ppermute | solution.py:478
  29.7 1.6 %collective-permute-start.10 = (bf16[40,6144]{1,0:T(8,128)(2,1)S(1)}, bf16[40,6144]{1,0:T(8,128)(2,1)S(1)}, u32[]{:S(2)}, u32[]{:S(2)}) collective-permute-start(bf16[40,6144]{1,0:T(8,128)(2,1)S(1)} %collective-permute-done.3.refs_3_), channel_id=1, source_target_pairs={{0,1},{4,5},{1,2},{5,6},{2,3},{6,7},{3,11},{7,15},{11,10},{15,14},... | collective-permute-start | bytes 1474568 | tf_op jit(solution)/shard_map/ppermute | solution.py:478
  31.8 10.3 %grad_act.2 = (bf16[400,6144]{1,0:T(8,128)(2,1)}, f32[400,1536]{1,0:T(8,128)}, bf16[160,1536]{1,0:T(8,128)(2,1)S(1)}, bf16[112,1536]{1,0:T(8,128)(2,1)}, bf16[128,1536]{1,0:T(8,128)(2,1)}) custom-call(bf16[40,6144]{1,0:T(8,128)(2,1)S(1)} %copy-done.9, bf16[40,6144]{1,0:T(8,128)(2,1)S(1)} %collective-permute-done.refs_1_, ...), custom_call_target="tpu_custom_call" | custom-call | flops 1 | bytes 1 | tf_op jit(solution)/shard_map/grad_act/pallas_call | solution.py:297
  42.1 1.6 collective-permute-start.11
  44.7 1.5 collective-permute-start.14
  47.2 3.4 %gelu.2 = (bf16[400,1536]{1,0:T(8,128)(2,1)}, f32[400,1536]{1,0:T(8,128)}) custom-call(bf16[320,1536]{1,0:T(8,128)(2,1)S(1)} %copy-done.7, bf16[160,1536]{1,0:T(8,128)(2,1)S(1)} %collective-permute-done.9.refs_1_, bf16[160,1536]{1,0:T(8,128)(2,1)S(1)} %collective-permute-done.13.refs_2_), custom_call_target="tpu_custom_call" | custom-call | flops 3686400000 | bytes 1 | tf_op jit(solution)/shard_map/gelu/pallas_call | solution.py:126
  50.6 2.4 %gelu.3 = (bf16[240,1536]{1,0:T(8,128)(2,1)}, f32[240,1536]{1,0:T(8,128)}) custom-call(bf16[320,1536]{1,0:T(8,128)(2,1)S(1)} %copy-done.7, bf16[160,1536]{1,0:T(8,128)(2,1)S(1)} %collective-permute-done.9.refs_1_, bf16[160,1536]{1,0:T(8,128)(2,1)S(1)} %collective-permute-done.13.refs_2_), custom_call_target="tpu_custom_call" | custom-call | flops 2211840000 | bytes 1 | tf_op jit(solution)/shard_map/gelu/pallas_call | solution.py:126
  53.6 1.5 collective-permute-start.20
  55.7 7.3 %grad_act.3 = (bf16[240,6144]{1,0:T(8,128)(2,1)}, f32[240,1536]{1,0:T(8,128)}, bf16[240,1536]{1,0:T(8,128)(2,1)}) custom-call(bf16[40,6144]{1,0:T(8,128)(2,1)S(1)} %collective-permute-done.10.left_ref.refs_0_, bf16[40,6144]{1,0:T(8,128)(2,1)S(1)} %collective-permute-done.12.right_ref.refs_1_, bf16[40,3072]{1,0:T(8,128)(2,1)S(1)} %collective-permute-done.14.refs_2_, ...), custom_call_target="tpu_custom_call" | custom-call | flops 1 | bytes 1 | tf_op jit(solution)/shard_map/grad_act/pallas_call | solution.py:297
  63.0 1.6 collective-permute-start.24
  64.6 5.6 %w_out_grad.3 = (bf16[1536,6144]{1,0:T(8,128)(2,1)}, bf16[1536,640]{1,0:T(8,128)(2,1)S(1)}) custom-call(bf16[400,1536]{1,0:T(8,128)(2,1)S(1)} %copy-done.11, bf16[240,1536]{1,0:T(8,128)(2,1)S(1)} %copy-done.12, bf16[400,6144]{1,0:T(8,128)(2,1)} %get-tuple-element.125.refs_2_.refs_1_, bf16[240,6144]{1,0:T(8,128)(2,1)} %get-tuple-element.126.refs_3_.refs_2_), custom_call_target="tpu_custom_call" | custom-call | flops 4026531840 | bytes 3145728 | tf_op jit(solution)/shard_map/w_out_grad/pallas_call | solution.py:394
  70.2 1.5 collective-permute-start.22
  72.3 11.6 %w_out_grad.4.refs_3_ = bf16[1536,6144]{1,0:T(8,128)(2,1)} custom-call(bf16[1536,640]{1,0:T(8,128)(2,1)S(1)} %get-tuple-element.147.refs_0_, bf16[400,6144]{1,0:T(8,128)(2,1)} %get-tuple-element.125.refs_2_.refs_1_, bf16[240,6144]{1,0:T(8,128)(2,1)} %get-tuple-element.126.refs_3_.refs_2_, ...), custom_call_target="tpu_custom_call", output_to_operand_aliasing={{}: (3, {})} | custom-call | flops 12079595520 | bytes 9437184 | tf_op jit(solution)/shard_map/w_out_grad/pallas_call | solution.py:394
  83.9 1.5 collective-permute-start.25
  86.6 6.4 %in_grad.2 = (bf16[240,1536]{1,0:T(8,128)(2,1)}, f32[120,6144]{1,0:T(8,128)S(1)}, bf16[120,6144]{1,0:T(8,128)(2,1)S(1)}) custom-call(f32[240,1536]{1,0:T(8,128)S(1)} %copy-done.5, f32[240,1536]{1,0:T(8,128)S(1)} %copy-done.4, bf16[240,1536]{1,0:T(8,128)(2,1)S(1)} %collective-permute-done.24.refs_2_, bf16[6144,1536]{1,0:T(8,128)(2,1)S(1)} %bitcast.1), custom_call_target="tpu_custom_call" | custom-call | flops 1 | bytes 1 | tf_op jit(solution)/shard_map/in_grad/pallas_call | solution.py:345
  92.9 1.6 pack.2.refs_0_
  97.5 2.7 %collective-permute-done.28.refs_1_.refs_3_ = bf16[120,6144]{1,0:T(8,128)(2,1)S(1)} collective-permute-done((bf16[120,6144]{1,0:T(8,128)(2,1)S(1)}, bf16[120,6144]{1,0:T(8,128)(2,1)S(1)}, u32[]{:S(2)}, u32[]{:S(2)}) %collective-permute-start.28) | collective-permute-done | bytes 1474592 | tf_op jit(solution)/shard_map/ppermute | solution.py:589
  101.0 1.4 collective-permute-start.33
  103.1 1.4 collective-permute-start.31
  104.5 8.2 %w_out_grad.5 = bf16[1536,6144]{1,0:T(8,128)(2,1)} custom-call(bf16[1536,640]{1,0:T(8,128)(2,1)S(1)} %get-tuple-element.147.refs_0_, bf16[400,6144]{1,0:T(8,128)(2,1)} %get-tuple-element.125.refs_2_.refs_1_, bf16[240,6144]{1,0:T(8,128)(2,1)} %get-tuple-element.126.refs_3_.refs_2_, bf16[1536,6144]{1,0:T(8,128)(2,1)} %w_out_grad.4.refs_3_), custom_call_target="tpu_custom_call", output_to_operand_aliasing={{}: (3, {})} | custom-call | flops 8053063680 | bytes 6291456 | tf_op jit(solution)/shard_map/w_out_grad/pallas_call | solution.py:394
  116.5 2.6 %collective-permute-done.34.refs_1_ = bf16[200,6144]{1,0:T(8,128)(2,1)S(1)} collective-permute-done((bf16[200,6144]{1,0:T(8,128)(2,1)S(1)}, bf16[200,6144]{1,0:T(8,128)(2,1)S(1)}, u32[]{:S(2)}, u32[]{:S(2)}) %collective-permute-start.34) | collective-permute-done | bytes 2457632 | tf_op jit(solution)/shard_map/ppermute | solution.py:484
  119.1 9.2 %in_grad.3 = (bf16[400,1536]{1,0:T(8,128)(2,1)}, f32[200,6144]{1,0:T(8,128)S(1)}, bf16[120,6144]{1,0:T(8,128)(2,1)S(1)}, bf16[80,6144]{1,0:T(8,128)(2,1)S(1)}) custom-call(f32[400,1536]{1,0:T(8,128)S(1)} %copy-done.2, f32[400,1536]{1,0:T(8,128)S(1)} %copy-done.3, bf16[160,1536]{1,0:T(8,128)(2,1)S(1)} %collective-permute-done.11.refs_2_, ...), custom_call_target="tpu_custom_call" | custom-call | flops 1 | bytes 1 | tf_op jit(solution)/shard_map/in_grad/pallas_call | solution.py:345
  129.3 2.1 %collective-permute-done.38.refs_1_.refs_3_ = bf16[80,6144]{1,0:T(8,128)(2,1)S(1)} collective-permute-done((bf16[80,6144]{1,0:T(8,128)(2,1)S(1)}, bf16[80,6144]{1,0:T(8,128)(2,1)S(1)}, u32[]{:S(2)}, u32[]{:S(2)}) %collective-permute-start.38) | collective-permute-done | bytes 983072 | tf_op jit(solution)/shard_map/ppermute | solution.py:589
  133.9 1.7 %collective-permute-done.39.refs_3_ = bf16[120,6144]{1,0:T(8,128)(2,1)S(1)} collective-permute-done((bf16[120,6144]{1,0:T(8,128)(2,1)S(1)}, bf16[120,6144]{1,0:T(8,128)(2,1)S(1)}, u32[]{:S(2)}, u32[]{:S(2)}) %collective-permute-start.39) | collective-permute-done | bytes 1474592 | tf_op jit(solution)/shard_map/ppermute | solution.py:484
  135.6 10.1 %w_in_grad.2.refs_6_ = bf16[6144,1536]{1,0:T(8,128)(2,1)} custom-call(bf16[200,6144]{1,0:T(8,128)(2,1)S(1)} %copy-done.1, bf16[200,6144]{1,0:T(8,128)(2,1)S(1)} %collective-permute-done.34.refs_1_, bf16[120,6144]{1,0:T(8,128)(2,1)S(1)} %pack.3.refs_2_, bf16[120,6144]{1,0:T(8,128)(2,1)S(1)} %collective-permute-done.39.refs_3_, ...), custom_call_target="tpu_custom_call" | custom-call | flops 9059696640 | bytes 9437184 | tf_op jit(solution)/shard_map/w_in_grad/pallas_call | solution.py:432
  148.2 10.1 %w_in_grad.3 = bf16[6144,1536]{1,0:T(8,128)(2,1)} custom-call(bf16[200,6144]{1,0:T(8,128)(2,1)S(1)} %copy-done.1, bf16[200,6144]{1,0:T(8,128)(2,1)S(1)} %collective-permute-done.34.refs_1_, bf16[120,6144]{1,0:T(8,128)(2,1)S(1)} %pack.3.refs_2_, bf16[120,6144]{1,0:T(8,128)(2,1)S(1)} %collective-permute-done.39.refs_3_, ...), custom_call_target="tpu_custom_call", output_to_operand_aliasing={{}: (6, {})} | custom-call | flops 9059696640 | bytes 9437184 | tf_op jit(solution)/shard_map/w_in_grad/pallas_call | solution.py:432
  (119 shorter events, 26.5 us)
Async XLA Ops:
  0.6 14.4 %collective-permute-start = (bf16[40,6144]{1,0:T(8,128)(2,1)}, bf16[40,6144]{1,0:T(8,128)(2,1)S(1)}, u32[]{:S(2)}, u32[]{:S(2)}) collective-permute-start(bf16[40,6144]{1,0:T(8,128)(2,1)} %refs_0_.1), channel_id=1, source_target_pairs={{0,1},{4,5},{1,2},{5,6},{2,3},{6,7},{3,11},{7,15},{11,10},{15,14},... | collective-permute-start | bytes 1474568 | tf_op jit(solution)/shard_map/ppermute | solution.py:478
  3.7 12.9 %collective-permute-start.1 = (bf16[40,6144]{1,0:T(8,128)(2,1)}, bf16[40,6144]{1,0:T(8,128)(2,1)S(1)}, u32[]{:S(2)}, u32[]{:S(2)}) collective-permute-start(bf16[40,6144]{1,0:T(8,128)(2,1)} %refs_0_.1), channel_id=1, source_target_pairs={{0,8},{4,12},{1,0},{5,4},{2,1},{6,5},{3,2},{7,6},{11,3},{15,7},{10... | collective-permute-start | bytes 1474568 | tf_op jit(solution)/shard_map/ppermute | solution.py:479
  3.7 12.9 %collective-permute-start.2 = (bf16[40,6144]{1,0:T(8,128)(2,1)}, bf16[40,6144]{1,0:T(8,128)(2,1)S(1)}, u32[]{:S(2)}, u32[]{:S(2)}) collective-permute-start(bf16[40,6144]{1,0:T(8,128)(2,1)} %refs_0_.1), channel_id=1, source_target_pairs={{0,4},{4,0},{1,5},{5,1},{2,6},{6,2},{3,7},{7,3},{11,15},{15,11},{1... | collective-permute-start | bytes 1474568 | tf_op jit(solution)/shard_map/ppermute | solution.py:484
  5.0 14.1 %collective-permute-start.9 = (bf16[160,1536]{1,0:T(8,128)(2,1)S(1)}, bf16[160,1536]{1,0:T(8,128)(2,1)S(1)}, u32[]{:S(2)}, u32[]{:S(2)}) collective-permute-start(bf16[160,1536]{1,0:T(8,128)(2,1)S(1)} %get-tuple-element.99), channel_id=1, source_target_pairs={{0,16},{16,0},{1,17},{17,1},{2,18},{18,2},{3,19},{19,3},{4,20},{20... | collective-permute-start | bytes 1474568 | tf_op jit(solution)/shard_map/ppermute | solution.py:490
  16.6 11.8 %collective-permute-start.3 = (bf16[40,6144]{1,0:T(8,128)(2,1)S(1)}, bf16[40,6144]{1,0:T(8,128)(2,1)S(1)}, u32[]{:S(2)}, u32[]{:S(2)}) collective-permute-start(bf16[40,6144]{1,0:T(8,128)(2,1)S(1)} %collective-permute-done.refs_1_), channel_id=1, source_target_pairs={{0,1},{4,5},{1,2},{5,6},{2,3},{6,7},{3,11},{7,15},{11,10},{15,14},... | collective-permute-start | bytes 1474568 | tf_op jit(solution)/shard_map/ppermute | solution.py:478
  18.2 11.5 %collective-permute-start.4 = (bf16[40,6144]{1,0:T(8,128)(2,1)S(1)}, bf16[40,6144]{1,0:T(8,128)(2,1)S(1)}, u32[]{:S(2)}, u32[]{:S(2)}) collective-permute-start(bf16[40,6144]{1,0:T(8,128)(2,1)S(1)} %collective-permute-done.1.refs_2_), channel_id=1, source_target_pairs={{0,8},{4,12},{1,0},{5,4},{2,1},{6,5},{3,2},{7,6},{11,3},{15,7},{10... | collective-permute-start | bytes 1474568 | tf_op jit(solution)/shard_map/ppermute | solution.py:479
  18.6 11.0 %collective-permute-start.5 = (bf16[40,6144]{1,0:T(8,128)(2,1)S(1)}, bf16[40,6144]{1,0:T(8,128)(2,1)S(1)}, u32[]{:S(2)}, u32[]{:S(2)}) collective-permute-start(bf16[40,6144]{1,0:T(8,128)(2,1)S(1)} %collective-permute-done.refs_1_), channel_id=1, source_target_pairs={{0,4},{4,0},{1,5},{5,1},{2,6},{6,2},{3,7},{7,3},{11,15},{15,11},{1... | collective-permute-start | bytes 1474568 | tf_op jit(solution)/shard_map/ppermute | solution.py:484
  18.6 11.0 %collective-permute-start.6 = (bf16[40,6144]{1,0:T(8,128)(2,1)S(1)}, bf16[40,6144]{1,0:T(8,128)(2,1)S(1)}, u32[]{:S(2)}, u32[]{:S(2)}) collective-permute-start(bf16[40,6144]{1,0:T(8,128)(2,1)S(1)} %collective-permute-done.1.refs_2_), channel_id=1, source_target_pairs={{0,4},{4,0},{1,5},{5,1},{2,6},{6,2},{3,7},{7,3},{11,15},{15,11},{1... | collective-permute-start | bytes 1474568 | tf_op jit(solution)/shard_map/ppermute | solution.py:484
  19.1 24.5 %collective-permute-start.13 = (bf16[160,1536]{1,0:T(8,128)(2,1)S(1)}, bf16[160,1536]{1,0:T(8,128)(2,1)S(1)}, u32[]{:S(2)}, u32[]{:S(2)}) collective-permute-start(bf16[160,1536]{1,0:T(8,128)(2,1)S(1)} %get-tuple-element.107), channel_id=1, source_target_pairs={{0,16},{16,0},{1,17},{17,1},{2,18},{18,2},{3,19},{19,3},{4,20},{20... | collective-permute-start | bytes 1474568 | tf_op jit(solution)/shard_map/ppermute | solution.py:490
  29.7 14.0 %collective-permute-start.10 = (bf16[40,6144]{1,0:T(8,128)(2,1)S(1)}, bf16[40,6144]{1,0:T(8,128)(2,1)S(1)}, u32[]{:S(2)}, u32[]{:S(2)}) collective-permute-start(bf16[40,6144]{1,0:T(8,128)(2,1)S(1)} %collective-permute-done.3.refs_3_), channel_id=1, source_target_pairs={{0,1},{4,5},{1,2},{5,6},{2,3},{6,7},{3,11},{7,15},{11,10},{15,14},... | collective-permute-start | bytes 1474568 | tf_op jit(solution)/shard_map/ppermute | solution.py:478
  31.3 13.3 %collective-permute-start.12 = (bf16[40,6144]{1,0:T(8,128)(2,1)S(1)}, bf16[40,6144]{1,0:T(8,128)(2,1)S(1)}, u32[]{:S(2)}, u32[]{:S(2)}) collective-permute-start(bf16[40,6144]{1,0:T(8,128)(2,1)S(1)} %collective-permute-done.4.refs_4_), channel_id=1, source_target_pairs={{0,8},{4,12},{1,0},{5,4},{2,1},{6,5},{3,2},{7,6},{11,3},{15,7},{10... | collective-permute-start | bytes 1474568 | tf_op jit(solution)/shard_map/ppermute | solution.py:479
  42.1 13.6 %collective-permute-start.11 = (bf16[160,1536]{1,0:T(8,128)(2,1)S(1)}, bf16[160,1536]{1,0:T(8,128)(2,1)S(1)}, u32[]{:S(2)}, u32[]{:S(2)}) collective-permute-start(bf16[160,1536]{1,0:T(8,128)(2,1)S(1)} %get-tuple-element.101), channel_id=1, source_target_pairs={{0,16},{16,0},{1,17},{17,1},{2,18},{18,2},{3,19},{19,3},{4,20},{20... | collective-permute-start | bytes 1474568 | tf_op jit(solution)/shard_map/ppermute | solution.py:490
  44.7 8.3 %collective-permute-start.14 = (bf16[40,3072]{1,0:T(8,128)(2,1)S(1)}, bf16[40,3072]{1,0:T(8,128)(2,1)S(1)}, u32[]{:S(2)}, u32[]{:S(2)}) collective-permute-start(bf16[40,3072]{1,0:T(8,128)(2,1)S(1)} %get-tuple-element.110), channel_id=1, source_target_pairs={{0,1},{4,5},{1,2},{5,6},{2,3},{6,7},{3,11},{7,15},{11,10},{15,14},... | collective-permute-start | bytes 737288 | tf_op jit(solution)/shard_map/ppermute | solution.py:472
  53.6 16.6 %collective-permute-start.20 = (bf16[40,6144]{1,0:T(8,128)(2,1)S(1)}, bf16[40,6144]{1,0:T(8,128)(2,1)S(1)}, u32[]{:S(2)}, u32[]{:S(2)}) collective-permute-start(bf16[40,6144]{1,0:T(8,128)(2,1)S(1)} %copy-done.10), channel_id=1, source_target_pairs={{0,1},{4,5},{1,2},{5,6},{2,3},{6,7},{3,11},{7,15},{11,10},{15,14},... | collective-permute-start | bytes 1474568 | tf_op jit(solution)/shard_map/ppermute | solution.py:478
  55.2 15.1 %collective-permute-start.21 = (bf16[40,6144]{1,0:T(8,128)(2,1)S(1)}, bf16[40,6144]{1,0:T(8,128)(2,1)S(1)}, u32[]{:S(2)}, u32[]{:S(2)}) collective-permute-start(bf16[40,6144]{1,0:T(8,128)(2,1)S(1)} %copy-done.10), channel_id=1, source_target_pairs={{0,8},{4,12},{1,0},{5,4},{2,1},{6,5},{3,2},{7,6},{11,3},{15,7},{10... | collective-permute-start | bytes 1474568 | tf_op jit(solution)/shard_map/ppermute | solution.py:479
  63.0 23.0 %collective-permute-start.24 = (bf16[240,1536]{1,0:T(8,128)(2,1)}, bf16[240,1536]{1,0:T(8,128)(2,1)S(1)}, u32[]{:S(2)}, u32[]{:S(2)}) collective-permute-start(bf16[240,1536]{1,0:T(8,128)(2,1)} %get-tuple-element.132), channel_id=1, source_target_pairs={{0,16},{16,0},{1,17},{17,1},{2,18},{18,2},{3,19},{19,3},{4,20},{20... | collective-permute-start | bytes 2211848 | tf_op jit(solution)/shard_map/ppermute | solution.py:490
  70.2 13.7 %collective-permute-start.22 = (bf16[40,6144]{1,0:T(8,128)(2,1)S(1)}, bf16[40,6144]{1,0:T(8,128)(2,1)S(1)}, u32[]{:S(2)}, u32[]{:S(2)}) collective-permute-start(bf16[40,6144]{1,0:T(8,128)(2,1)S(1)} %collective-permute-done.20.refs_1_), channel_id=1, source_target_pairs={{0,1},{4,5},{1,2},{5,6},{2,3},{6,7},{3,11},{7,15},{11,10},{15,14},... | collective-permute-start | bytes 1474568 | tf_op jit(solution)/shard_map/ppermute | solution.py:478
  71.7 12.3 %collective-permute-start.23 = (bf16[40,6144]{1,0:T(8,128)(2,1)S(1)}, bf16[40,6144]{1,0:T(8,128)(2,1)S(1)}, u32[]{:S(2)}, u32[]{:S(2)}) collective-permute-start(bf16[40,6144]{1,0:T(8,128)(2,1)S(1)} %collective-permute-done.21.refs_2_), channel_id=1, source_target_pairs={{0,8},{4,12},{1,0},{5,4},{2,1},{6,5},{3,2},{7,6},{11,3},{15,7},{10... | collective-permute-start | bytes 1474568 | tf_op jit(solution)/shard_map/ppermute | solution.py:479
  83.9 11.8 %collective-permute-start.25 = (bf16[40,6144]{1,0:T(8,128)(2,1)S(1)}, bf16[40,6144]{1,0:T(8,128)(2,1)S(1)}, u32[]{:S(2)}, u32[]{:S(2)}) collective-permute-start(bf16[40,6144]{1,0:T(8,128)(2,1)S(1)} %collective-permute-done.22.refs_3_), channel_id=1, source_target_pairs={{0,1},{4,5},{1,2},{5,6},{2,3},{6,7},{3,11},{7,15},{11,10},{15,14},... | collective-permute-start | bytes 1474568 | tf_op jit(solution)/shard_map/ppermute | solution.py:478
  85.5 11.5 %collective-permute-start.26 = (bf16[40,6144]{1,0:T(8,128)(2,1)S(1)}, bf16[40,6144]{1,0:T(8,128)(2,1)S(1)}, u32[]{:S(2)}, u32[]{:S(2)}) collective-permute-start(bf16[40,6144]{1,0:T(8,128)(2,1)S(1)} %collective-permute-done.23.refs_4_), channel_id=1, source_target_pairs={{0,8},{4,12},{1,0},{5,4},{2,1},{6,5},{3,2},{7,6},{11,3},{15,7},{10... | collective-permute-start | bytes 1474568 | tf_op jit(solution)/shard_map/ppermute | solution.py:479
  86.0 8.5 %collective-permute-start.27 = (bf16[112,1536]{1,0:T(8,128)(2,1)S(1)}, bf16[112,1536]{1,0:T(8,128)(2,1)S(1)}, u32[]{:S(2)}, u32[]{:S(2)}) collective-permute-start(bf16[112,1536]{1,0:T(8,128)(2,1)S(1)} %copy-done.14), channel_id=1, source_target_pairs={{0,16},{16,0},{1,17},{17,1},{2,18},{18,2},{3,19},{19,3},{4,20},{20... | collective-permute-start | bytes 1032200 | tf_op jit(solution)/shard_map/ppermute | solution.py:490
  97.0 15.8 %collective-permute-start.29 = (bf16[128,1536]{1,0:T(8,128)(2,1)S(1)}, bf16[128,1536]{1,0:T(8,128)(2,1)S(1)}, u32[]{:S(2)}, u32[]{:S(2)}) collective-permute-start(bf16[128,1536]{1,0:T(8,128)(2,1)S(1)} %copy-done.13), channel_id=1, source_target_pairs={{0,16},{16,0},{1,17},{17,1},{2,18},{18,2},{3,19},{19,3},{4,20},{20... | collective-permute-start | bytes 1179656 | tf_op jit(solution)/shard_map/ppermute | solution.py:490
  100.3 13.7 %collective-permute-start.32 = (bf16[40,3072]{1,0:T(8,128)(2,1)S(1)}, bf16[40,3072]{1,0:T(8,128)(2,1)S(1)}, u32[]{:S(2)}, u32[]{:S(2)}) collective-permute-start(bf16[40,3072]{1,0:T(8,128)(2,1)S(1)} %get-tuple-element.145), channel_id=1, source_target_pairs={{0,1},{4,5},{1,2},{5,6},{2,3},{6,7},{3,11},{7,15},{11,10},{15,14},... | collective-permute-start | bytes 737288 | tf_op jit(solution)/shard_map/ppermute | solution.py:622
  101.0 13.0 %collective-permute-start.33 = (bf16[40,3072]{1,0:T(8,128)(2,1)S(1)}, bf16[40,3072]{1,0:T(8,128)(2,1)S(1)}, u32[]{:S(2)}, u32[]{:S(2)}) collective-permute-start(bf16[40,3072]{1,0:T(8,128)(2,1)S(1)} %get-tuple-element.146), channel_id=1, source_target_pairs={{0,8},{4,12},{1,0},{5,4},{2,1},{6,5},{3,2},{7,6},{11,3},{15,7},{10... | collective-permute-start | bytes 737288 | tf_op jit(solution)/shard_map/ppermute | solution.py:623
  102.4 11.2 %collective-permute-start.30 = (bf16[40,3072]{1,0:T(8,128)(2,1)S(1)}, bf16[40,3072]{1,0:T(8,128)(2,1)S(1)}, u32[]{:S(2)}, u32[]{:S(2)}) collective-permute-start(bf16[40,3072]{1,0:T(8,128)(2,1)S(1)} %get-tuple-element.151), channel_id=1, source_target_pairs={{0,1},{4,5},{1,2},{5,6},{2,3},{6,7},{3,11},{7,15},{11,10},{15,14},... | collective-permute-start | bytes 737288 | tf_op jit(solution)/shard_map/ppermute | solution.py:472
  103.1 10.9 %collective-permute-start.31 = (bf16[40,3072]{1,0:T(8,128)(2,1)S(1)}, bf16[40,3072]{1,0:T(8,128)(2,1)S(1)}, u32[]{:S(2)}, u32[]{:S(2)}) collective-permute-start(bf16[40,3072]{1,0:T(8,128)(2,1)S(1)} %get-tuple-element.152), channel_id=1, source_target_pairs={{0,8},{4,12},{1,0},{5,4},{2,1},{6,5},{3,2},{7,6},{11,3},{15,7},{10... | collective-permute-start | bytes 737288 | tf_op jit(solution)/shard_map/ppermute | solution.py:473
  114.4 14.0 %collective-permute-start.35 = (bf16[40,6144]{1,0:T(8,128)(2,1)S(1)}, bf16[40,6144]{1,0:T(8,128)(2,1)S(1)}, u32[]{:S(2)}, u32[]{:S(2)}) collective-permute-start(bf16[40,6144]{1,0:T(8,128)(2,1)S(1)} %get-tuple-element.154), channel_id=1, source_target_pairs={{0,1},{4,5},{1,2},{5,6},{2,3},{6,7},{3,11},{7,15},{11,10},{15,14},... | collective-permute-start | bytes 1474568 | tf_op jit(solution)/shard_map/ppermute | solution.py:622
  115.5 13.3 %collective-permute-start.36 = (bf16[40,6144]{1,0:T(8,128)(2,1)S(1)}, bf16[40,6144]{1,0:T(8,128)(2,1)S(1)}, u32[]{:S(2)}, u32[]{:S(2)}) collective-permute-start(bf16[40,6144]{1,0:T(8,128)(2,1)S(1)} %get-tuple-element.155), channel_id=1, source_target_pairs={{0,8},{4,12},{1,0},{5,4},{2,1},{6,5},{3,2},{7,6},{11,3},{15,7},{10... | collective-permute-start | bytes 1474568 | tf_op jit(solution)/shard_map/ppermute | solution.py:623
  131.8 13.8 %collective-permute-start.40 = (bf16[40,6144]{1,0:T(8,128)(2,1)S(1)}, bf16[40,6144]{1,0:T(8,128)(2,1)S(1)}, u32[]{:S(2)}, u32[]{:S(2)}) collective-permute-start(bf16[40,6144]{1,0:T(8,128)(2,1)S(1)} %get-tuple-element.169), channel_id=1, source_target_pairs={{0,1},{4,5},{1,2},{5,6},{2,3},{6,7},{3,11},{7,15},{11,10},{15,14},... | collective-permute-start | bytes 1474568 | tf_op jit(solution)/shard_map/ppermute | solution.py:622
  132.6 13.2 %collective-permute-start.41 = (bf16[40,6144]{1,0:T(8,128)(2,1)S(1)}, bf16[40,6144]{1,0:T(8,128)(2,1)S(1)}, u32[]{:S(2)}, u32[]{:S(2)}) collective-permute-start(bf16[40,6144]{1,0:T(8,128)(2,1)S(1)} %get-tuple-element.170), channel_id=1, source_target_pairs={{0,8},{4,12},{1,0},{5,4},{2,1},{6,5},{3,2},{7,6},{11,3},{15,7},{10... | collective-permute-start | bytes 1474568 | tf_op jit(solution)/shard_map/ppermute | solution.py:623
  146.1 13.1 %collective-permute-start.42 = (bf16[40,6144]{1,0:T(8,128)(2,1)S(1)}, bf16[40,6144]{1,0:T(8,128)(2,1)S(1)}, u32[]{:S(2)}, u32[]{:S(2)}) collective-permute-start(bf16[40,6144]{1,0:T(8,128)(2,1)S(1)} %get-tuple-element.174), channel_id=1, source_target_pairs={{0,1},{4,5},{1,2},{5,6},{2,3},{6,7},{3,11},{7,15},{11,10},{15,14},... | collective-permute-start | bytes 1474568 | tf_op jit(solution)/shard_map/ppermute | solution.py:622
  146.9 12.8 %collective-permute-start.43 = (bf16[40,6144]{1,0:T(8,128)(2,1)S(1)}, bf16[40,6144]{1,0:T(8,128)(2,1)S(1)}, u32[]{:S(2)}, u32[]{:S(2)}) collective-permute-start(bf16[40,6144]{1,0:T(8,128)(2,1)S(1)} %get-tuple-element.175), channel_id=1, source_target_pairs={{0,8},{4,12},{1,0},{5,4},{2,1},{6,5},{3,2},{7,6},{11,3},{15,7},{10... | collective-permute-start | bytes 1474568 | tf_op jit(solution)/shard_map/ppermute | solution.py:623
  (32 other events, 249.7 us)

commit v5 on v4

--- a/solution.py
+++ b/solution.py
@@ -362,8 +362,8 @@
     )(part, slope, *flat, weights)
 
 
-def pieces_of(width, most):
-    tile = tile_of(width, 1024)
+def pieces_of(width, most, widest=1024):
+    tile = tile_of(width, widest)
     tiles = width // tile
     calls = min(most, tiles)
     ends = [tiles * i // calls for i in range(calls + 1)]
@@ -394,13 +394,13 @@
     return pl.pallas_call(
         kernel,
         grid=(count,),
-        in_specs=[whole(*act.shape) for act in acts]
+        in_specs=([VMEM] if earlier else [whole(*act.shape) for act in acts])
         + [pl.BlockSpec((size, tile), lambda i: (0, first + i)) for size in sizes]
         + [pl.BlockSpec(memory_space=pl.ANY)] * len(earlier),
         out_specs=[out_spec] + ([] if earlier else [whole(hidden, total)]),
         out_shape=[shape(hidden, width)] + ([] if earlier else [shape(hidden, total)]),
         input_output_aliases={len(acts) + many: 0} if earlier else {},
-        cost_estimate=cost(16 * total * tile // 4 * count * hidden, 2 * hidden * tile * count),
+        cost_estimate=cost(4 * total * max(tile * count, 1024) * hidden, 2 * hidden * tile * count),
         compiler_params=pltpu.CompilerParams(vmem_limit_bytes=26 * MIB),
         name="w_out_grad",
     )(*acts, *chunks, *earlier)
@@ -545,17 +545,18 @@
         return arrived
 
     tile, in_cuts = pieces_of(width, 2)
-    out_cuts = pieces_of(width, 6)[1]
-    if len(out_cuts) == 6:
-        out_cuts = [(0, 1), (1, 3), (4, 2)]
+    small, out_cuts = pieces_of(width, 12, 512)
+    out_cuts = [(small,) + cut for cut in out_cuts]
+    if len(out_cuts) == 12:
+        out_cuts = [(small, 11, 1), (2 * small, 0, 3), (small, 6, 5)]
     w_out_grad, w_in_grad, turned = [], [], None
 
     def w_out_piece(*others):
         nonlocal w_out_grad, turned
-        first, count = out_cuts.pop(0)
+        out_tile, first, count = out_cuts.pop(0)
         given = list(acts) if turned is None else [turned]
         given[0] = after(given[0], *others)
-        got = w_out_grad_call(given, chunks, factor, tile, first, count, w_out_grad)
+        got = w_out_grad_call(given, chunks, factor, out_tile, first, count, w_out_grad)
         w_out_grad = got[:1]
         if turned is None:
             turned = got[1]

time: 161 us -> 161 us (level)
  waiting for transfers between devices: 27.3 us -> 25.2 us
  transfers between devices with their start and end apart: 44 -> 44, of which waited for: 18 -> 15; matrix products, arithmetic and copies ran while one was open for 0% -> 0% of each run, Pallas kernels for 58% -> 58%
where the time goes in v5:
time: 161 us; the launch traced here: 160 us
  Pallas kernels  94.8 us (59%)
  starting transfers between devices  36.7 us (23%)
  waiting for transfers between devices  25.2 us (16%)
  local copies, waits for them, and re-layouts  2.67 us (2%)
    pallas_call x3, Pallas kernels, w_out_grad_call(): pl.pallas_call(kernel, grid=(count,), in_specs=([VMEM] if earlier else [w...  24.9 us
    pallas_call x2, Pallas kernels, w_in_grad_call(): pl.pallas_call(kernel, grid=(count,), in_specs=[pl.BlockSpec((each.shape[...  20.1 us
    pallas_call x2, Pallas kernels, grad_act_call(): pl.pallas_call(kernel, grid=(steps,), in_specs=[VMEM] * (len(flat) + 1),...  17.6 us
    pallas_call x2, Pallas kernels, in_grad_call(): pl.pallas_call(kernel, grid=(width // tile,), in_specs=[whole(count, hidd...  15.6 us
    ppermute x6, starting transfers between devices, step(): self.left = lax.ppermute(left, RING, ring.shift(1))  10.7 us
    ppermute x6, waiting for transfers between devices, step(): self.left = lax.ppermute(left, RING, ring.shift(1))  9.02 us
    ppermute x6, starting transfers between devices, exchange(): lax.ppermute(values, axis, [(i, (i + by) % size) for i in range(size)])  8.61 us
    pallas_call x1, Pallas kernels, hold_call(): pl.pallas_call(kernel, in_specs=[pl.BlockSpec(memory_space=pl.ANY)], out_...  7.09 us
  transfers between devices with their start and end apart: 44, of which 15 were waited for; matrix products, arithmetic and copies ran while one was open for 0% of the time, Pallas kernels for 58%

profile of v5, /device:TPU:0, one launch (start us, length us, event | category | flops | bytes accessed | tf_op | source)
XLA Modules:
  0.0 160.2 jit_solution(1400260631257956562)
XLA Ops:
  0.6 3.1 %collective-permute-start = (bf16[40,6144]{1,0:T(8,128)(2,1)}, bf16[40,6144]{1,0:T(8,128)(2,1)S(1)}, u32[]{:S(2)}, u32[]{:S(2)}) collective-permute-start(bf16[40,6144]{1,0:T(8,128)(2,1)} %refs_0_.1), channel_id=1, source_target_pairs={{0,1},{4,5},{1,2},{5,6},{2,3},{6,7},{3,11},{7,15},{11,10},{15,14},... | collective-permute-start | bytes 1474568 | tf_op jit(solution)/shard_map/ppermute | solution.py:478
  5.0 2.0 %collective-permute-start.9 = (bf16[160,1536]{1,0:T(8,128)(2,1)S(1)}, bf16[160,1536]{1,0:T(8,128)(2,1)S(1)}, u32[]{:S(2)}, u32[]{:S(2)}) collective-permute-start(bf16[160,1536]{1,0:T(8,128)(2,1)S(1)} %get-tuple-element.99), channel_id=1, source_target_pairs={{0,16},{16,0},{1,17},{17,1},{2,18},{18,2},{3,19},{19,3},{4,20},{20... | collective-permute-start | bytes 1474568 | tf_op jit(solution)/shard_map/ppermute | solution.py:490
  7.0 7.1 %hold.1 = (bf16[1536,6144]{1,0:T(8,128)(2,1)S(1)}, f32[8,128]{1,0:T(8,128)}) custom-call(bf16[1536,6144]{1,0:T(8,128)(2,1)} %weight_ref.1), custom_call_target="tpu_custom_call" | custom-call | flops 1 | bytes 1 | tf_op jit(solution)/shard_map/hold/pallas_call | solution.py:157
  15.1 1.5 collective-permute-done.1.refs_2_
  16.6 1.6 collective-permute-start.3
  19.1 1.5 collective-permute-start.13
  20.7 7.7 %collective-permute-done.3.refs_3_ = bf16[40,6144]{1,0:T(8,128)(2,1)S(1)} collective-permute-done((bf16[40,6144]{1,0:T(8,128)(2,1)S(1)}, bf16[40,6144]{1,0:T(8,128)(2,1)S(1)}, u32[]{:S(2)}, u32[]{:S(2)}) %collective-permute-start.3) | collective-permute-done | bytes 491552 | tf_op jit(solution)/shard_map/ppermute | solution.py:478
  29.7 1.6 %collective-permute-start.10 = (bf16[40,6144]{1,0:T(8,128)(2,1)S(1)}, bf16[40,6144]{1,0:T(8,128)(2,1)S(1)}, u32[]{:S(2)}, u32[]{:S(2)}) collective-permute-start(bf16[40,6144]{1,0:T(8,128)(2,1)S(1)} %collective-permute-done.3.refs_3_), channel_id=1, source_target_pairs={{0,1},{4,5},{1,2},{5,6},{2,3},{6,7},{3,11},{7,15},{11,10},{15,14},... | collective-permute-start | bytes 1474568 | tf_op jit(solution)/shard_map/ppermute | solution.py:478
  31.8 10.3 %grad_act.2 = (bf16[400,6144]{1,0:T(8,128)(2,1)}, f32[400,1536]{1,0:T(8,128)}, bf16[160,1536]{1,0:T(8,128)(2,1)S(1)}, bf16[112,1536]{1,0:T(8,128)(2,1)}, bf16[128,1536]{1,0:T(8,128)(2,1)}) custom-call(bf16[40,6144]{1,0:T(8,128)(2,1)S(1)} %copy-done.9, bf16[40,6144]{1,0:T(8,128)(2,1)S(1)} %collective-permute-done.refs_1_, ...), custom_call_target="tpu_custom_call" | custom-call | flops 1 | bytes 1 | tf_op jit(solution)/shard_map/grad_act/pallas_call | solution.py:297
  42.1 1.6 collective-permute-start.11
  44.7 1.5 collective-permute-start.14
  47.2 3.4 %gelu.2 = (bf16[400,1536]{1,0:T(8,128)(2,1)}, f32[400,1536]{1,0:T(8,128)}) custom-call(bf16[320,1536]{1,0:T(8,128)(2,1)S(1)} %copy-done.7, bf16[160,1536]{1,0:T(8,128)(2,1)S(1)} %collective-permute-done.9.refs_1_, bf16[160,1536]{1,0:T(8,128)(2,1)S(1)} %collective-permute-done.13.refs_2_), custom_call_target="tpu_custom_call" | custom-call | flops 3686400000 | bytes 1 | tf_op jit(solution)/shard_map/gelu/pallas_call | solution.py:126
  50.6 2.4 %gelu.3 = (bf16[240,1536]{1,0:T(8,128)(2,1)}, f32[240,1536]{1,0:T(8,128)}) custom-call(bf16[320,1536]{1,0:T(8,128)(2,1)S(1)} %copy-done.7, bf16[160,1536]{1,0:T(8,128)(2,1)S(1)} %collective-permute-done.9.refs_1_, bf16[160,1536]{1,0:T(8,128)(2,1)S(1)} %collective-permute-done.13.refs_2_), custom_call_target="tpu_custom_call" | custom-call | flops 2211840000 | bytes 1 | tf_op jit(solution)/shard_map/gelu/pallas_call | solution.py:126
  53.6 1.5 collective-permute-start.20
  55.7 7.3 %grad_act.3 = (bf16[240,6144]{1,0:T(8,128)(2,1)}, f32[240,1536]{1,0:T(8,128)}, bf16[240,1536]{1,0:T(8,128)(2,1)}) custom-call(bf16[40,6144]{1,0:T(8,128)(2,1)S(1)} %collective-permute-done.10.left_ref.refs_0_, bf16[40,6144]{1,0:T(8,128)(2,1)S(1)} %collective-permute-done.12.right_ref.refs_1_, bf16[40,3072]{1,0:T(8,128)(2,1)S(1)} %collective-permute-done.14.refs_2_, ...), custom_call_target="tpu_custom_call" | custom-call | flops 1 | bytes 1 | tf_op jit(solution)/shard_map/grad_act/pallas_call | solution.py:297
  63.0 1.6 collective-permute-start.24
  64.6 3.6 %w_out_grad.3 = (bf16[1536,6144]{1,0:T(8,128)(2,1)}, bf16[1536,640]{1,0:T(8,128)(2,1)S(1)}) custom-call(bf16[400,1536]{1,0:T(8,128)(2,1)S(1)} %copy-done.11, bf16[240,1536]{1,0:T(8,128)(2,1)S(1)} %copy-done.12, bf16[400,6144]{1,0:T(8,128)(2,1)} %get-tuple-element.125.refs_2_.refs_1_, bf16[240,6144]{1,0:T(8,128)(2,1)} %get-tuple-element.126.refs_3_.refs_2_), custom_call_target="tpu_custom_call" | custom-call | flops 4026531840 | bytes 1572864 | tf_op jit(solution)/shard_map/w_out_grad/pallas_call | solution.py:394
  68.3 1.5 collective-permute-start.22
  70.3 11.6 %w_out_grad.4.refs_3_ = bf16[1536,6144]{1,0:T(8,128)(2,1)} custom-call(bf16[1536,640]{1,0:T(8,128)(2,1)S(1)} %get-tuple-element.147.refs_0_, bf16[400,6144]{1,0:T(8,128)(2,1)} %get-tuple-element.125.refs_2_.refs_1_, bf16[240,6144]{1,0:T(8,128)(2,1)} %get-tuple-element.126.refs_3_.refs_2_, ...), custom_call_target="tpu_custom_call", output_to_operand_aliasing={{}: (3, {})} | custom-call | flops 12079595520 | bytes 9437184 | tf_op jit(solution)/shard_map/w_out_grad/pallas_call | solution.py:394
  82.0 1.5 collective-permute-start.25
  85.5 6.4 %in_grad.2 = (bf16[240,1536]{1,0:T(8,128)(2,1)}, f32[120,6144]{1,0:T(8,128)S(1)}, bf16[120,6144]{1,0:T(8,128)(2,1)S(1)}) custom-call(f32[240,1536]{1,0:T(8,128)S(1)} %copy-done.5, f32[240,1536]{1,0:T(8,128)S(1)} %copy-done.4, bf16[240,1536]{1,0:T(8,128)(2,1)S(1)} %collective-permute-done.24.refs_2_, bf16[6144,1536]{1,0:T(8,128)(2,1)S(1)} %bitcast.1), custom_call_target="tpu_custom_call" | custom-call | flops 1 | bytes 1 | tf_op jit(solution)/shard_map/in_grad/pallas_call | solution.py:345
  91.9 1.6 pack.2.refs_0_
  95.5 2.7 %collective-permute-done.28.refs_1_.refs_3_ = bf16[120,6144]{1,0:T(8,128)(2,1)S(1)} collective-permute-done((bf16[120,6144]{1,0:T(8,128)(2,1)S(1)}, bf16[120,6144]{1,0:T(8,128)(2,1)S(1)}, u32[]{:S(2)}, u32[]{:S(2)}) %collective-permute-start.28) | collective-permute-done | bytes 1474592 | tf_op jit(solution)/shard_map/ppermute | solution.py:590
  99.0 1.4 collective-permute-start.33
  102.5 9.7 %w_out_grad.5 = bf16[1536,6144]{1,0:T(8,128)(2,1)} custom-call(bf16[1536,640]{1,0:T(8,128)(2,1)S(1)} %get-tuple-element.147.refs_0_, bf16[400,6144]{1,0:T(8,128)(2,1)} %get-tuple-element.125.refs_2_.refs_1_, bf16[240,6144]{1,0:T(8,128)(2,1)} %get-tuple-element.126.refs_3_.refs_2_, bf16[1536,6144]{1,0:T(8,128)(2,1)} %w_out_grad.4.refs_3_), custom_call_target="tpu_custom_call", output_to_operand_aliasing={{}: (3, {})} | custom-call | flops 10066329600 | bytes 7864320 | tf_op jit(solution)/shard_map/w_out_grad/pallas_call | solution.py:394
  114.5 1.4 collective-permute-start.36
  116.0 2.6 %collective-permute-done.34.refs_1_ = bf16[200,6144]{1,0:T(8,128)(2,1)S(1)} collective-permute-done((bf16[200,6144]{1,0:T(8,128)(2,1)S(1)}, bf16[200,6144]{1,0:T(8,128)(2,1)S(1)}, u32[]{:S(2)}, u32[]{:S(2)}) %collective-permute-start.34) | collective-permute-done | bytes 2457632 | tf_op jit(solution)/shard_map/ppermute | solution.py:484
  118.6 9.2 %in_grad.3 = (bf16[400,1536]{1,0:T(8,128)(2,1)}, f32[200,6144]{1,0:T(8,128)S(1)}, bf16[120,6144]{1,0:T(8,128)(2,1)S(1)}, bf16[80,6144]{1,0:T(8,128)(2,1)S(1)}) custom-call(f32[400,1536]{1,0:T(8,128)S(1)} %copy-done.2, f32[400,1536]{1,0:T(8,128)S(1)} %copy-done.3, bf16[160,1536]{1,0:T(8,128)(2,1)S(1)} %collective-permute-done.11.refs_2_, ...), custom_call_target="tpu_custom_call" | custom-call | flops 1 | bytes 1 | tf_op jit(solution)/shard_map/in_grad/pallas_call | solution.py:345
  128.5 2.1 %collective-permute-done.38.refs_1_.refs_3_ = bf16[80,6144]{1,0:T(8,128)(2,1)S(1)} collective-permute-done((bf16[80,6144]{1,0:T(8,128)(2,1)S(1)}, bf16[80,6144]{1,0:T(8,128)(2,1)S(1)}, u32[]{:S(2)}, u32[]{:S(2)}) %collective-permute-start.38) | collective-permute-done | bytes 983072 | tf_op jit(solution)/shard_map/ppermute | solution.py:590
  133.2 1.7 %collective-permute-done.39.refs_3_ = bf16[120,6144]{1,0:T(8,128)(2,1)S(1)} collective-permute-done((bf16[120,6144]{1,0:T(8,128)(2,1)S(1)}, bf16[120,6144]{1,0:T(8,128)(2,1)S(1)}, u32[]{:S(2)}, u32[]{:S(2)}) %collective-permute-start.39) | collective-permute-done | bytes 1474592 | tf_op jit(solution)/shard_map/ppermute | solution.py:484
  134.8 10.1 %w_in_grad.2.refs_6_ = bf16[6144,1536]{1,0:T(8,128)(2,1)} custom-call(bf16[200,6144]{1,0:T(8,128)(2,1)S(1)} %copy-done.1, bf16[200,6144]{1,0:T(8,128)(2,1)S(1)} %collective-permute-done.34.refs_1_, bf16[120,6144]{1,0:T(8,128)(2,1)S(1)} %pack.3.refs_2_, bf16[120,6144]{1,0:T(8,128)(2,1)S(1)} %collective-permute-done.39.refs_3_, ...), custom_call_target="tpu_custom_call" | custom-call | flops 9059696640 | bytes 9437184 | tf_op jit(solution)/shard_map/w_in_grad/pallas_call | solution.py:432
  147.7 10.1 %w_in_grad.3 = bf16[6144,1536]{1,0:T(8,128)(2,1)} custom-call(bf16[200,6144]{1,0:T(8,128)(2,1)S(1)} %copy-done.1, bf16[200,6144]{1,0:T(8,128)(2,1)S(1)} %collective-permute-done.34.refs_1_, bf16[120,6144]{1,0:T(8,128)(2,1)S(1)} %pack.3.refs_2_, bf16[120,6144]{1,0:T(8,128)(2,1)S(1)} %collective-permute-done.39.refs_3_, ...), custom_call_target="tpu_custom_call", output_to_operand_aliasing={{}: (6, {})} | custom-call | flops 9059696640 | bytes 9437184 | tf_op jit(solution)/shard_map/w_in_grad/pallas_call | solution.py:432
  (119 shorter events, 26.4 us)
Async XLA Ops:
  0.6 14.4 %collective-permute-start = (bf16[40,6144]{1,0:T(8,128)(2,1)}, bf16[40,6144]{1,0:T(8,128)(2,1)S(1)}, u32[]{:S(2)}, u32[]{:S(2)}) collective-permute-start(bf16[40,6144]{1,0:T(8,128)(2,1)} %refs_0_.1), channel_id=1, source_target_pairs={{0,1},{4,5},{1,2},{5,6},{2,3},{6,7},{3,11},{7,15},{11,10},{15,14},... | collective-permute-start | bytes 1474568 | tf_op jit(solution)/shard_map/ppermute | solution.py:478
  3.7 12.9 %collective-permute-start.1 = (bf16[40,6144]{1,0:T(8,128)(2,1)}, bf16[40,6144]{1,0:T(8,128)(2,1)S(1)}, u32[]{:S(2)}, u32[]{:S(2)}) collective-permute-start(bf16[40,6144]{1,0:T(8,128)(2,1)} %refs_0_.1), channel_id=1, source_target_pairs={{0,8},{4,12},{1,0},{5,4},{2,1},{6,5},{3,2},{7,6},{11,3},{15,7},{10... | collective-permute-start | bytes 1474568 | tf_op jit(solution)/shard_map/ppermute | solution.py:479
  3.7 12.9 %collective-permute-start.2 = (bf16[40,6144]{1,0:T(8,128)(2,1)}, bf16[40,6144]{1,0:T(8,128)(2,1)S(1)}, u32[]{:S(2)}, u32[]{:S(2)}) collective-permute-start(bf16[40,6144]{1,0:T(8,128)(2,1)} %refs_0_.1), channel_id=1, source_target_pairs={{0,4},{4,0},{1,5},{5,1},{2,6},{6,2},{3,7},{7,3},{11,15},{15,11},{1... | collective-permute-start | bytes 1474568 | tf_op jit(solution)/shard_map/ppermute | solution.py:484
  5.0 14.1 %collective-permute-start.9 = (bf16[160,1536]{1,0:T(8,128)(2,1)S(1)}, bf16[160,1536]{1,0:T(8,128)(2,1)S(1)}, u32[]{:S(2)}, u32[]{:S(2)}) collective-permute-start(bf16[160,1536]{1,0:T(8,128)(2,1)S(1)} %get-tuple-element.99), channel_id=1, source_target_pairs={{0,16},{16,0},{1,17},{17,1},{2,18},{18,2},{3,19},{19,3},{4,20},{20... | collective-permute-start | bytes 1474568 | tf_op jit(solution)/shard_map/ppermute | solution.py:490
  16.6 11.8 %collective-permute-start.3 = (bf16[40,6144]{1,0:T(8,128)(2,1)S(1)}, bf16[40,6144]{1,0:T(8,128)(2,1)S(1)}, u32[]{:S(2)}, u32[]{:S(2)}) collective-permute-start(bf16[40,6144]{1,0:T(8,128)(2,1)S(1)} %collective-permute-done.refs_1_), channel_id=1, source_target_pairs={{0,1},{4,5},{1,2},{5,6},{2,3},{6,7},{3,11},{7,15},{11,10},{15,14},... | collective-permute-start | bytes 1474568 | tf_op jit(solution)/shard_map/ppermute | solution.py:478
  18.2 11.5 %collective-permute-start.4 = (bf16[40,6144]{1,0:T(8,128)(2,1)S(1)}, bf16[40,6144]{1,0:T(8,128)(2,1)S(1)}, u32[]{:S(2)}, u32[]{:S(2)}) collective-permute-start(bf16[40,6144]{1,0:T(8,128)(2,1)S(1)} %collective-permute-done.1.refs_2_), channel_id=1, source_target_pairs={{0,8},{4,12},{1,0},{5,4},{2,1},{6,5},{3,2},{7,6},{11,3},{15,7},{10... | collective-permute-start | bytes 1474568 | tf_op jit(solution)/shard_map/ppermute | solution.py:479
  18.6 11.0 %collective-permute-start.5 = (bf16[40,6144]{1,0:T(8,128)(2,1)S(1)}, bf16[40,6144]{1,0:T(8,128)(2,1)S(1)}, u32[]{:S(2)}, u32[]{:S(2)}) collective-permute-start(bf16[40,6144]{1,0:T(8,128)(2,1)S(1)} %collective-permute-done.refs_1_), channel_id=1, source_target_pairs={{0,4},{4,0},{1,5},{5,1},{2,6},{6,2},{3,7},{7,3},{11,15},{15,11},{1... | collective-permute-start | bytes 1474568 | tf_op jit(solution)/shard_map/ppermute | solution.py:484
  18.6 11.0 %collective-permute-start.6 = (bf16[40,6144]{1,0:T(8,128)(2,1)S(1)}, bf16[40,6144]{1,0:T(8,128)(2,1)S(1)}, u32[]{:S(2)}, u32[]{:S(2)}) collective-permute-start(bf16[40,6144]{1,0:T(8,128)(2,1)S(1)} %collective-permute-done.1.refs_2_), channel_id=1, source_target_pairs={{0,4},{4,0},{1,5},{5,1},{2,6},{6,2},{3,7},{7,3},{11,15},{15,11},{1... | collective-permute-start | bytes 1474568 | tf_op jit(solution)/shard_map/ppermute | solution.py:484
  19.1 24.5 %collective-permute-start.13 = (bf16[160,1536]{1,0:T(8,128)(2,1)S(1)}, bf16[160,1536]{1,0:T(8,128)(2,1)S(1)}, u32[]{:S(2)}, u32[]{:S(2)}) collective-permute-start(bf16[160,1536]{1,0:T(8,128)(2,1)S(1)} %get-tuple-element.107), channel_id=1, source_target_pairs={{0,16},{16,0},{1,17},{17,1},{2,18},{18,2},{3,19},{19,3},{4,20},{20... | collective-permute-start | bytes 1474568 | tf_op jit(solution)/shard_map/ppermute | solution.py:490
  29.7 14.0 %collective-permute-start.10 = (bf16[40,6144]{1,0:T(8,128)(2,1)S(1)}, bf16[40,6144]{1,0:T(8,128)(2,1)S(1)}, u32[]{:S(2)}, u32[]{:S(2)}) collective-permute-start(bf16[40,6144]{1,0:T(8,128)(2,1)S(1)} %collective-permute-done.3.refs_3_), channel_id=1, source_target_pairs={{0,1},{4,5},{1,2},{5,6},{2,3},{6,7},{3,11},{7,15},{11,10},{15,14},... | collective-permute-start | bytes 1474568 | tf_op jit(solution)/shard_map/ppermute | solution.py:478
  31.3 13.3 %collective-permute-start.12 = (bf16[40,6144]{1,0:T(8,128)(2,1)S(1)}, bf16[40,6144]{1,0:T(8,128)(2,1)S(1)}, u32[]{:S(2)}, u32[]{:S(2)}) collective-permute-start(bf16[40,6144]{1,0:T(8,128)(2,1)S(1)} %collective-permute-done.4.refs_4_), channel_id=1, source_target_pairs={{0,8},{4,12},{1,0},{5,4},{2,1},{6,5},{3,2},{7,6},{11,3},{15,7},{10... | collective-permute-start | bytes 1474568 | tf_op jit(solution)/shard_map/ppermute | solution.py:479
  42.1 13.6 %collective-permute-start.11 = (bf16[160,1536]{1,0:T(8,128)(2,1)S(1)}, bf16[160,1536]{1,0:T(8,128)(2,1)S(1)}, u32[]{:S(2)}, u32[]{:S(2)}) collective-permute-start(bf16[160,1536]{1,0:T(8,128)(2,1)S(1)} %get-tuple-element.101), channel_id=1, source_target_pairs={{0,16},{16,0},{1,17},{17,1},{2,18},{18,2},{3,19},{19,3},{4,20},{20... | collective-permute-start | bytes 1474568 | tf_op jit(solution)/shard_map/ppermute | solution.py:490
  44.7 8.3 %collective-permute-start.14 = (bf16[40,3072]{1,0:T(8,128)(2,1)S(1)}, bf16[40,3072]{1,0:T(8,128)(2,1)S(1)}, u32[]{:S(2)}, u32[]{:S(2)}) collective-permute-start(bf16[40,3072]{1,0:T(8,128)(2,1)S(1)} %get-tuple-element.110), channel_id=1, source_target_pairs={{0,1},{4,5},{1,2},{5,6},{2,3},{6,7},{3,11},{7,15},{11,10},{15,14},... | collective-permute-start | bytes 737288 | tf_op jit(solution)/shard_map/ppermute | solution.py:472
  53.6 14.6 %collective-permute-start.20 = (bf16[40,6144]{1,0:T(8,128)(2,1)S(1)}, bf16[40,6144]{1,0:T(8,128)(2,1)S(1)}, u32[]{:S(2)}, u32[]{:S(2)}) collective-permute-start(bf16[40,6144]{1,0:T(8,128)(2,1)S(1)} %copy-done.10), channel_id=1, source_target_pairs={{0,1},{4,5},{1,2},{5,6},{2,3},{6,7},{3,11},{7,15},{11,10},{15,14},... | collective-permute-start | bytes 1474568 | tf_op jit(solution)/shard_map/ppermute | solution.py:478
  55.2 13.1 %collective-permute-start.21 = (bf16[40,6144]{1,0:T(8,128)(2,1)S(1)}, bf16[40,6144]{1,0:T(8,128)(2,1)S(1)}, u32[]{:S(2)}, u32[]{:S(2)}) collective-permute-start(bf16[40,6144]{1,0:T(8,128)(2,1)S(1)} %copy-done.10), channel_id=1, source_target_pairs={{0,8},{4,12},{1,0},{5,4},{2,1},{6,5},{3,2},{7,6},{11,3},{15,7},{10... | collective-permute-start | bytes 1474568 | tf_op jit(solution)/shard_map/ppermute | solution.py:479
  63.0 21.0 %collective-permute-start.24 = (bf16[240,1536]{1,0:T(8,128)(2,1)}, bf16[240,1536]{1,0:T(8,128)(2,1)S(1)}, u32[]{:S(2)}, u32[]{:S(2)}) collective-permute-start(bf16[240,1536]{1,0:T(8,128)(2,1)} %get-tuple-element.132), channel_id=1, source_target_pairs={{0,16},{16,0},{1,17},{17,1},{2,18},{18,2},{3,19},{19,3},{4,20},{20... | collective-permute-start | bytes 2211848 | tf_op jit(solution)/shard_map/ppermute | solution.py:490
  68.3 13.7 %collective-permute-start.22 = (bf16[40,6144]{1,0:T(8,128)(2,1)S(1)}, bf16[40,6144]{1,0:T(8,128)(2,1)S(1)}, u32[]{:S(2)}, u32[]{:S(2)}) collective-permute-start(bf16[40,6144]{1,0:T(8,128)(2,1)S(1)} %collective-permute-done.20.refs_1_), channel_id=1, source_target_pairs={{0,1},{4,5},{1,2},{5,6},{2,3},{6,7},{3,11},{7,15},{11,10},{15,14},... | collective-permute-start | bytes 1474568 | tf_op jit(solution)/shard_map/ppermute | solution.py:478
  69.7 12.2 %collective-permute-start.23 = (bf16[40,6144]{1,0:T(8,128)(2,1)S(1)}, bf16[40,6144]{1,0:T(8,128)(2,1)S(1)}, u32[]{:S(2)}, u32[]{:S(2)}) collective-permute-start(bf16[40,6144]{1,0:T(8,128)(2,1)S(1)} %collective-permute-done.21.refs_2_), channel_id=1, source_target_pairs={{0,8},{4,12},{1,0},{5,4},{2,1},{6,5},{3,2},{7,6},{11,3},{15,7},{10... | collective-permute-start | bytes 1474568 | tf_op jit(solution)/shard_map/ppermute | solution.py:479
  82.0 11.9 %collective-permute-start.25 = (bf16[40,6144]{1,0:T(8,128)(2,1)S(1)}, bf16[40,6144]{1,0:T(8,128)(2,1)S(1)}, u32[]{:S(2)}, u32[]{:S(2)}) collective-permute-start(bf16[40,6144]{1,0:T(8,128)(2,1)S(1)} %collective-permute-done.22.refs_3_), channel_id=1, source_target_pairs={{0,1},{4,5},{1,2},{5,6},{2,3},{6,7},{3,11},{7,15},{11,10},{15,14},... | collective-permute-start | bytes 1474568 | tf_op jit(solution)/shard_map/ppermute | solution.py:478
  83.5 11.5 %collective-permute-start.26 = (bf16[40,6144]{1,0:T(8,128)(2,1)S(1)}, bf16[40,6144]{1,0:T(8,128)(2,1)S(1)}, u32[]{:S(2)}, u32[]{:S(2)}) collective-permute-start(bf16[40,6144]{1,0:T(8,128)(2,1)S(1)} %collective-permute-done.23.refs_4_), channel_id=1, source_target_pairs={{0,8},{4,12},{1,0},{5,4},{2,1},{6,5},{3,2},{7,6},{11,3},{15,7},{10... | collective-permute-start | bytes 1474568 | tf_op jit(solution)/shard_map/ppermute | solution.py:479
  84.0 9.4 %collective-permute-start.27 = (bf16[112,1536]{1,0:T(8,128)(2,1)S(1)}, bf16[112,1536]{1,0:T(8,128)(2,1)S(1)}, u32[]{:S(2)}, u32[]{:S(2)}) collective-permute-start(bf16[112,1536]{1,0:T(8,128)(2,1)S(1)} %copy-done.14), channel_id=1, source_target_pairs={{0,16},{16,0},{1,17},{17,1},{2,18},{18,2},{3,19},{19,3},{4,20},{20... | collective-permute-start | bytes 1032200 | tf_op jit(solution)/shard_map/ppermute | solution.py:490
  95.0 17.2 %collective-permute-start.29 = (bf16[128,1536]{1,0:T(8,128)(2,1)S(1)}, bf16[128,1536]{1,0:T(8,128)(2,1)S(1)}, u32[]{:S(2)}, u32[]{:S(2)}) collective-permute-start(bf16[128,1536]{1,0:T(8,128)(2,1)S(1)} %copy-done.13), channel_id=1, source_target_pairs={{0,16},{16,0},{1,17},{17,1},{2,18},{18,2},{3,19},{19,3},{4,20},{20... | collective-permute-start | bytes 1179656 | tf_op jit(solution)/shard_map/ppermute | solution.py:490
  98.4 13.9 %collective-permute-start.32 = (bf16[40,3072]{1,0:T(8,128)(2,1)S(1)}, bf16[40,3072]{1,0:T(8,128)(2,1)S(1)}, u32[]{:S(2)}, u32[]{:S(2)}) collective-permute-start(bf16[40,3072]{1,0:T(8,128)(2,1)S(1)} %get-tuple-element.145), channel_id=1, source_target_pairs={{0,1},{4,5},{1,2},{5,6},{2,3},{6,7},{3,11},{7,15},{11,10},{15,14},... | collective-permute-start | bytes 737288 | tf_op jit(solution)/shard_map/ppermute | solution.py:623
  99.0 13.3 %collective-permute-start.33 = (bf16[40,3072]{1,0:T(8,128)(2,1)S(1)}, bf16[40,3072]{1,0:T(8,128)(2,1)S(1)}, u32[]{:S(2)}, u32[]{:S(2)}) collective-permute-start(bf16[40,3072]{1,0:T(8,128)(2,1)S(1)} %get-tuple-element.146), channel_id=1, source_target_pairs={{0,8},{4,12},{1,0},{5,4},{2,1},{6,5},{3,2},{7,6},{11,3},{15,7},{10... | collective-permute-start | bytes 737288 | tf_op jit(solution)/shard_map/ppermute | solution.py:624
  100.5 11.8 %collective-permute-start.30 = (bf16[40,3072]{1,0:T(8,128)(2,1)S(1)}, bf16[40,3072]{1,0:T(8,128)(2,1)S(1)}, u32[]{:S(2)}, u32[]{:S(2)}) collective-permute-start(bf16[40,3072]{1,0:T(8,128)(2,1)S(1)} %get-tuple-element.151), channel_id=1, source_target_pairs={{0,1},{4,5},{1,2},{5,6},{2,3},{6,7},{3,11},{7,15},{11,10},{15,14},... | collective-permute-start | bytes 737288 | tf_op jit(solution)/shard_map/ppermute | solution.py:472
  101.1 11.1 %collective-permute-start.31 = (bf16[40,3072]{1,0:T(8,128)(2,1)S(1)}, bf16[40,3072]{1,0:T(8,128)(2,1)S(1)}, u32[]{:S(2)}, u32[]{:S(2)}) collective-permute-start(bf16[40,3072]{1,0:T(8,128)(2,1)S(1)} %get-tuple-element.152), channel_id=1, source_target_pairs={{0,8},{4,12},{1,0},{5,4},{2,1},{6,5},{3,2},{7,6},{11,3},{15,7},{10... | collective-permute-start | bytes 737288 | tf_op jit(solution)/shard_map/ppermute | solution.py:473
  113.9 14.0 %collective-permute-start.35 = (bf16[40,6144]{1,0:T(8,128)(2,1)S(1)}, bf16[40,6144]{1,0:T(8,128)(2,1)S(1)}, u32[]{:S(2)}, u32[]{:S(2)}) collective-permute-start(bf16[40,6144]{1,0:T(8,128)(2,1)S(1)} %get-tuple-element.154), channel_id=1, source_target_pairs={{0,1},{4,5},{1,2},{5,6},{2,3},{6,7},{3,11},{7,15},{11,10},{15,14},... | collective-permute-start | bytes 1474568 | tf_op jit(solution)/shard_map/ppermute | solution.py:623
  114.5 13.4 %collective-permute-start.36 = (bf16[40,6144]{1,0:T(8,128)(2,1)S(1)}, bf16[40,6144]{1,0:T(8,128)(2,1)S(1)}, u32[]{:S(2)}, u32[]{:S(2)}) collective-permute-start(bf16[40,6144]{1,0:T(8,128)(2,1)S(1)} %get-tuple-element.155), channel_id=1, source_target_pairs={{0,8},{4,12},{1,0},{5,4},{2,1},{6,5},{3,2},{7,6},{11,3},{15,7},{10... | collective-permute-start | bytes 1474568 | tf_op jit(solution)/shard_map/ppermute | solution.py:624
  131.1 13.8 %collective-permute-start.40 = (bf16[40,6144]{1,0:T(8,128)(2,1)S(1)}, bf16[40,6144]{1,0:T(8,128)(2,1)S(1)}, u32[]{:S(2)}, u32[]{:S(2)}) collective-permute-start(bf16[40,6144]{1,0:T(8,128)(2,1)S(1)} %get-tuple-element.169), channel_id=1, source_target_pairs={{0,1},{4,5},{1,2},{5,6},{2,3},{6,7},{3,11},{7,15},{11,10},{15,14},... | collective-permute-start | bytes 1474568 | tf_op jit(solution)/shard_map/ppermute | solution.py:623
  132.1 13.2 %collective-permute-start.41 = (bf16[40,6144]{1,0:T(8,128)(2,1)S(1)}, bf16[40,6144]{1,0:T(8,128)(2,1)S(1)}, u32[]{:S(2)}, u32[]{:S(2)}) collective-permute-start(bf16[40,6144]{1,0:T(8,128)(2,1)S(1)} %get-tuple-element.170), channel_id=1, source_target_pairs={{0,8},{4,12},{1,0},{5,4},{2,1},{6,5},{3,2},{7,6},{11,3},{15,7},{10... | collective-permute-start | bytes 1474568 | tf_op jit(solution)/shard_map/ppermute | solution.py:624
  145.6 12.9 %collective-permute-start.42 = (bf16[40,6144]{1,0:T(8,128)(2,1)S(1)}, bf16[40,6144]{1,0:T(8,128)(2,1)S(1)}, u32[]{:S(2)}, u32[]{:S(2)}) collective-permute-start(bf16[40,6144]{1,0:T(8,128)(2,1)S(1)} %get-tuple-element.174), channel_id=1, source_target_pairs={{0,1},{4,5},{1,2},{5,6},{2,3},{6,7},{3,11},{7,15},{11,10},{15,14},... | collective-permute-start | bytes 1474568 | tf_op jit(solution)/shard_map/ppermute | solution.py:623
  146.4 12.8 %collective-permute-start.43 = (bf16[40,6144]{1,0:T(8,128)(2,1)S(1)}, bf16[40,6144]{1,0:T(8,128)(2,1)S(1)}, u32[]{:S(2)}, u32[]{:S(2)}) collective-permute-start(bf16[40,6144]{1,0:T(8,128)(2,1)S(1)} %get-tuple-element.175), channel_id=1, source_target_pairs={{0,8},{4,12},{1,0},{5,4},{2,1},{6,5},{3,2},{7,6},{11,3},{15,7},{10... | collective-permute-start | bytes 1474568 | tf_op jit(solution)/shard_map/ppermute | solution.py:624
  (32 other events, 254.8 us)
